TPU v7x, 512 devices: a whole 4x8x8 slice. The times are simulated.
512 devices in a mesh: rows: 128 (over x, z, y_hi, core), repl: 4 (over y_lo).
Axes of the slice: x: 4, y: 8 (y_hi: 2, y_lo: 4; y = y_hi * 4 + y_lo), z: 8, core: 2. Of those that a mesh axis runs over, the one named last changes fastest.
Arguments:
- features: bfloat16 [128, 16384], P(None, 'rows'), may hold values from -6 to 6
- tile_blocks: int32 [16384], P(('rows', 'repl')), may hold values from -1 to 127, as said below
- tile_counts: int32 [16384, 128, 128], P(('rows', 'repl')), may hold values from 0 to 3, as said below
- train_mask: int32 [16384], P('rows'), may hold values 0 or 1
- cotangent: bfloat16 [47, 16384], P(None, 'rows'), may hold values from -6 to 6
- self_one: bfloat16 [128, 256], P(None, 'repl'), may hold values from -0.5 to 0.5
- neighbor_one: bfloat16 [128, 256], P(None, 'repl'), may hold values from -1.5 to 1.5
- bias_one: bfloat16 [256], P('repl'), may hold values from -3 to 3
- self_two: bfloat16 [256, 47], P('repl'), may hold values from -0.375 to 0.375
- neighbor_two: bfloat16 [256, 47], P('repl'), may hold values from -1 to 1
- bias_two: bfloat16 [47], replicated, may hold values from -3 to 3
Outputs:
- scores: float32 [47, 16384], P(None, 'rows')
- selfgrad_one: float32 [128, 256], P(None, 'repl')
- neighgrad_one: float32 [128, 256], P(None, 'repl')
- biasgrad_one: float32 [256], P('repl')
- selfgrad_two: float32 [256, 47], P('repl')
- neighgrad_two: float32 [256, 47], P('repl')
- biasgrad_two: float32 [47], replicated
Inputs may be any that keep to these rules, and one draw needn't show every extreme that they name: `tile_blocks`: each device's 32 slots hold the column blocks of its live tiles first and -1 after them; every device has at least one live tile, and some device has all 32 live. `tile_counts`: entries count edges; most are zero.
All inputs are finite; a program needn't handle non-finite values. No bound on the sum of `train_mask` on one device may be relied on, other than what follows from the above.
Results may differ from a plain program's by a relative error of at most 0.0045.
Values may be sent and summed in bfloat16 or wider, within the bound.
No kernel may reach another device: no remote copies, remote signals or barrier semaphores. Data moves between devices by JAX's collectives and lax.ppermute only.
A program may use at most 64 MiB of HBM per device.

v0:
```python
import jax
import jax.numpy as jnp
from jax import lax
from jax.sharding import PartitionSpec as P


def live_total(tile_blocks):
    return jnp.sum((tile_blocks >= 0).astype(jnp.int32))


def gather_terms(whole, tile_counts, tile_blocks, live_count):
    tile_edge = tile_counts.shape[1]

    def gather_advance(position, running):
        column_block = tile_blocks[position]
        columns = lax.dynamic_slice_in_dim(whole, column_block * tile_edge, tile_edge, 1)
        counts = tile_counts[position].astype(jnp.bfloat16)
        return running + lax.dot_general(
            columns, counts, (((1,), (1,)), ((), ())), preferred_element_type=jnp.float32
        )

    return lax.fori_loop(
        0, live_count, gather_advance, jnp.zeros((whole.shape[0], tile_edge), jnp.float32)
    )


def spread_terms(scaled, tile_counts, tile_blocks, live_count, node_total):
    tile_edge = tile_counts.shape[1]

    def spread_advance(position, running):
        column_block = tile_blocks[position]
        counts = tile_counts[position].astype(jnp.bfloat16)
        product = jnp.dot(scaled, counts, preferred_element_type=jnp.float32)
        current = lax.dynamic_slice_in_dim(running, column_block * tile_edge, tile_edge, 1)
        return lax.dynamic_update_slice_in_dim(
            running, current + product, column_block * tile_edge, 1
        )

    return lax.fori_loop(
        0, live_count, spread_advance, jnp.zeros((scaled.shape[0], node_total), jnp.float32)
    )


def pair_total(leading, trailing):
    return lax.psum((leading, trailing), "repl")


def per_device(
    features,
    tile_blocks,
    tile_counts,
    train_mask,
    cotangent,
    self_one,
    neighbor_one,
    bias_one,
    self_two,
    neighbor_two,
    bias_two,
):
    contract = (((0,), (0,)), ((), ()))
    rowwise = (((1,), (1,)), ((), ()))
    live_count = live_total(tile_blocks)
    tile_edge = tile_counts.shape[1]
    node_total = tile_edge * lax.axis_size("rows")
    everywhere = lax.all_gather(features, "rows", axis=1, tiled=True)
    valid = (tile_blocks >= 0).astype(jnp.float32)
    degree_part = jnp.sum(jnp.sum(tile_counts, axis=2).astype(jnp.float32) * valid[:, None], axis=0)
    layer_part = gather_terms(everywhere, tile_counts, tile_blocks, live_count)
    layer_sum, degree = pair_total(layer_part, degree_part)
    inverse = 1.0 / (degree + 1.0)
    upstream = cotangent * train_mask.astype(jnp.bfloat16)[None, :]
    scaled = (upstream.astype(jnp.float32) * inverse[None, :]).astype(jnp.bfloat16)
    back_term = spread_terms(scaled, tile_counts, tile_blocks, live_count, node_total)
    back_part = lax.psum_scatter(back_term, "rows", scatter_dimension=1, tiled=True)
    mean_one = (layer_sum * inverse[None, :]).astype(jnp.bfloat16)
    hidden_pre = lax.dot_general(self_one, features, contract, preferred_element_type=jnp.float32)
    hidden_pre = hidden_pre + lax.dot_general(
        neighbor_one, mean_one, contract, preferred_element_type=jnp.float32
    )
    hidden_pre = hidden_pre + bias_one.astype(jnp.float32)[:, None]
    hidden = jax.nn.silu(hidden_pre).astype(jnp.bfloat16)
    project_part = lax.dot_general(
        neighbor_two, hidden, contract, preferred_element_type=jnp.float32
    )
    skip_part = lax.dot_general(self_two, hidden, contract, preferred_element_type=jnp.float32)
    projected, skipped = pair_total(project_part, skip_part)
    projected_whole = lax.all_gather(projected.astype(jnp.bfloat16), "rows", axis=1, tiled=True)
    second_part = gather_terms(projected_whole, tile_counts, tile_blocks, live_count)
    second_sum, pulled_sum = pair_total(second_part, back_part)
    pulled = pulled_sum.astype(jnp.bfloat16)
    scores = skipped + second_sum * inverse[None, :] + bias_two.astype(jnp.float32)[:, None]
    hidden_grad = jnp.dot(self_two, upstream, preferred_element_type=jnp.float32) + jnp.dot(
        neighbor_two, pulled, preferred_element_type=jnp.float32
    )
    sigmoid = jax.nn.sigmoid(hidden_pre)
    pre_grad = (hidden_grad * sigmoid * (1.0 + hidden_pre * (1.0 - sigmoid))).astype(jnp.bfloat16)
    selfgrad_one = lax.dot_general(features, pre_grad, rowwise, preferred_element_type=jnp.float32)
    neighgrad_one = lax.dot_general(mean_one, pre_grad, rowwise, preferred_element_type=jnp.float32)
    biasgrad_one = jnp.sum(pre_grad.astype(jnp.float32), axis=1)
    selfgrad_two = lax.dot_general(hidden, upstream, rowwise, preferred_element_type=jnp.float32)
    neighgrad_two = lax.dot_general(hidden, pulled, rowwise, preferred_element_type=jnp.float32)
    biasgrad_two = jnp.sum(upstream.astype(jnp.float32), axis=1)
    summed = lax.psum(
        (selfgrad_one, neighgrad_one, biasgrad_one, selfgrad_two, neighgrad_two, biasgrad_two),
        "rows",
    )
    return (scores, summed[0], summed[1], summed[2], summed[3], summed[4], summed[5])


def solution(mesh):
    return jax.shard_map(
        per_device,
        mesh=mesh,
        in_specs=(
            P(None, "rows"),
            P(("rows", "repl")),
            P(("rows", "repl"), None, None),
            P("rows"),
            P(None, "rows"),
            P(None, "repl"),
            P(None, "repl"),
            P("repl"),
            P("repl", None),
            P("repl", None),
            P(),
        ),
        out_specs=(
            P(None, "rows"),
            P(None, "repl"),
            P(None, "repl"),
            P("repl"),
            P("repl", None),
            P("repl", None),
            P(),
        ),
        check_vma=False,
    )
```

profile of v0, /device:TPU:8, one launch (start us, length us, event | category | flops | bytes accessed | tf_op | source)
XLA Modules:
  0.0 2157.4 jit_solution(1325008807589575193)
XLA Ops:
  8.0 2.2 reduce_sum.46
  11.0 14.1 psum.85
  25.1 1.3 fusion.30
  27.3 101.5 %all-gather.3.cloned.1.call-done = bf16[128,16384]{1,0:T(8,128)(2,1)} async-done(((bf16[128,128]{1,0:T(8,128)(2,1)}), bf16[128,16384]{1,0:T(8,128)(2,1)}) %all-gather.3.cloned.1.call-update) | async-done | bytes 4194320 | tf_op jit(solution)/shard_map/all_gather | solution.py:66
  128.7 47.4 %while.30 = (s32[]{:T(128)}, f32[128,128]{1,0:T(8,128)S(1)}, s32[]{:T(128)}, s32[32]{0:T(128)}, bf16[128,16384]{1,0:T(8,128)(2,1)}, /*index=5*/s32[32,128,128]{2...) while((s32[]{:T(128)}, f32[128,128]{1,0:T(8,128)S(1)}, s32[]{:T(128)}, ...), condition=%wide.region_2.0_spmd, body=%wide.region_1.0_spmd.sunk | while | flops 4227081 | bytes 229585 | solution.py:22
  129.4 1.2 dynamic_slice.55
  133.0 1.2 dynamic_slice.55
  136.6 1.2 dynamic_slice.55
  140.2 1.2 dynamic_slice.55
  143.8 1.2 dynamic_slice.55
  158.2 1.2 dynamic_slice.55
  176.8 116.1 %all-reduce.5.cloned.1.call-done = f32[128,128]{1,0:T(8,128)} async-done(((f32[128,128]{1,0:T(8,128)}), f32[128,128]{1,0:T(8,128)}) %all-reduce.5.cloned.1.call-update) | async-done | bytes 65552 | tf_op jit(solution)/shard_map/psum | solution.py:45
  294.1 16.7 psum.87
  311.7 38.3 %while.32 = (s32[]{:T(128)}, f32[47,16384]{1,0:T(8,128)S(1)}, s32[]{:T(128)}, s32[32]{0:T(128)S(1)}, s32[32,128,128]{2,1,0:T(8,128)}, /*index=5*/bf16[47,128]{1,...) while((s32[]{:T(128)}, f32[47,16384]{1,0:T(8,128)S(1)}, ...), condition=%wide.region_13.14_spmd, body=%wide.region_12.13_spmd.sunk | while | flops 1562505 | bytes 127185 | solution.py:39
  350.0 1.6 copy-done.1
  352.8 65.6 %all-gather.5.cloned.1.call-done = bf16[47,16384]{1,0:T(8,128)(2,1)} async-done(((bf16[47,128]{1,0:T(8,128)(2,1)}), bf16[47,16384]{1,0:T(8,128)(2,1)}) %all-gather.5.cloned.1.call-update) | async-done | bytes 1540112 | tf_op jit(solution)/shard_map/all_gather | solution.py:88
  418.4 38.8 %while.31 = (s32[]{:T(128)}, f32[47,128]{1,0:T(8,128)S(1)}, s32[]{:T(128)}, s32[32]{0:T(128)S(1)}, bf16[47,16384]{1,0:T(8,128)(2,1)}, /*index=5*/s32[32,128,128]...) while((s32[]{:T(128)}, f32[47,128]{1,0:T(8,128)S(1)}, s32[]{:T(128)}, ...), condition=%wide.region_10.11_spmd, body=%wide.region_9.0_spmd.sunk | while | flops 1562505 | bytes 126161 | solution.py:22
  457.2 252.2 %reduce-scatter.2.cloned.1.call-done = f32[47,128]{1,0:T(8,128)} async-done(((f32[47,16384]{1,0:T(8,128)}), f32[47,128]{1,0:T(8,128)}) %reduce-scatter.2.cloned.1.call-update) | async-done | bytes 24080 | tf_op jit(solution)/shard_map/reduce_scatter | solution.py:75
  709.4 16.6 all-reduce.1
  729.8 1413.2 %all-reduce.7.cloned.1.call-done = (f32[128,64]{0,1:T(8,128)}, f32[128,64]{0,1:T(8,128)}, f32[64]{0:T(128)}, f32[64,47]{0,1:T(8,128)}, f32[64,47]{0,1:T(8,128)}, /*index=5*/f32[47]{0:T(128)}) async-done(((f32[128,64]{0,1:T(8,128)}, f32[128,64]{0,1:T(8,128)}, f32[64]{0:T(128)}, f32[64,47]{0,1:T(8,128)}, f32[64,47]{0,1:T(8,128)}, /*index=5*/f32[47]{0:T(128)}), (f32[128,64]{0,1:T(8,128)}, f32[128,64]{0,1:T(8,128)}, ...) | async-done | bytes 90060 | tf_op jit(solution)/shard_map/psum | solution.py:104
  2143.1 1.4 copy.44
  2144.5 1.4 copy.45
  2147.0 1.3 copy.47
  2148.4 1.3 copy.48
  (128 shorter events, 75.1 us)
Async XLA Ops:
  7.2 285.8 %copy-start = (bf16[128,64]{0,1:T(8,128)(2,1)S(1)}, bf16[128,64]{0,1:T(8,128)(2,1)}, u32[]{:S(2)}) copy-start(bf16[128,64]{0,1:T(8,128)(2,1)} %param.23) | copy-start | bytes 49156
  7.2 169.6 %copy-start.8 = (bf16[64]{0:T(256)(128)(2,1)S(1)}, bf16[64]{0:T(256)(128)(2,1)}, u32[]{:S(2)}) copy-start(bf16[64]{0:T(256)(128)(2,1)} %param.24) | copy-start | bytes 388
  7.2 286.7 %copy-start.7 = (bf16[64,47]{0,1:T(8,128)(2,1)S(1)}, bf16[64,47]{0,1:T(8,128)(2,1)}, u32[]{:S(2)}) copy-start(bf16[64,47]{0,1:T(8,128)(2,1)} %param.26) | copy-start | bytes 18052
  7.2 303.6 %copy-start.9 = (s32[128]{0:T(128)S(1)}, s32[128]{0:T(128)}, u32[]{:S(2)}) copy-start(s32[128]{0:T(128)} %param.20) | copy-start | bytes 1540
  7.2 303.6 %copy-start.5 = (bf16[47,128]{1,0:T(8,128)(2,1)S(1)}, bf16[47,128]{1,0:T(8,128)(2,1)}, u32[]{:S(2)}) copy-start(bf16[47,128]{1,0:T(8,128)(2,1)} %param.21) | copy-start | bytes 36100
  7.2 121.5 %all-gather.3.cloned.1.call-start = ((), (), s32[]{:S(2)}) async-start(), calls=%async_computation.1 | async-start | bytes 4227072 | tf_op jit(solution)/shard_map/all_gather | solution.py:66
  8.0 285.0 %all-reduce.5.cloned.1.call-start = ((), (), s32[]{:S(2)}) async-start(), calls=%async_computation.2 | async-start | bytes 131072 | tf_op jit(solution)/shard_map/psum | solution.py:45
  176.1 0.6 copy-start.2
  176.1 135.5 %copy-start.11 = (s32[32]{0:T(128)S(1)}, s32[32]{0:T(128)}, u32[]{:S(2)}) copy-start(s32[32]{0:T(128)} %get-tuple-element.422) | copy-start | bytes 388
  176.8 241.7 %all-gather.5.cloned.1.call-start = ((), (), s32[]{:S(2)}) async-start(), calls=%async_computation.3 | async-start | bytes 1585152 | tf_op jit(solution)/shard_map/all_gather | solution.py:88
  310.8 398.7 %reduce-scatter.2.cloned.1.call-start = ((), (), s32[]{:S(2)}) async-start(), calls=%async_computation.4 | async-start | bytes 3170304 | tf_op jit(solution)/shard_map/reduce_scatter | solution.py:75
  311.5 40.3 %copy-start.10 = (bf16[47]{0:T(256)(128)(2,1)S(1)}, bf16[47]{0:T(256)(128)(2,1)}, u32[]{:S(2)}) copy-start(bf16[47]{0:T(256)(128)(2,1)} %param.27) | copy-start | bytes 286
  311.5 40.3 %copy-start.6 = (bf16[64,47]{0,1:T(8,128)(2,1)S(1)}, bf16[64,47]{0,1:T(8,128)(2,1)}, u32[]{:S(2)}) copy-start(bf16[64,47]{0,1:T(8,128)(2,1)} %param.25) | copy-start | bytes 18052
  311.7 415.9 %copy-start.3 = (bf16[128,128]{1,0:T(8,128)(2,1)S(1)}, bf16[128,128]{1,0:T(8,128)(2,1)}, u32[]{:S(2)}) copy-start(bf16[128,128]{1,0:T(8,128)(2,1)} %param.17) | copy-start | bytes 98308
  311.7 416.7 %copy-start.4 = (f32[128,128]{1,0:T(8,128)S(1)}, f32[128,128]{1,0:T(8,128)}, u32[]{:S(2)}) copy-start(f32[128,128]{1,0:T(8,128)} %all-reduce.5.cloned.1.call-done) | copy-start | bytes 196612
  350.0 1.6 copy-start.1
  351.7 1791.4 %all-reduce.7.cloned.1.call-start = ((), (), s32[]{:S(2)}) async-start(), calls=%async_computation.5 | async-start | bytes 231424 | tf_op jit(solution)/shard_map/psum | solution.py:104
Sparse Core Ops, SparseCore 0:
  12.7 115.9 all-gather.2
  176.9 115.9 all-reduce.4
  310.9 107.4 all-gather.4
  425.8 283.5 reduce-scatter.1
  729.3 1413.7 all-reduce.6
where the time goes:
time: 2170 us; the launch traced here: 2160 us
  waiting for transfers between devices  1950 us (90%)
  loops' own time  54.2 us (2%)
  blocking collectives  47.4 us (2%)
  matrix products  45 us (2%)
  local copies, waits for them, and re-layouts  41.6 us (2%)
    psum x1, waiting for transfers between devices, per_device(): lax.psum((selfgrad_one, neighgrad_one, biasgrad_one, selfgrad_two, neighg...  1410 us
    reduce_scatter x1, waiting for transfers between devices, per_device(): lax.psum_scatter(back_term, 'rows', scatter_dimension=1, tiled=True)  252 us
    psum x1, waiting for transfers between devices, pair_total(): return lax.psum((leading, trailing), 'repl')  116 us
    all_gather x1, waiting for transfers between devices, per_device(): everywhere = lax.all_gather(features, 'rows', axis=1, tiled=True)  101 us
    all_gather x1, waiting for transfers between devices, per_device(): lax.all_gather(projected.astype(jnp.bfloat16), 'rows', axis=1, tiled=True)  65.6 us
    psum x3, blocking collectives, pair_total(): return lax.psum((leading, trailing), 'repl')  47.4 us
  transfers between devices with their start and end apart: 5, of which 5 were waited for; matrix products, arithmetic and copies ran while one was open for 2% of the time, Pallas kernels for 0%

commit v1 on v0

v1 whole, which is shorter than its diff:
```python
import functools

import jax
import jax.numpy as jnp
from jax import lax
from jax.experimental import pallas as pl
from jax.experimental.pallas import tpu as pltpu
from jax.sharding import Mesh, PartitionSpec as P

BF = jnp.bfloat16
F32 = jnp.float32
CLASSES = 47
WIDE = 48
EDGE = 128
ROWS = ("x", "z", "yh", "core")
PLANE = ("x", "z")
COLUMN = ("yh", "yl")
GRADS = 256
VMEM = pl.BlockSpec(memory_space=pltpu.VMEM)
SMEM = pl.BlockSpec(memory_space=pltpu.SMEM)
NT = (((1,), (1,)), ((), ()))
TN = (((0,), (0,)), ((), ()))


def dot(a, b, dims=(((1,), (0,)), ((), ()))):
    return lax.dot_general(a, b, dims, preferred_element_type=F32)


def call(body, outs, in_specs, scratch=()):
    return pl.pallas_call(
        body,
        out_shape=outs,
        in_specs=in_specs,
        out_specs=jax.tree.map(lambda _: VMEM, outs),
        scratch_shapes=list(scratch),
        compiler_params=pltpu.CompilerParams(vmem_limit_bytes=40 * 1024 * 1024),
    )


def halves(value):
    high = value.astype(BF).astype(F32)
    return jnp.concatenate([high, value - high], axis=0).astype(BF)


def prepare_kernel(steps, n_repl, blocks, counts, weights, cat, send, total):
    step = pl.program_id(0)
    per = counts.shape[0]
    for t in range(per):
        live = blocks[step * per + t] >= 0
        tile = jnp.where(live, counts[t], 0).astype(F32).astype(BF)
        cat[:, t * EDGE : (t + 1) * EDGE] = tile
    part = dot(jnp.ones((8, per * EDGE), BF), cat[...], NT)

    @pl.when(step == 0)
    def _():
        total[...] = part

    @pl.when(step > 0)
    def _():
        total[...] += part

    @pl.when(step == steps - 1)
    def _():
        whole = total[0:1]
        high = jnp.floor(whole * (1.0 / 256.0))
        low = whole - high * 256.0
        row = lax.broadcasted_iota(jnp.int32, (16, EDGE), 0)
        both = jnp.where(row == 0, high, jnp.where(row == 1, low, 0.0)).astype(BF)
        for r in range(n_repl):
            send[r, 0:192] = weights[...]
            send[r, 192:208] = both


def spread_kernel(blocks, core, cat, got, cot, mask, mine, other, up_out, inv_out):
    degree = jnp.zeros((1, EDGE), F32)
    for r in range(got.shape[0]):
        both = got[r, 192:208].astype(F32)
        degree = degree + both[0:1] * 256.0 + both[1:2]
    inverse = 1.0 / (degree + 1.0)
    inv_out[...] = jnp.broadcast_to(inverse, inv_out.shape)
    upstream = cot[...].astype(F32) * mask[...].astype(F32)
    up_out[...] = upstream.astype(BF)
    scaled = (upstream * inverse).astype(BF)
    mine[...] = jnp.zeros_like(mine)
    other[...] = jnp.zeros_like(other)
    me = core[0]
    for t in range(cat.shape[1] // EDGE):
        block = jnp.maximum(blocks[t], 0)
        product = dot(scaled, cat[:, t * EDGE : (t + 1) * EDGE])
        own = (block & 1) == me
        at = block >> 1
        mine[at] += jnp.where(own, product, 0.0)
        other[at] += jnp.where(own, 0.0, product)


def plane_sum_kernel(got, send):
    n_repl = send.shape[0] * WIDE // got.shape[1]
    total = got[0].astype(F32)
    for j in range(1, got.shape[0]):
        total = total + got[j].astype(F32)
    for h in range(got.shape[1] // WIDE):
        piece = total[h * WIDE : (h + 1) * WIDE].astype(BF)
        for r in range(n_repl):
            send[h * n_repl + r] = piece


def gather_one_kernel(blocks, core, own, far, cat, send, picked):
    me = core[0]
    n_repl, part = send.shape[0], own.shape[2]
    for t in range(cat.shape[1] // EDGE):
        block = jnp.maximum(blocks[t], 0)
        half = (block >> 1) & 1
        at = block >> 2
        near = (block & 1) == me
        for q in range(n_repl):
            a = own[half * n_repl + q, at]
            b = far[half * n_repl + q, at]
            picked[q * part : (q + 1) * part, t * EDGE : (t + 1) * EDGE] = jnp.where(near, a, b)
    total = dot(picked[...], cat[...], NT)
    for r in range(n_repl):
        send[r] = total


def layer_kernel(repl, parts, got, back, up, inv, features, send, skipped, packed):
    plane = send.shape[0]
    chunk = GRADS // plane
    total = parts[0]
    for r in range(1, parts.shape[0]):
        total = total + parts[r]
    mean = (total * inv[0:1]).astype(BF)
    feat = features[...]

    def before(r):
        bias = got[r, 128:192][:, 2 * WIDE - 1 : 2 * WIDE].astype(F32)
        return (dot(got[r, 0:64], feat) + dot(got[r, 64:128], mean)) + bias

    projections = jnp.zeros((EDGE, EDGE), F32)
    for r in range(parts.shape[0]):
        pre = before(r)
        hidden = (pre * jax.nn.sigmoid(pre)).astype(BF)
        projections = projections + dot(got[r, 128:192], hidden, TN)
    skipped[...] = projections[WIDE : 2 * WIDE]
    projected = projections[0:WIDE].astype(BF)

    pulled = back[0].astype(F32)
    for r in range(1, back.shape[0]):
        pulled = pulled + back[r].astype(F32)
    upstream = up[...]
    right = jnp.concatenate(
        [pulled, upstream.astype(F32), jnp.zeros((EDGE - 2 * WIDE, EDGE), F32)], axis=0
    ).astype(BF)
    mine = repl[0]
    pre = before(mine)
    sigmoid = jax.nn.sigmoid(pre)
    hidden = (pre * sigmoid).astype(BF)
    hidden_grad = dot(got[mine, 128:192], right)
    pre_grad = (hidden_grad * sigmoid * (1.0 + pre * (1.0 - sigmoid))).astype(BF)
    lane = lax.broadcasted_iota(jnp.int32, (EDGE, EDGE), 1)
    twice = jnp.concatenate([pre_grad, pre_grad], axis=0)
    packed[0:128] = jnp.where(lane < 64, dot(feat, twice, NT), dot(mean, twice, NT))
    bias_one = jnp.sum(pre_grad.astype(F32), axis=1, keepdims=True)
    bias_two = jnp.sum(upstream.astype(F32), axis=1, keepdims=True)
    bias_two = jnp.concatenate([bias_two, jnp.zeros((64 - WIDE, 1), F32)], axis=0)
    second = dot(hidden, right, NT)
    lane = lane[0:64]
    second = jnp.where(lane == 96, bias_one, jnp.where(lane == 97, bias_two, second))
    packed[128:192] = second
    packed[192:256] = jnp.zeros((64, EDGE), F32)
    for j in range(plane):
        send[j, 0:WIDE] = projected
        send[j, WIDE : WIDE + 2 * chunk] = halves(packed[j * chunk : (j + 1) * chunk])


def relay_kernel(repl, got, send):
    share = (send.shape[1] - (got.shape[1] - WIDE)) // WIDE
    chunk = (got.shape[1] - WIDE) // 2
    total = got[0, WIDE:].astype(F32)
    for j in range(1, got.shape[0]):
        total = total + got[j, WIDE:].astype(F32)
    both = halves(total[0:chunk] + total[chunk:])
    first = repl[0] * share
    for j in range(share):
        piece = got[first + j, 0:WIDE]
        for d in range(send.shape[0]):
            send[d, j * WIDE : (j + 1) * WIDE] = piece
    for d in range(send.shape[0]):
        send[d, share * WIDE :] = both


def gather_two_kernel(blocks, core, repl, own, far, cat, send, grads, picked):
    me = core[0]
    n_repl = send.shape[0]
    chunk = grads.shape[1]
    share = (own.shape[1] - 2 * chunk) // WIDE
    for t in range(cat.shape[1] // EDGE):
        block = jnp.maximum(blocks[t], 0)
        half = (block >> 1) & 1
        plane = block >> 2
        owner = plane // share
        at = pl.multiple_of((plane - owner * share) * WIDE, 16)
        near = (block & 1) == me
        a = own[half * n_repl + owner, pl.ds(at, WIDE)]
        b = far[half * n_repl + owner, pl.ds(at, WIDE)]
        picked[:, t * EDGE : (t + 1) * EDGE] = jnp.where(near, a, b)
    total = dot(picked[...], cat[...], NT)
    for r in range(n_repl):
        send[r] = total
    sums = []
    for ref in (own, far):
        both = jnp.zeros((2 * chunk, EDGE), F32)
        for h in range(own.shape[0] // n_repl):
            both = both + ref[h * n_repl + repl[0], share * WIDE :].astype(F32)
        sums.append(both[0:chunk] + both[chunk:])
    whole = sums[0] + sums[1]
    for j in range(grads.shape[0]):
        grads[j] = whole


def per_device(
    sizes,
    features,
    tile_blocks,
    tile_counts,
    train_mask,
    cotangent,
    self_one,
    neighbor_one,
    bias_one,
    self_two,
    neighbor_two,
    bias_two,
):
    n_repl = sizes["yl"]
    plane = sizes["x"] * sizes["z"]
    halves_n = sizes["yh"]
    column = halves_n * n_repl
    tiles = tile_counts.shape[0]
    chunk = GRADS // plane
    share = plane // n_repl
    core = lax.axis_index("core").astype(jnp.int32).reshape(1)
    repl = lax.axis_index("yl").astype(jnp.int32).reshape(1)
    swap = [(0, 1), (1, 0)]

    part = features.shape[0] // n_repl
    quarter = lax.dynamic_slice_in_dim(features, repl[0] * part, part, 0)
    quarters = lax.all_to_all(
        jnp.broadcast_to(quarter[None], (plane, part, EDGE)), PLANE, 0, 0, tiled=True
    )
    tile_counts, quarters = lax.optimization_barrier((tile_counts, quarters))
    near = lax.all_gather(quarters.reshape(plane * part, EDGE), COLUMN, axis=0, tiled=True)

    second = jnp.concatenate(
        [
            neighbor_two,
            jnp.zeros((64, WIDE - CLASSES), BF),
            self_two,
            bias_one[:, None],
            jnp.zeros((64, EDGE - 2 * WIDE), BF),
        ],
        axis=1,
    )
    weights = jnp.concatenate([self_one.T, neighbor_one.T, second], axis=0)
    steps = 4
    per = tiles // steps
    cat, send = pl.pallas_call(
        functools.partial(prepare_kernel, steps, n_repl),
        grid=(steps,),
        out_shape=(
            jax.ShapeDtypeStruct((EDGE, tiles * EDGE), BF),
            jax.ShapeDtypeStruct((n_repl, 208, EDGE), BF),
        ),
        in_specs=[
            SMEM,
            pl.BlockSpec((per, EDGE, EDGE), lambda i: (i, 0, 0)),
            pl.BlockSpec((192, EDGE), lambda i: (0, 0)),
        ],
        out_specs=(
            pl.BlockSpec((EDGE, per * EDGE), lambda i: (0, i)),
            pl.BlockSpec((n_repl, 208, EDGE), lambda i: (0, 0, 0)),
        ),
        scratch_shapes=[pltpu.VMEM((8, EDGE), F32)],
    )(tile_blocks, tile_counts, weights)
    got = lax.all_to_all(send, "yl", 0, 0, tiled=True)

    cot = jnp.pad(cotangent, ((0, WIDE - CLASSES), (0, 0)))
    mine, other, up, inv = call(
        spread_kernel,
        (
            jax.ShapeDtypeStruct((plane * halves_n, WIDE, EDGE), F32),
            jax.ShapeDtypeStruct((plane * halves_n, WIDE, EDGE), F32),
            jax.ShapeDtypeStruct((WIDE, EDGE), BF),
            jax.ShapeDtypeStruct((8, EDGE), F32),
        ),
        [SMEM, SMEM] + [VMEM] * 4,
    )(tile_blocks, core, cat, got, cot, train_mask[None, :])
    back = (mine + lax.ppermute(other, "core", swap)).astype(BF)
    back = lax.all_to_all(back.reshape(plane, halves_n * WIDE, EDGE), PLANE, 0, 0, tiled=True)
    back = call(plane_sum_kernel, jax.ShapeDtypeStruct((column, WIDE, EDGE), BF), [VMEM])(back)
    back = lax.all_to_all(back, COLUMN, 0, 0, tiled=True)

    far = lax.ppermute(near, "core", swap)
    shape = (column, plane, part, EDGE)
    parts = call(
        gather_one_kernel,
        jax.ShapeDtypeStruct((n_repl, EDGE, EDGE), F32),
        [SMEM, SMEM] + [VMEM] * 3,
        [pltpu.VMEM((EDGE, tiles * EDGE), BF)],
    )(tile_blocks, core, near.reshape(shape), far.reshape(shape), cat)
    parts = lax.all_to_all(parts, "yl", 0, 0, tiled=True)

    send, skipped = call(
        layer_kernel,
        (
            jax.ShapeDtypeStruct((plane, WIDE + 2 * chunk, EDGE), BF),
            jax.ShapeDtypeStruct((WIDE, EDGE), F32),
        ),
        [SMEM] + [VMEM] * 6,
        [pltpu.VMEM((GRADS, EDGE), F32)],
    )(repl, parts, got, back, up, inv, features)

    relay = lax.all_to_all(send, PLANE, 0, 0, tiled=True)
    relay = call(
        relay_kernel,
        jax.ShapeDtypeStruct((column, share * WIDE + 2 * chunk, EDGE), BF),
        [SMEM, VMEM],
    )(repl, relay)
    near_two = lax.all_to_all(relay, COLUMN, 0, 0, tiled=True)
    far_two = lax.ppermute(near_two, "core", swap)
    second_parts, grads = call(
        gather_two_kernel,
        (
            jax.ShapeDtypeStruct((n_repl, WIDE, EDGE), F32),
            jax.ShapeDtypeStruct((plane, chunk, EDGE), F32),
        ),
        [SMEM] * 3 + [VMEM] * 3,
        [pltpu.VMEM((WIDE, tiles * EDGE), BF)],
    )(tile_blocks, core, repl, near_two, far_two, cat)
    second_parts = lax.all_to_all(second_parts, "yl", 0, 0, tiled=True)
    grads = lax.all_to_all(grads, PLANE, 0, 0, tiled=True).reshape(GRADS, EDGE)

    second_sum = jnp.sum(second_parts, axis=0)
    scores = skipped + second_sum * inv[0:1]
    scores = scores[:CLASSES] + bias_two.astype(F32)[:, None]
    return (
        scores,
        grads[0:128, 0:64],
        grads[0:128, 64:128],
        grads[128:192, 96],
        grads[128:192, WIDE : WIDE + CLASSES],
        grads[128:192, 0:CLASSES],
        grads[128 : 128 + CLASSES, 97],
    )


def solution(mesh):
    sizes = {"x": 4, "z": 8, "yh": 2, "core": 2, "yl": 4}
    fine = Mesh(mesh.devices.reshape(tuple(sizes.values())), tuple(sizes))
    return sharded(fine, sizes)


def sharded(fine, sizes):
    both = ROWS + ("yl",)
    return jax.shard_map(
        functools.partial(per_device, sizes),
        mesh=fine,
        in_specs=(
            P(None, ROWS),
            P(both),
            P(both, None, None),
            P(ROWS),
            P(None, ROWS),
            P(None, "yl"),
            P(None, "yl"),
            P("yl"),
            P("yl", None),
            P("yl", None),
            P(),
        ),
        out_specs=(
            P(None, ROWS),
            P(None, "yl"),
            P(None, "yl"),
            P("yl"),
            P("yl", None),
            P("yl", None),
            P(),
        ),
        check_vma=False,
    )
```

time: 2170 us -> 227 us (0.10)
  waiting for transfers between devices: 1950 us -> 44.9 us
  blocking collectives: 47.4 us -> 110 us
  loops' own time: 54.2 us -> 0 us
  matrix products: 45 us -> 0 us
  starting transfers between devices: 0.2 us -> 30.3 us
  local copies, waits for them, and re-layouts: 41.6 us -> 11.8 us
    psum x2 -> x0, waiting for transfers between devices: 1530 us -> none  [the longest x1 1410 us: per_device(): lax.psum((selfgrad_one, neighgrad_one, biasgrad_one, selfgrad_two, neighg...]
    reduce_scatter x1 -> x0, waiting for transfers between devices: 252 us -> none  [per_device(): lax.psum_scatter(back_term, 'rows', scatter_dimension=1, tiled=True)]
    all_gather x2 -> x1, waiting for transfers between devices: 167 us -> 14.8 us  [per_device(): lax.all_gather(quarters.reshape(plane * part, EDGE), COLUMN, axis=0, tile...]
    all_to_all x0 -> x5, blocking collectives: none -> 110 us  [the longest x1 30.1 us: per_device(): lax.all_to_all(back.reshape(plane, halves_n * WIDE, EDGE), PLANE, 0, 0, t...]
    another operation x3 -> x0, loops' own time: 54.2 us -> none  [the longest x2 36.2 us: gather_terms(): lax.fori_loop(0, live_count, gather_advance, jnp.zeros((whole.shape[0], t...]
    psum x3 -> x0, blocking collectives: 47.4 us -> none  [pair_total(): return lax.psum((leading, trailing), 'repl')]
    dot_general x49 -> x0, matrix products: 45 us -> none  [the longest x26 26.2 us: gather_advance(): lax.dot_general(columns, counts, (((1,), (1,)), ((), ())), preferred_elem...]
    dynamic_slice x39 -> x1, local copies, waits for them, and re-layouts: 31.4 us -> 0.7 us  [per_device(): quarter = lax.dynamic_slice_in_dim(features, repl[0] * part, part, 0)]
  transfers between devices with their start and end apart: 5 -> 8, of which waited for: 5 -> 6; matrix products, arithmetic and copies ran while one was open for 2% -> 3% of each run, Pallas kernels for 0% -> 4%
where the time goes in v1:
time: 227 us; the launch traced here: 226 us
  blocking collectives  110 us (48%)
  waiting for transfers between devices  44.9 us (20%)
  starting transfers between devices  30.3 us (13%)
  between operations  14.2 us (6%)
  local copies, waits for them, and re-layouts  11.8 us (5%)
  Pallas kernels  10.7 us (5%)
  other arithmetic  4.28 us (2%)
    all_to_all x1, blocking collectives, per_device(): lax.all_to_all(back.reshape(plane, halves_n * WIDE, EDGE), PLANE, 0, 0, t...  30.1 us
    all_to_all x1, blocking collectives, per_device(): lax.all_to_all(jnp.broadcast_to(quarter[None], (plane, part, EDGE)), PLAN...  25.5 us
    all_to_all x1, blocking collectives, per_device(): near_two = lax.all_to_all(relay, COLUMN, 0, 0, tiled=True)  24 us
    all_to_all x1, blocking collectives, per_device(): relay = lax.all_to_all(send, PLANE, 0, 0, tiled=True)  19.2 us
    all_gather x1, waiting for transfers between devices, per_device(): lax.all_gather(quarters.reshape(plane * part, EDGE), COLUMN, axis=0, tile...  14.8 us
    all_to_all x1, blocking collectives, per_device(): parts = lax.all_to_all(parts, 'yl', 0, 0, tiled=True)  11 us
    unnamed x30, local copies, waits for them, and re-layouts  9.86 us
    all_to_all x1, waiting for transfers between devices, per_device(): grads = lax.all_to_all(grads, PLANE, 0, 0, tiled=True).reshape(GRADS, EDGE)  9.69 us
  transfers between devices with their start and end apart: 8, of which 6 were waited for; matrix products, arithmetic and copies ran while one was open for 3% of the time, Pallas kernels for 4%

profile of v1, /device:TPU:8, one launch (start us, length us, event | category | flops | bytes accessed | tf_op | source)
XLA Modules:
  0.0 226.2 jit_solution(6292783341516983628)
XLA Ops:
  8.0 25.5 %all_to_all.45 = bf16[32,32,128]{2,1,0:T(8,128)(2,1)} all-to-all(bf16[32,32,128]{2,1,0:T(8,128)(2,1)S(1)} %broadcast_in_dim.19), channel_id=1, replica_groups=mesh['x'=4,'z'=8,'yh'=2,'core'=2,'yl'=4] {'x','z'}, dimensions={0} | all-to-all | bytes 524288 | tf_op jit(solution)/shard_map/all_to_all | solution.py:246
  36.0 1.4 pad_maximum_fusion.weights
  37.4 4.1 %shard_map.162 = (bf16[128,4096]{1,0:T(8,128)(2,1)}, bf16[4,208,128]{2,1,0:T(8,128)(2,1)}) custom-call(s32[32]{0:T(128)} %blocks.7, s32[32,128,128]{2,1,0:T(8,128)} %counts, bf16[192,128]{1,0:T(8,128)(2,1)} %pad_maximum_fusion.weights), custom_call_target="tpu_custom_call" | custom-call | tf_op jit(solution)/shard_map/pallas_call | solution.py:265
  41.5 5.3 %all-to-all-start.2 = ((bf16[4,208,128]{2,1,0:T(8,128)(2,1)}), bf16[4,208,128]{2,1,0:T(8,128)(2,1)S(1)}, u32[]{:S(2)}, u32[]{:S(2)}) async-start(bf16[4,208,128]{2,1,0:T(8,128)(2,1)} %get-tuple-element.22), calls=%async_computation.2 | async-start | bytes 425984 | tf_op jit(solution)/shard_map/all_to_all | solution.py:283
  46.9 8.9 %all-to-all-done.2.got = bf16[4,208,128]{2,1,0:T(8,128)(2,1)S(1)} async-done(((bf16[4,208,128]{2,1,0:T(8,128)(2,1)}), bf16[4,208,128]{2,1,0:T(8,128)(2,1)S(1)}, u32[]{:S(2)}, u32[]{:S(2)}) %all-to-all-start.2) | async-done | bytes 213024 | tf_op jit(solution)/shard_map/all_to_all | solution.py:283
  55.8 1.2 copy-done
  59.4 1.9 collective-permute-start.1
  61.3 14.8 %all-gather.2.cloned.1.call-done = bf16[8192,128]{1,0:T(8,128)(2,1)} async-done(((bf16[1024,128]{1,0:T(8,128)(2,1)}), bf16[8192,128]{1,0:T(8,128)(2,1)}) %all-gather.2.cloned.1.call-update) | async-done | bytes 2097168 | tf_op jit(solution)/shard_map/all_gather | solution.py:250
  76.0 1.9 collective-permute-start
  79.1 2.2 add_convert_fusion
  81.4 30.1 %all_to_all.46.got = bf16[32,96,128]{2,1,0:T(8,128)(2,1)S(1)} all-to-all(bf16[32,96,128]{2,1,0:T(8,128)(2,1)S(1)} %bitcast.17), channel_id=1, replica_groups=mesh['x'=4,'z'=8,'yh'=2,'core'=2,'yl'=4] {'x','z'}, dimensions={0} | all-to-all | bytes 1572864 | tf_op jit(solution)/shard_map/all_to_all | solution.py:297
  112.2 5.5 %all-to-all-start.4 = ((bf16[8,48,128]{2,1,0:T(8,128)(2,1)}), bf16[8,48,128]{2,1,0:T(8,128)(2,1)S(1)}, u32[]{:S(2)}, u32[]{:S(2)}) async-start(bf16[8,48,128]{2,1,0:T(8,128)(2,1)} %shard_map.165), calls=%async_computation.4 | async-start | bytes 196608 | tf_op jit(solution)/shard_map/all_to_all | solution.py:299
  117.8 2.2 shard_map.163
  120.7 4.4 %all-to-all-done.4.back = bf16[8,48,128]{2,1,0:T(8,128)(2,1)S(1)} async-done(((bf16[8,48,128]{2,1,0:T(8,128)(2,1)}), bf16[8,48,128]{2,1,0:T(8,128)(2,1)S(1)}, u32[]{:S(2)}, u32[]{:S(2)}) %all-to-all-start.4) | async-done | bytes 98336 | tf_op jit(solution)/shard_map/all_to_all | solution.py:299
  125.0 11.0 %all_to_all.47.parts = f32[4,128,128]{2,1,0:T(8,128)S(1)} all-to-all(f32[4,128,128]{2,1,0:T(8,128)} %copy-done.4), channel_id=1, replica_groups=mesh['x'=4,'z'=8,'yh'=2,'core'=2,'yl'=4] {'yl'}, dimensions={0} | all-to-all | bytes 524288 | tf_op jit(solution)/shard_map/all_to_all | solution.py:309
  136.7 19.2 %all_to_all.48.got = bf16[32,64,128]{2,1,0:T(8,128)(2,1)S(1)} all-to-all(bf16[32,64,128]{2,1,0:T(8,128)(2,1)S(1)} %get-tuple-element.28), channel_id=1, replica_groups=mesh['x'=4,'z'=8,'yh'=2,'core'=2,'yl'=4] {'x','z'}, dimensions={0} | all-to-all | bytes 1048576 | tf_op jit(solution)/shard_map/all_to_all | solution.py:321
  156.1 24.0 %all_to_all.49.own = bf16[8,400,128]{2,1,0:T(8,128)(2,1)S(1)} all-to-all(bf16[8,400,128]{2,1,0:T(8,128)(2,1)S(1)} %shard_map.167), channel_id=1, replica_groups=mesh['x'=4,'z'=8,'yh'=2,'core'=2,'yl'=4] {'yh','yl'}, dimensions={0} | all-to-all | bytes 1638400 | tf_op jit(solution)/shard_map/all_to_all | solution.py:327
  180.1 2.0 collective-permute-start.2
  182.2 2.3 %collective-permute-done.2.far = bf16[8,400,128]{2,1,0:T(8,128)(2,1)S(1)} collective-permute-done((bf16[8,400,128]{2,1,0:T(8,128)(2,1)S(1)}, bf16[8,400,128]{2,1,0:T(8,128)(2,1)S(1)}, u32[]{:S(2)}, u32[]{:S(2)}) %collective-permute-start.2) | collective-permute-done | bytes 819232 | tf_op jit(solution)/shard_map/ppermute | solution.py:328
  184.5 1.7 shard_map.168
  186.2 4.7 %all-to-all-start.7 = ((f32[4,48,128]{2,1,0:T(8,128)}), f32[4,48,128]{2,1,0:T(8,128)S(1)}, u32[]{:S(2)}, u32[]{:S(2)}) async-start(f32[4,48,128]{2,1,0:T(8,128)} %get-tuple-element.29), calls=%async_computation.7 | async-start | bytes 196608 | tf_op jit(solution)/shard_map/all_to_all | solution.py:338
  190.9 4.9 %all-to-all-done.7 = f32[4,48,128]{2,1,0:T(8,128)S(1)} async-done(((f32[4,48,128]{2,1,0:T(8,128)}), f32[4,48,128]{2,1,0:T(8,128)S(1)}, u32[]{:S(2)}, u32[]{:S(2)}) %all-to-all-start.7) | async-done | bytes 98336 | tf_op jit(solution)/shard_map/all_to_all | solution.py:338
  195.8 8.9 %all-to-all-start.8 = ((f32[32,8,128]{2,1,0:T(8,128)}), f32[32,8,128]{2,1,0:T(8,128)S(1)}, u32[]{:S(2)}, u32[]{:S(2)}) async-start(f32[32,8,128]{2,1,0:T(8,128)} %get-tuple-element.30), calls=%async_computation.8 | async-start | bytes 262144 | tf_op jit(solution)/shard_map/all_to_all | solution.py:339
  205.4 9.7 %all-to-all-done.8 = f32[32,8,128]{2,1,0:T(8,128)S(1)} async-done(((f32[32,8,128]{2,1,0:T(8,128)}), f32[32,8,128]{2,1,0:T(8,128)S(1)}, u32[]{:S(2)}, u32[]{:S(2)}) %all-to-all-start.8) | async-done | bytes 131104 | tf_op jit(solution)/shard_map/all_to_all | solution.py:339
  (52 shorter events, 14.0 us)
Async XLA Ops:
  7.2 68.9 %all-gather.2.cloned.1.call-start = ((), (), s32[]{:S(2)}) async-start(), calls=%async_computation.9 | async-start | bytes 2359296 | tf_op jit(solution)/shard_map/all_gather | solution.py:250
  33.5 13.4 %copy-start.9 = (bf16[47,128]{1,0:T(8,128)(2,1)S(1)}, bf16[47,128]{1,0:T(8,128)(2,1)}, u32[]{:S(2)}) copy-start(bf16[47,128]{1,0:T(8,128)(2,1)} %param.15) | copy-start | bytes 36100
  33.5 22.3 %copy-start.6 = (s32[32]{0:T(128)S(1)}, s32[32]{0:T(128)}, u32[]{:S(2)}) copy-start(s32[32]{0:T(128)} %blocks.7) | copy-start | bytes 388
  33.5 22.3 %copy-start.7 = (s32[128]{0:T(128)S(1)}, s32[128]{0:T(128)}, u32[]{:S(2)}) copy-start(s32[128]{0:T(128)} %param.14) | copy-start | bytes 1540
  41.5 14.2 %all-to-all-start.2 = ((bf16[4,208,128]{2,1,0:T(8,128)(2,1)}), bf16[4,208,128]{2,1,0:T(8,128)(2,1)S(1)}, u32[]{:S(2)}, u32[]{:S(2)}) async-start(bf16[4,208,128]{2,1,0:T(8,128)(2,1)} %get-tuple-element.22), calls=%async_computation.2 | async-start | bytes 425984 | tf_op jit(solution)/shard_map/all_to_all | solution.py:283
  55.8 1.2 copy-start
  58.2 1.2 copy-start.3
  59.4 18.6 %collective-permute-start.1 = (f32[64,48,128]{2,1,0:T(8,128)S(1)}, f32[64,48,128]{2,1,0:T(8,128)S(1)}, u32[]{:S(2)}, u32[]{:S(2)}) collective-permute-start(f32[64,48,128]{2,1,0:T(8,128)S(1)} %get-tuple-element.24), channel_id=1, source_target_pairs={{0,4},{4,0},{1,5},{5,1},{2,6},{6,2},{3,7},{7,3},{8,12},{12,8},{9,1... | collective-permute-start | bytes 4718600 | tf_op jit(solution)/shard_map/ppermute | solution.py:296
  76.0 41.7 %collective-permute-start = (bf16[8192,128]{1,0:T(8,128)(2,1)}, bf16[8192,128]{1,0:T(8,128)(2,1)}, u32[]{:S(2)}, u32[]{:S(2)}) collective-permute-start(bf16[8192,128]{1,0:T(8,128)(2,1)} %all-gather.2.cloned.1.call-done), channel_id=1, source_target_pairs={{0,4},{4,0},{1,5},{5,1},{2,6},{6,2},{3,7},{7,3},{8,12},{12,8},{9,1... | collective-permute-start | bytes 6291464 | tf_op jit(solution)/shard_map/ppermute | solution.py:301
  78.0 1.1 copy-start.8
  79.1 38.6 %copy-start.2 = (bf16[8192,128]{1,0:T(8,128)(2,1)S(1)}, bf16[8192,128]{1,0:T(8,128)(2,1)}, u32[]{:S(2)}) copy-start(bf16[8192,128]{1,0:T(8,128)(2,1)} %all-gather.2.cloned.1.call-done) | copy-start | bytes 6291460
  81.3 36.4 %copy-start.1 = (bf16[128,4096]{1,0:T(8,128)(2,1)S(1)}, bf16[128,4096]{1,0:T(8,128)(2,1)}, u32[]{:S(2)}) copy-start(bf16[128,4096]{1,0:T(8,128)(2,1)} %get-tuple-element.21.cat) | copy-start | bytes 3145732
  112.2 12.8 %all-to-all-start.4 = ((bf16[8,48,128]{2,1,0:T(8,128)(2,1)}), bf16[8,48,128]{2,1,0:T(8,128)(2,1)S(1)}, u32[]{:S(2)}, u32[]{:S(2)}) async-start(bf16[8,48,128]{2,1,0:T(8,128)(2,1)} %shard_map.165), calls=%async_computation.4 | async-start | bytes 196608 | tf_op jit(solution)/shard_map/all_to_all | solution.py:299
  117.8 18.3 %copy-start.5 = (bf16[128,128]{1,0:T(8,128)(2,1)S(1)}, bf16[128,128]{1,0:T(8,128)(2,1)}, u32[]{:S(2)}) copy-start(bf16[128,128]{1,0:T(8,128)(2,1)} %features.1) | copy-start | bytes 98308
  120.0 0.7 copy-start.4
  180.1 10.8 %copy-start.10 = (bf16[47]{0:T(256)(128)(2,1)S(1)}, bf16[47]{0:T(256)(128)(2,1)}, u32[]{:S(2)}) copy-start(bf16[47]{0:T(256)(128)(2,1)} %param.21) | copy-start | bytes 286
  180.1 4.3 %collective-permute-start.2 = (bf16[8,400,128]{2,1,0:T(8,128)(2,1)S(1)}, bf16[8,400,128]{2,1,0:T(8,128)(2,1)S(1)}, u32[]{:S(2)}, u32[]{:S(2)}) collective-permute-start(bf16[8,400,128]{2,1,0:T(8,128)(2,1)S(1)} %all_to_all.49.own), channel_id=1, source_target_pairs={{0,4},{4,0},{1,5},{5,1},{2,6},{6,2},{3,7},{7,3},{8,12},{12,8},{9,1... | collective-permute-start | bytes 2457608 | tf_op jit(solution)/shard_map/ppermute | solution.py:328
  186.2 9.6 %all-to-all-start.7 = ((f32[4,48,128]{2,1,0:T(8,128)}), f32[4,48,128]{2,1,0:T(8,128)S(1)}, u32[]{:S(2)}, u32[]{:S(2)}) async-start(f32[4,48,128]{2,1,0:T(8,128)} %get-tuple-element.29), calls=%async_computation.7 | async-start | bytes 196608 | tf_op jit(solution)/shard_map/all_to_all | solution.py:338
  195.8 19.3 %all-to-all-start.8 = ((f32[32,8,128]{2,1,0:T(8,128)}), f32[32,8,128]{2,1,0:T(8,128)S(1)}, u32[]{:S(2)}, u32[]{:S(2)}) async-start(f32[32,8,128]{2,1,0:T(8,128)} %get-tuple-element.30), calls=%async_computation.8 | async-start | bytes 262144 | tf_op jit(solution)/shard_map/all_to_all | solution.py:339
Sparse Core Ops, SparseCore 0:
  33.6 42.3 all-gather.1

commit v2 on v1

--- a/solution.py
+++ b/solution.py
@@ -42,39 +42,47 @@
     return jnp.concatenate([high, value - high], axis=0).astype(BF)
 
 
-def prepare_kernel(steps, n_repl, blocks, counts, weights, cat, send, total):
+def prepare_kernel(
+    steps, n_repl, blocks, counts, self_one, neighbor_one, neighbor_two, self_two, bias, cat, send, total, second
+):
     step = pl.program_id(0)
     per = counts.shape[0]
+
+    @pl.when(step == 0)
+    def _():
+        total[...] = jnp.zeros_like(total)
+
+    running = total[...]
     for t in range(per):
         live = blocks[step * per + t] >= 0
-        tile = jnp.where(live, counts[t], 0).astype(F32).astype(BF)
-        cat[:, t * EDGE : (t + 1) * EDGE] = tile
-    part = dot(jnp.ones((8, per * EDGE), BF), cat[...], NT)
-
-    @pl.when(step == 0)
-    def _():
-        total[...] = part
-
-    @pl.when(step > 0)
-    def _():
-        total[...] += part
+        tile = jnp.where(live, counts[t], 0).astype(F32)
+        cat[:, t * EDGE : (t + 1) * EDGE] = tile.astype(BF)
+        running = running + tile
+    total[...] = running
 
     @pl.when(step == steps - 1)
     def _():
-        whole = total[0:1]
+        whole = dot(jnp.ones((8, EDGE), BF), running.astype(BF), NT)[0:1]
         high = jnp.floor(whole * (1.0 / 256.0))
         low = whole - high * 256.0
         row = lax.broadcasted_iota(jnp.int32, (16, EDGE), 0)
         both = jnp.where(row == 0, high, jnp.where(row == 1, low, 0.0)).astype(BF)
+        second[...] = jnp.zeros_like(second)
+        second[0:CLASSES, 0:64] = neighbor_two[...].astype(F32)
+        second[CLASSES:WIDE, 0:64] = bias[...].astype(F32)
+        second[0:CLASSES, 64:128] = self_two[...].astype(F32)
+        layer_two = second[...].astype(BF)
         for r in range(n_repl):
-            send[r, 0:192] = weights[...]
-            send[r, 192:208] = both
-
-
-def spread_kernel(blocks, core, cat, got, cot, mask, mine, other, up_out, inv_out):
+            send[r, 0:64] = self_one[...]
+            send[r, 64:128] = neighbor_one[...]
+            send[r, 128:176] = layer_two
+            send[r, 176:192] = both
+
+
+def spread_kernel(blocks, core, cat, got, cot, mask, mine, other, up_out, inv_out, far):
     degree = jnp.zeros((1, EDGE), F32)
     for r in range(got.shape[0]):
-        both = got[r, 192:208].astype(F32)
+        both = got[r, 176:192].astype(F32)
         degree = degree + both[0:1] * 256.0 + both[1:2]
     inverse = 1.0 / (degree + 1.0)
     inv_out[...] = jnp.broadcast_to(inverse, inv_out.shape)
@@ -82,7 +90,7 @@
     up_out[...] = upstream.astype(BF)
     scaled = (upstream * inverse).astype(BF)
     mine[...] = jnp.zeros_like(mine)
-    other[...] = jnp.zeros_like(other)
+    far[...] = jnp.zeros_like(far)
     me = core[0]
     for t in range(cat.shape[1] // EDGE):
         block = jnp.maximum(blocks[t], 0)
@@ -90,7 +98,12 @@
         own = (block & 1) == me
         at = block >> 1
         mine[at] += jnp.where(own, product, 0.0)
-        other[at] += jnp.where(own, 0.0, product)
+        far[at] += jnp.where(own, 0.0, product)
+    other[...] = far[...].astype(BF)
+
+
+def pair_sum_kernel(mine, other, total):
+    total[...] = (mine[...] + other[...].astype(F32)).astype(BF)
 
 
 def plane_sum_kernel(got, send):
@@ -121,7 +134,7 @@
         send[r] = total
 
 
-def layer_kernel(repl, parts, got, back, up, inv, features, send, skipped, packed):
+def layer_kernel(repl, parts, got, back, up, inv, features, bias_two, send, base, packed, pad):
     plane = send.shape[0]
     chunk = GRADS // plane
     total = parts[0]
@@ -129,43 +142,48 @@
         total = total + parts[r]
     mean = (total * inv[0:1]).astype(BF)
     feat = features[...]
+    last = lax.broadcasted_iota(jnp.int32, (WIDE, EDGE), 0) == CLASSES
+    unit = jnp.where(last, 1.0, 0.0).astype(BF)
+    none = jnp.zeros((64, EDGE), BF)
 
     def before(r):
-        bias = got[r, 128:192][:, 2 * WIDE - 1 : 2 * WIDE].astype(F32)
+        bias = dot(got[r, 128:176], unit, TN)[0:64]
         return (dot(got[r, 0:64], feat) + dot(got[r, 64:128], mean)) + bias
 
-    projections = jnp.zeros((EDGE, EDGE), F32)
+    projected = jnp.zeros((WIDE, EDGE), F32)
+    skipped = jnp.zeros((WIDE, EDGE), F32)
     for r in range(parts.shape[0]):
         pre = before(r)
         hidden = (pre * jax.nn.sigmoid(pre)).astype(BF)
-        projections = projections + dot(got[r, 128:192], hidden, TN)
-    skipped[...] = projections[WIDE : 2 * WIDE]
-    projected = projections[0:WIDE].astype(BF)
+        projected = projected + dot(got[r, 128:176], jnp.concatenate([hidden, none], axis=0))
+        skipped = skipped + dot(got[r, 128:176], jnp.concatenate([none, hidden], axis=0))
+    projected = projected.astype(BF)
+    pad[...] = jnp.zeros_like(pad)
+    pad[0:1, 0:CLASSES] = bias_two[...].astype(F32)
+    base[...] = skipped + dot(pad[...].astype(BF), jnp.ones((8, EDGE), BF), TN)[0:WIDE]
 
     pulled = back[0].astype(F32)
     for r in range(1, back.shape[0]):
         pulled = pulled + back[r].astype(F32)
+    pulled = pulled.astype(BF)
     upstream = up[...]
-    right = jnp.concatenate(
-        [pulled, upstream.astype(F32), jnp.zeros((EDGE - 2 * WIDE, EDGE), F32)], axis=0
-    ).astype(BF)
     mine = repl[0]
     pre = before(mine)
     sigmoid = jax.nn.sigmoid(pre)
     hidden = (pre * sigmoid).astype(BF)
-    hidden_grad = dot(got[mine, 128:192], right)
+    second = got[mine, 128:176]
+    hidden_grad = dot(second, upstream, TN)[64:128] + dot(second, pulled, TN)[0:64]
     pre_grad = (hidden_grad * sigmoid * (1.0 + pre * (1.0 - sigmoid))).astype(BF)
-    lane = lax.broadcasted_iota(jnp.int32, (EDGE, EDGE), 1)
-    twice = jnp.concatenate([pre_grad, pre_grad], axis=0)
-    packed[0:128] = jnp.where(lane < 64, dot(feat, twice, NT), dot(mean, twice, NT))
-    bias_one = jnp.sum(pre_grad.astype(F32), axis=1, keepdims=True)
-    bias_two = jnp.sum(upstream.astype(F32), axis=1, keepdims=True)
-    bias_two = jnp.concatenate([bias_two, jnp.zeros((64 - WIDE, 1), F32)], axis=0)
-    second = dot(hidden, right, NT)
-    lane = lane[0:64]
-    second = jnp.where(lane == 96, bias_one, jnp.where(lane == 97, bias_two, second))
-    packed[128:192] = second
-    packed[192:256] = jnp.zeros((64, EDGE), F32)
+    packed[0:64] = dot(pre_grad, feat, NT)
+    packed[64:128] = dot(pre_grad, mean, NT)
+    ones = jnp.ones((8, EDGE), BF)
+    twice = jnp.concatenate([hidden, hidden], axis=0)
+    left = lax.broadcasted_iota(jnp.int32, (WIDE, EDGE), 1) < 64
+    grads_two = jnp.where(left, dot(pulled, twice, NT), dot(upstream, twice, NT))
+    bias_one = dot(ones, jnp.concatenate([pre_grad, none], axis=0), NT)[0:1]
+    packed[128:176] = jnp.where(last, bias_one, grads_two)
+    packed[176:184] = dot(ones, jnp.concatenate([upstream, jnp.zeros((EDGE - WIDE, EDGE), BF)], axis=0), NT)
+    packed[184:256] = jnp.zeros((72, EDGE), F32)
     for j in range(plane):
         send[j, 0:WIDE] = projected
         send[j, WIDE : WIDE + 2 * chunk] = halves(packed[j * chunk : (j + 1) * chunk])
@@ -189,7 +207,7 @@
 
 def gather_two_kernel(blocks, core, repl, own, far, cat, send, grads, picked):
     me = core[0]
-    n_repl = send.shape[0]
+    n_repl = own.shape[0] // 2
     chunk = grads.shape[1]
     share = (own.shape[1] - 2 * chunk) // WIDE
     for t in range(cat.shape[1] // EDGE):
@@ -202,9 +220,7 @@
         a = own[half * n_repl + owner, pl.ds(at, WIDE)]
         b = far[half * n_repl + owner, pl.ds(at, WIDE)]
         picked[:, t * EDGE : (t + 1) * EDGE] = jnp.where(near, a, b)
-    total = dot(picked[...], cat[...], NT)
-    for r in range(n_repl):
-        send[r] = total
+    send[...] = dot(picked[...], cat[...], NT)
     sums = []
     for ref in (own, far):
         both = jnp.zeros((2 * chunk, EDGE), F32)
@@ -214,6 +230,26 @@
     whole = sums[0] + sums[1]
     for j in range(grads.shape[0]):
         grads[j] = whole
+
+
+def scores_kernel(repl, own, first, second, third, base, inv, scores, parts):
+    n_repl = parts.shape[0]
+    for k, ref in enumerate((own, first, second, third)[:n_repl]):
+        at = repl[0] + k
+        parts[jnp.where(at >= n_repl, at - n_repl, at)] = ref[...]
+    total = parts[0]
+    for r in range(1, n_repl):
+        total = total + parts[r]
+    scores[...] = (base[...] + total * inv[0:1])[0:CLASSES]
+
+
+def unpack_kernel(grads, self_one, neighbor_one, bias_one, self_two, neighbor_two, bias_two):
+    self_one[...] = grads[0:64]
+    neighbor_one[...] = grads[64:128]
+    neighbor_two[...] = grads[128 : 128 + CLASSES, 0:64]
+    self_two[...] = grads[128 : 128 + CLASSES, 64:128]
+    bias_one[...] = grads[175:176, 0:64]
+    bias_two[...] = grads[176:177, 0:CLASSES]
 
 
 def per_device(
@@ -249,37 +285,39 @@
     tile_counts, quarters = lax.optimization_barrier((tile_counts, quarters))
     near = lax.all_gather(quarters.reshape(plane * part, EDGE), COLUMN, axis=0, tiled=True)
 
-    second = jnp.concatenate(
-        [
-            neighbor_two,
-            jnp.zeros((64, WIDE - CLASSES), BF),
-            self_two,
-            bias_one[:, None],
-            jnp.zeros((64, EDGE - 2 * WIDE), BF),
-        ],
-        axis=1,
-    )
-    weights = jnp.concatenate([self_one.T, neighbor_one.T, second], axis=0)
     steps = 4
     per = tiles // steps
+    whole = lambda shape: pl.BlockSpec(shape, lambda i: (0,) * len(shape))
     cat, send = pl.pallas_call(
         functools.partial(prepare_kernel, steps, n_repl),
         grid=(steps,),
         out_shape=(
             jax.ShapeDtypeStruct((EDGE, tiles * EDGE), BF),
-            jax.ShapeDtypeStruct((n_repl, 208, EDGE), BF),
+            jax.ShapeDtypeStruct((n_repl, 192, EDGE), BF),
         ),
         in_specs=[
             SMEM,
             pl.BlockSpec((per, EDGE, EDGE), lambda i: (i, 0, 0)),
-            pl.BlockSpec((192, EDGE), lambda i: (0, 0)),
+            whole((64, EDGE)),
+            whole((64, EDGE)),
+            whole((CLASSES, 64)),
+            whole((CLASSES, 64)),
+            whole((1, 64)),
         ],
         out_specs=(
             pl.BlockSpec((EDGE, per * EDGE), lambda i: (0, i)),
-            pl.BlockSpec((n_repl, 208, EDGE), lambda i: (0, 0, 0)),
-        ),
-        scratch_shapes=[pltpu.VMEM((8, EDGE), F32)],
-    )(tile_blocks, tile_counts, weights)
+            whole((n_repl, 192, EDGE)),
+        ),
+        scratch_shapes=[pltpu.VMEM((EDGE, EDGE), F32), pltpu.VMEM((WIDE, EDGE), F32)],
+    )(
+        tile_blocks,
+        tile_counts,
+        self_one.T,
+        neighbor_one.T,
+        neighbor_two.T,
+        self_two.T,
+        bias_one[None, :],
+    )
     got = lax.all_to_all(send, "yl", 0, 0, tiled=True)
 
     cot = jnp.pad(cotangent, ((0, WIDE - CLASSES), (0, 0)))
@@ -287,18 +325,24 @@
         spread_kernel,
         (
             jax.ShapeDtypeStruct((plane * halves_n, WIDE, EDGE), F32),
-            jax.ShapeDtypeStruct((plane * halves_n, WIDE, EDGE), F32),
+            jax.ShapeDtypeStruct((plane * halves_n, WIDE, EDGE), BF),
             jax.ShapeDtypeStruct((WIDE, EDGE), BF),
             jax.ShapeDtypeStruct((8, EDGE), F32),
         ),
         [SMEM, SMEM] + [VMEM] * 4,
+        [pltpu.VMEM((plane * halves_n, WIDE, EDGE), F32)],
     )(tile_blocks, core, cat, got, cot, train_mask[None, :])
-    back = (mine + lax.ppermute(other, "core", swap)).astype(BF)
+    back = call(
+        pair_sum_kernel,
+        jax.ShapeDtypeStruct((plane * halves_n, WIDE, EDGE), BF),
+        [VMEM] * 2,
+    )(mine, lax.ppermute(other, "core", swap))
     back = lax.all_to_all(back.reshape(plane, halves_n * WIDE, EDGE), PLANE, 0, 0, tiled=True)
+    near, back = lax.optimization_barrier((near, back))
+    far = lax.ppermute(near, "core", swap)
     back = call(plane_sum_kernel, jax.ShapeDtypeStruct((column, WIDE, EDGE), BF), [VMEM])(back)
     back = lax.all_to_all(back, COLUMN, 0, 0, tiled=True)
 
-    far = lax.ppermute(near, "core", swap)
     shape = (column, plane, part, EDGE)
     parts = call(
         gather_one_kernel,
@@ -308,15 +352,15 @@
     )(tile_blocks, core, near.reshape(shape), far.reshape(shape), cat)
     parts = lax.all_to_all(parts, "yl", 0, 0, tiled=True)
 
-    send, skipped = call(
+    send, base = call(
         layer_kernel,
         (
             jax.ShapeDtypeStruct((plane, WIDE + 2 * chunk, EDGE), BF),
             jax.ShapeDtypeStruct((WIDE, EDGE), F32),
         ),
-        [SMEM] + [VMEM] * 6,
-        [pltpu.VMEM((GRADS, EDGE), F32)],
-    )(repl, parts, got, back, up, inv, features)
+        [SMEM] + [VMEM] * 7,
+        [pltpu.VMEM((GRADS, EDGE), F32), pltpu.VMEM((8, EDGE), F32)],
+    )(repl, parts, got, back, up, inv, features, bias_two[None, :])
 
     relay = lax.all_to_all(send, PLANE, 0, 0, tiled=True)
     relay = call(
@@ -326,29 +370,49 @@
     )(repl, relay)
     near_two = lax.all_to_all(relay, COLUMN, 0, 0, tiled=True)
     far_two = lax.ppermute(near_two, "core", swap)
-    second_parts, grads = call(
+    second, grads = call(
         gather_two_kernel,
         (
-            jax.ShapeDtypeStruct((n_repl, WIDE, EDGE), F32),
+            jax.ShapeDtypeStruct((WIDE, EDGE), F32),
             jax.ShapeDtypeStruct((plane, chunk, EDGE), F32),
         ),
         [SMEM] * 3 + [VMEM] * 3,
         [pltpu.VMEM((WIDE, tiles * EDGE), BF)],
     )(tile_blocks, core, repl, near_two, far_two, cat)
-    second_parts = lax.all_to_all(second_parts, "yl", 0, 0, tiled=True)
+    others = [
+        lax.ppermute(second, "yl", [((i + k) % n_repl, i) for i in range(n_repl)])
+        for k in range(1, n_repl)
+    ]
     grads = lax.all_to_all(grads, PLANE, 0, 0, tiled=True).reshape(GRADS, EDGE)
-
-    second_sum = jnp.sum(second_parts, axis=0)
-    scores = skipped + second_sum * inv[0:1]
-    scores = scores[:CLASSES] + bias_two.astype(F32)[:, None]
+    others = others + [second] * (3 - len(others))
+    scores = call(
+        scores_kernel,
+        jax.ShapeDtypeStruct((CLASSES, EDGE), F32),
+        [SMEM] + [VMEM] * 6,
+        [pltpu.VMEM((n_repl, WIDE, EDGE), F32)],
+    )(repl, second, *others, base, inv)
+    one = jax.ShapeDtypeStruct((64, EDGE), F32)
+    two = jax.ShapeDtypeStruct((CLASSES, 64), F32)
+    self_one, neighbor_one, bias_one, self_two, neighbor_two, bias_two = call(
+        unpack_kernel,
+        (
+            one,
+            one,
+            jax.ShapeDtypeStruct((1, 64), F32),
+            two,
+            two,
+            jax.ShapeDtypeStruct((1, CLASSES), F32),
+        ),
+        [VMEM],
+    )(grads)
     return (
         scores,
-        grads[0:128, 0:64],
-        grads[0:128, 64:128],
-        grads[128:192, 96],
-        grads[128:192, WIDE : WIDE + CLASSES],
-        grads[128:192, 0:CLASSES],
-        grads[128 : 128 + CLASSES, 97],
+        self_one.T,
+        neighbor_one.T,
+        bias_one[0],
+        self_two.T,
+        neighbor_two.T,
+        bias_two[0],
     )
 
 

time: 227 us -> 196 us (0.86)
  the two profiles are of different devices: /device:TPU:8 before, /device:TPU:2 now
where the time goes in v2:
time: 196 us; the launch traced here: 195 us
  blocking collectives  106 us (54%)
  starting transfers between devices  36.4 us (19%)
  waiting for transfers between devices  23.1 us (12%)
  between operations  14.2 us (7%)
  Pallas kernels  12.5 us (6%)
  local copies, waits for them, and re-layouts  3.61 us (2%)
    all_to_all x1, blocking collectives, per_device(): lax.all_to_all(back.reshape(plane, halves_n * WIDE, EDGE), PLANE, 0, 0, t...  25.5 us
    all_to_all x1, blocking collectives, per_device(): near_two = lax.all_to_all(relay, COLUMN, 0, 0, tiled=True)  25.1 us
    all_to_all x1, blocking collectives, per_device(): lax.all_to_all(jnp.broadcast_to(quarter[None], (plane, part, EDGE)), PLAN...  24.7 us
    all_to_all x1, blocking collectives, per_device(): relay = lax.all_to_all(send, PLANE, 0, 0, tiled=True)  19.7 us
    all_to_all x1, blocking collectives, per_device(): parts = lax.all_to_all(parts, 'yl', 0, 0, tiled=True)  10.7 us
    all_to_all x1, starting transfers between devices, per_device(): grads = lax.all_to_all(grads, PLANE, 0, 0, tiled=True).reshape(GRADS, EDGE)  10 us
    ppermute x3, starting transfers between devices, per_device(): lax.ppermute(second, 'yl', [((i + k) % n_repl, i) for i in range(n_repl)])  8.27 us
    all_to_all x1, waiting for transfers between devices, per_device(): got = lax.all_to_all(send, 'yl', 0, 0, tiled=True)  8.18 us
  transfers between devices with their start and end apart: 10, of which 6 were waited for; matrix products, arithmetic and copies ran while one was open for 0% of the time, Pallas kernels for 5%

profile of v2, /device:TPU:2, one launch (start us, length us, event | category | flops | bytes accessed | tf_op | source)
XLA Modules:
  0.0 195.4 jit_solution(2844049804878656854)
XLA Ops:
  8.0 24.7 %all_to_all.40 = bf16[32,32,128]{2,1,0:T(8,128)(2,1)} all-to-all(bf16[32,32,128]{2,1,0:T(8,128)(2,1)S(1)} %broadcast_in_dim.15), channel_id=1, replica_groups=mesh['x'=4,'z'=8,'yh'=2,'core'=2,'yl'=4] {'x','z'}, dimensions={0} | all-to-all | bytes 524288 | tf_op jit(solution)/shard_map/all_to_all | solution.py:282
  32.7 4.0 %shard_map.162 = (bf16[128,4096]{1,0:T(8,128)(2,1)}, bf16[4,192,128]{2,1,0:T(8,128)(2,1)}) custom-call(s32[32]{0:T(128)} %blocks.7, s32[32,128,128]{2,1,0:T(8,128)} %counts, bf16[64,128]{1,0:T(8,128)(2,1)} %bitcast.26, bf16[64,128]{1,0:T(8,128)(2,1)} %bitcast.27, bf16[47,64]{1,0:T(8,128)(2,1)} %bitcast.28, bf16[47,64]{1,0:T(8,128)(2,1)} %bitcast.29, ...), custom_call_target="tpu_custom_call" | custom-call | tf_op jit(solution)/shard_map/pallas_call | solution.py:291
  36.7 4.9 %all-to-all-start.1 = ((bf16[4,192,128]{2,1,0:T(8,128)(2,1)}), bf16[4,192,128]{2,1,0:T(8,128)(2,1)S(1)}, u32[]{:S(2)}, u32[]{:S(2)}) async-start(bf16[4,192,128]{2,1,0:T(8,128)(2,1)} %get-tuple-element.30), calls=%async_computation.1 | async-start | bytes 393216 | tf_op jit(solution)/shard_map/all_to_all | solution.py:321
  41.6 8.2 %all-to-all-done.1.got = bf16[4,192,128]{2,1,0:T(8,128)(2,1)S(1)} async-done(((bf16[4,192,128]{2,1,0:T(8,128)(2,1)}), bf16[4,192,128]{2,1,0:T(8,128)(2,1)S(1)}, u32[]{:S(2)}, u32[]{:S(2)}) %all-to-all-start.1) | async-done | bytes 196640 | tf_op jit(solution)/shard_map/all_to_all | solution.py:321
  51.0 1.2 shard_map.163
  52.3 1.9 collective-permute-start
  54.2 2.3 %collective-permute-done.other = bf16[64,48,128]{2,1,0:T(8,128)(2,1)S(1)} collective-permute-done((bf16[64,48,128]{2,1,0:T(8,128)(2,1)S(1)}, bf16[64,48,128]{2,1,0:T(8,128)(2,1)S(1)}, u32[]{:S(2)}, u32[]{:S(2)}) %collective-permute-start) | collective-permute-done | bytes 786464 | tf_op jit(solution)/shard_map/ppermute | solution.py:339
  56.6 25.5 %all_to_all.41.got = bf16[32,96,128]{2,1,0:T(8,128)(2,1)S(1)} all-to-all(bf16[32,96,128]{2,1,0:T(8,128)(2,1)S(1)} %bitcast.20), channel_id=1, replica_groups=mesh['x'=4,'z'=8,'yh'=2,'core'=2,'yl'=4] {'x','z'}, dimensions={0} | all-to-all | bytes 1572864 | tf_op jit(solution)/shard_map/all_to_all | solution.py:340
  82.1 1.9 collective-permute-start.1
  84.8 7.5 %all-to-all-start.4 = ((bf16[8,48,128]{2,1,0:T(8,128)(2,1)}), bf16[8,48,128]{2,1,0:T(8,128)(2,1)S(1)}, u32[]{:S(2)}, u32[]{:S(2)}) async-start(bf16[8,48,128]{2,1,0:T(8,128)(2,1)} %shard_map.166), calls=%async_computation.4 | async-start | bytes 196608 | tf_op jit(solution)/shard_map/all_to_all | solution.py:344
  92.3 1.6 copy-done.2
  93.9 2.2 %shard_map.165 = f32[4,128,128]{2,1,0:T(8,128)S(1)} custom-call(s32[32]{0:T(128)S(1)} %copy-done.4, s32[1]{0:T(128)} %bitcast.1.core, bf16[8,32,32,128]{3,2,1,0:T(8,128)(2,1)S(1)} %bitcast.21, bf16[8,32,32,128]{3,2,1,0:T(8,128)(2,1)} %bitcast.11.far, bf16[128,4096]{1,0:T(8,128)(2,1)S(1)} %copy-done.1), custom_call_target="tpu_custom_call" | custom-call | tf_op jit(solution)/shard_map/pallas_call | solution.py:347
  96.1 5.2 %all-to-all-done.4.back = bf16[8,48,128]{2,1,0:T(8,128)(2,1)S(1)} async-done(((bf16[8,48,128]{2,1,0:T(8,128)(2,1)}), bf16[8,48,128]{2,1,0:T(8,128)(2,1)S(1)}, u32[]{:S(2)}, u32[]{:S(2)}) %all-to-all-start.4) | async-done | bytes 98336 | tf_op jit(solution)/shard_map/all_to_all | solution.py:344
  101.3 10.7 %all_to_all.42.parts = f32[4,128,128]{2,1,0:T(8,128)S(1)} all-to-all(f32[4,128,128]{2,1,0:T(8,128)S(1)} %shard_map.165), channel_id=1, replica_groups=mesh['x'=4,'z'=8,'yh'=2,'core'=2,'yl'=4] {'yl'}, dimensions={0} | all-to-all | bytes 524288 | tf_op jit(solution)/shard_map/all_to_all | solution.py:353
  113.1 19.7 %all_to_all.43.got = bf16[32,64,128]{2,1,0:T(8,128)(2,1)S(1)} all-to-all(bf16[32,64,128]{2,1,0:T(8,128)(2,1)S(1)} %get-tuple-element.37), channel_id=1, replica_groups=mesh['x'=4,'z'=8,'yh'=2,'core'=2,'yl'=4] {'x','z'}, dimensions={0} | all-to-all | bytes 1048576 | tf_op jit(solution)/shard_map/all_to_all | solution.py:365
  132.9 25.1 %all_to_all.44.own = bf16[8,400,128]{2,1,0:T(8,128)(2,1)S(1)} all-to-all(bf16[8,400,128]{2,1,0:T(8,128)(2,1)S(1)} %shard_map.168), channel_id=1, replica_groups=mesh['x'=4,'z'=8,'yh'=2,'core'=2,'yl'=4] {'yh','yl'}, dimensions={0} | all-to-all | bytes 1638400 | tf_op jit(solution)/shard_map/all_to_all | solution.py:371
  158.0 1.9 collective-permute-start.2
  159.9 2.3 %collective-permute-done.2.far = bf16[8,400,128]{2,1,0:T(8,128)(2,1)S(1)} collective-permute-done((bf16[8,400,128]{2,1,0:T(8,128)(2,1)S(1)}, bf16[8,400,128]{2,1,0:T(8,128)(2,1)S(1)}, u32[]{:S(2)}, u32[]{:S(2)}) %collective-permute-start.2) | collective-permute-done | bytes 819232 | tf_op jit(solution)/shard_map/ppermute | solution.py:372
  162.2 1.6 shard_map.169
  163.8 10.0 %all-to-all-start.7 = ((f32[32,8,128]{2,1,0:T(8,128)}), f32[32,8,128]{2,1,0:T(8,128)S(1)}, u32[]{:S(2)}, u32[]{:S(2)}) async-start(f32[32,8,128]{2,1,0:T(8,128)} %get-tuple-element.40), calls=%async_computation.7 | async-start | bytes 262144 | tf_op jit(solution)/shard_map/all_to_all | solution.py:386
  173.9 2.4 %collective-permute-start.3 = (f32[48,128]{1,0:T(8,128)S(1)}, f32[48,128]{1,0:T(8,128)S(1)}, u32[]{:S(2)}, u32[]{:S(2)}) collective-permute-start(f32[48,128]{1,0:T(8,128)S(1)} %get-tuple-element.38.own), channel_id=1, source_target_pairs={{1,0},{2,1},{3,2},{0,3},{5,4},{6,5},{7,6},{4,7},{9,8},{10,9},{11,1... | collective-permute-start | bytes 73736 | tf_op jit(solution)/shard_map/ppermute | solution.py:383
  176.3 3.5 %collective-permute-start.4 = (f32[48,128]{1,0:T(8,128)S(1)}, f32[48,128]{1,0:T(8,128)S(1)}, u32[]{:S(2)}, u32[]{:S(2)}) collective-permute-start(f32[48,128]{1,0:T(8,128)S(1)} %get-tuple-element.38.own), channel_id=1, source_target_pairs={{2,0},{3,1},{0,2},{1,3},{6,4},{7,5},{4,6},{5,7},{10,8},{11,9},{8,1... | collective-permute-start | bytes 73736 | tf_op jit(solution)/shard_map/ppermute | solution.py:383
  179.7 2.4 %collective-permute-start.5 = (f32[48,128]{1,0:T(8,128)S(1)}, f32[48,128]{1,0:T(8,128)S(1)}, u32[]{:S(2)}, u32[]{:S(2)}) collective-permute-start(f32[48,128]{1,0:T(8,128)S(1)} %get-tuple-element.38.own), channel_id=1, source_target_pairs={{3,0},{0,1},{1,2},{2,3},{7,4},{4,5},{5,6},{6,7},{11,8},{8,9},{9,10... | collective-permute-start | bytes 73736 | tf_op jit(solution)/shard_map/ppermute | solution.py:383
  182.9 4.4 %collective-permute-done.5.third = f32[48,128]{1,0:T(8,128)S(1)} collective-permute-done((f32[48,128]{1,0:T(8,128)S(1)}, f32[48,128]{1,0:T(8,128)S(1)}, u32[]{:S(2)}, u32[]{:S(2)}) %collective-permute-start.5) | collective-permute-done | bytes 24608 | tf_op jit(solution)/shard_map/ppermute | solution.py:383
  (31 shorter events, 6.2 us)
Async XLA Ops:
  7.2 42.6 %copy-start.4 = (s32[32]{0:T(128)S(1)}, s32[32]{0:T(128)}, u32[]{:S(2)}) copy-start(s32[32]{0:T(128)} %blocks.7) | copy-start | bytes 388
  7.2 34.4 %copy-start.7 = (bf16[47,128]{1,0:T(8,128)(2,1)S(1)}, bf16[47,128]{1,0:T(8,128)(2,1)}, u32[]{:S(2)}) copy-start(bf16[47,128]{1,0:T(8,128)(2,1)} %param.15) | copy-start | bytes 36100
  7.2 42.6 %copy-start.5 = (s32[128]{0:T(128)S(1)}, s32[128]{0:T(128)}, u32[]{:S(2)}) copy-start(s32[128]{0:T(128)} %param.14) | copy-start | bytes 1540
  7.2 74.9 %all-gather.2.cloned.1.call-start = ((), (), s32[]{:S(2)}) async-start(), calls=%async_computation.8 | async-start | bytes 2359296 | tf_op jit(solution)/shard_map/all_gather | solution.py:286
  36.7 13.1 %all-to-all-start.1 = ((bf16[4,192,128]{2,1,0:T(8,128)(2,1)}), bf16[4,192,128]{2,1,0:T(8,128)(2,1)S(1)}, u32[]{:S(2)}, u32[]{:S(2)}) async-start(bf16[4,192,128]{2,1,0:T(8,128)(2,1)} %get-tuple-element.30), calls=%async_computation.1 | async-start | bytes 393216 | tf_op jit(solution)/shard_map/all_to_all | solution.py:321
  49.8 1.2 copy-start
  52.3 4.2 %collective-permute-start = (bf16[64,48,128]{2,1,0:T(8,128)(2,1)S(1)}, bf16[64,48,128]{2,1,0:T(8,128)(2,1)S(1)}, u32[]{:S(2)}, u32[]{:S(2)}) collective-permute-start(bf16[64,48,128]{2,1,0:T(8,128)(2,1)S(1)} %get-tuple-element.32), channel_id=1, source_target_pairs={{0,4},{4,0},{1,5},{5,1},{2,6},{6,2},{3,7},{7,3},{8,12},{12,8},{9,1... | collective-permute-start | bytes 2359304 | tf_op jit(solution)/shard_map/ppermute | solution.py:339
  56.6 35.7 %copy-start.1 = (bf16[128,4096]{1,0:T(8,128)(2,1)S(1)}, bf16[128,4096]{1,0:T(8,128)(2,1)}, u32[]{:S(2)}) copy-start(bf16[128,4096]{1,0:T(8,128)(2,1)} %get-tuple-element.29.cat) | copy-start | bytes 3145732
  82.1 10.1 %collective-permute-start.1 = (bf16[8192,128]{1,0:T(8,128)(2,1)}, bf16[8192,128]{1,0:T(8,128)(2,1)}, u32[]{:S(2)}, u32[]{:S(2)}) collective-permute-start(bf16[8192,128]{1,0:T(8,128)(2,1)} %all-gather.2.cloned.1.call-done), channel_id=1, source_target_pairs={{0,4},{4,0},{1,5},{5,1},{2,6},{6,2},{3,7},{7,3},{8,12},{12,8},{9,1... | collective-permute-start | bytes 6291464 | tf_op jit(solution)/shard_map/ppermute | solution.py:342
  84.8 16.5 %all-to-all-start.4 = ((bf16[8,48,128]{2,1,0:T(8,128)(2,1)}), bf16[8,48,128]{2,1,0:T(8,128)(2,1)S(1)}, u32[]{:S(2)}, u32[]{:S(2)}) async-start(bf16[8,48,128]{2,1,0:T(8,128)(2,1)} %shard_map.166), calls=%async_computation.4 | async-start | bytes 196608 | tf_op jit(solution)/shard_map/all_to_all | solution.py:344
  92.3 1.6 copy-start.2
  93.9 18.1 %copy-start.3 = (bf16[128,128]{1,0:T(8,128)(2,1)S(1)}, bf16[128,128]{1,0:T(8,128)(2,1)}, u32[]{:S(2)}) copy-start(bf16[128,128]{1,0:T(8,128)(2,1)} %features.1) | copy-start | bytes 98308
  93.9 18.1 %copy-start.6 = (bf16[47]{0:T(256)(128)(2,1)S(1)}, bf16[47]{0:T(256)(128)(2,1)}, u32[]{:S(2)}) copy-start(bf16[47]{0:T(256)(128)(2,1)} %param.21) | copy-start | bytes 286
  158.0 4.2 %collective-permute-start.2 = (bf16[8,400,128]{2,1,0:T(8,128)(2,1)S(1)}, bf16[8,400,128]{2,1,0:T(8,128)(2,1)S(1)}, u32[]{:S(2)}, u32[]{:S(2)}) collective-permute-start(bf16[8,400,128]{2,1,0:T(8,128)(2,1)S(1)} %all_to_all.44.own), channel_id=1, source_target_pairs={{0,4},{4,0},{1,5},{5,1},{2,6},{6,2},{3,7},{7,3},{8,12},{12,8},{9,1... | collective-permute-start | bytes 2457608 | tf_op jit(solution)/shard_map/ppermute | solution.py:372
  163.8 24.0 %all-to-all-start.7 = ((f32[32,8,128]{2,1,0:T(8,128)}), f32[32,8,128]{2,1,0:T(8,128)S(1)}, u32[]{:S(2)}, u32[]{:S(2)}) async-start(f32[32,8,128]{2,1,0:T(8,128)} %get-tuple-element.40), calls=%async_computation.7 | async-start | bytes 262144 | tf_op jit(solution)/shard_map/all_to_all | solution.py:386
  173.9 8.3 %collective-permute-start.3 = (f32[48,128]{1,0:T(8,128)S(1)}, f32[48,128]{1,0:T(8,128)S(1)}, u32[]{:S(2)}, u32[]{:S(2)}) collective-permute-start(f32[48,128]{1,0:T(8,128)S(1)} %get-tuple-element.38.own), channel_id=1, source_target_pairs={{1,0},{2,1},{3,2},{0,3},{5,4},{6,5},{7,6},{4,7},{9,8},{10,9},{11,1... | collective-permute-start | bytes 73736 | tf_op jit(solution)/shard_map/ppermute | solution.py:383
  176.3 6.6 %collective-permute-start.4 = (f32[48,128]{1,0:T(8,128)S(1)}, f32[48,128]{1,0:T(8,128)S(1)}, u32[]{:S(2)}, u32[]{:S(2)}) collective-permute-start(f32[48,128]{1,0:T(8,128)S(1)} %get-tuple-element.38.own), channel_id=1, source_target_pairs={{2,0},{3,1},{0,2},{1,3},{6,4},{7,5},{4,6},{5,7},{10,8},{11,9},{8,1... | collective-permute-start | bytes 73736 | tf_op jit(solution)/shard_map/ppermute | solution.py:383
  179.7 7.5 %collective-permute-start.5 = (f32[48,128]{1,0:T(8,128)S(1)}, f32[48,128]{1,0:T(8,128)S(1)}, u32[]{:S(2)}, u32[]{:S(2)}) collective-permute-start(f32[48,128]{1,0:T(8,128)S(1)} %get-tuple-element.38.own), channel_id=1, source_target_pairs={{3,0},{0,1},{1,2},{2,3},{7,4},{4,5},{5,6},{6,7},{11,8},{8,9},{9,10... | collective-permute-start | bytes 73736 | tf_op jit(solution)/shard_map/ppermute | solution.py:383
Sparse Core Ops, SparseCore 0:
  32.8 41.5 all-gather.1

commit v3 on v2

v3 whole, which is shorter than its diff:
```python
import functools

import jax
import jax.numpy as jnp
from jax import lax
from jax.experimental import pallas as pl
from jax.experimental.pallas import tpu as pltpu
from jax.sharding import Mesh, PartitionSpec as P

BF = jnp.bfloat16
F32 = jnp.float32
CLASSES = 47
WIDE = 48
EDGE = 128
ROWS = ("x", "z", "yh", "core")
PLANE = ("x", "z")
COLUMN = ("yh", "yl")
SHEET = ("z", "yh")
GRADS = 256
VMEM = pl.BlockSpec(memory_space=pltpu.VMEM)
SMEM = pl.BlockSpec(memory_space=pltpu.SMEM)
NT = (((1,), (1,)), ((), ()))
TN = (((0,), (0,)), ((), ()))


def dot(a, b, dims=(((1,), (0,)), ((), ()))):
    return lax.dot_general(a, b, dims, preferred_element_type=F32)


def call(body, outs, in_specs, scratch=(), room=40):
    return pl.pallas_call(
        body,
        out_shape=outs,
        in_specs=in_specs,
        out_specs=jax.tree.map(lambda _: VMEM, outs),
        scratch_shapes=list(scratch),
        compiler_params=pltpu.CompilerParams(vmem_limit_bytes=room * 1024 * 1024),
    )


def halves(value):
    high = value.astype(BF).astype(F32)
    return jnp.concatenate([high, value - high], axis=0).astype(BF)


def lay_kernel(blocks, counts, cat):
    for t in range(counts.shape[0]):
        tile = jnp.where(blocks[t] >= 0, counts[t], 0).astype(F32)
        cat[:, t * EDGE : (t + 1) * EDGE] = tile.astype(BF)


def prepare_kernel(blocks, order, counts, one, two, three, four, five, send, *scratch):
    held, self_one, neighbor_one, neighbor_two, self_two, bias, second, done, ready = scratch
    steps = done.shape[0]
    per = held.shape[0] // steps
    copies = [
        pltpu.make_async_copy(
            counts.at[pl.ds(i * per, per)], held.at[pl.ds(i * per, per)], done.at[i]
        )
        for i in range(steps)
    ]
    pairs = zip((one, two, three, four, five), scratch[1:6])
    weights = [pltpu.make_async_copy(a, b, ready.at[i]) for i, (a, b) in enumerate(pairs)]
    for copy in copies + weights:
        copy.start()
    running = jnp.zeros((EDGE, EDGE), jnp.int32)
    for i, copy in enumerate(copies):
        copy.wait()
        for t in range(i * per, (i + 1) * per):
            running = running + jnp.where(blocks[t] >= 0, held[t], 0)
    for copy in weights:
        copy.wait()
    whole = dot(jnp.ones((8, EDGE), BF), running.astype(F32).astype(BF), NT)[0:1]
    high = jnp.floor(whole * (1.0 / 256.0))
    low = whole - high * 256.0
    row = lax.broadcasted_iota(jnp.int32, (16, EDGE), 0)
    both = jnp.where(row == 0, high, jnp.where(row == 1, low, 0.0)).astype(BF)
    second[...] = jnp.zeros_like(second)
    second[0:CLASSES, 0:64] = neighbor_two[...].astype(F32)
    second[CLASSES:WIDE, 0:64] = bias[...].astype(F32)
    second[0:CLASSES, 64:128] = self_two[...].astype(F32)
    layer_two = second[...].astype(BF)
    for r in range(send.shape[0]):
        send[r, 0:64] = self_one[...]
        send[r, 64:128] = neighbor_one[...]
        send[r, 128:176] = layer_two
        send[r, 176:192] = both


def spread_kernel(blocks, core, cat, got, cot, mask, mine, other, up_out, inv_out, far):
    degree = jnp.zeros((1, EDGE), F32)
    for r in range(got.shape[0]):
        both = got[r, 176:192].astype(F32)
        degree = degree + both[0:1] * 256.0 + both[1:2]
    inverse = 1.0 / (degree + 1.0)
    inv_out[...] = jnp.broadcast_to(inverse, inv_out.shape)
    upstream = cot[...].astype(F32) * mask[...].astype(F32)
    up_out[...] = upstream.astype(BF)
    scaled = (upstream * inverse).astype(BF)
    mine[...] = jnp.zeros_like(mine)
    far[...] = jnp.zeros_like(far)
    me = core[0]
    for t in range(cat.shape[1] // EDGE):
        block = jnp.maximum(blocks[t], 0)
        product = dot(scaled, cat[:, t * EDGE : (t + 1) * EDGE])
        own = (block & 1) == me
        at = block >> 1
        mine[at] += jnp.where(own, product, 0.0)
        far[at] += jnp.where(own, 0.0, product)
    other[...] = far[...].astype(BF)


def pair_sum_kernel(mine, other, total):
    total[...] = (mine[...] + other[...].astype(F32)).astype(BF)


def plane_sum_kernel(side, got, keep, give):
    total = got[0].astype(F32)
    for j in range(1, got.shape[0]):
        total = total + got[j].astype(F32)
    first = side[0] == 0
    keep[...] = jnp.where(first, total[0:WIDE], total[WIDE:])
    give[...] = jnp.where(first, total[WIDE:], total[0:WIDE])


def gather_one_kernel(blocks, core, own, far, cat, keep, came, send, picked):
    me = core[0]
    n_repl, part = send.shape[0], own.shape[2]
    for t in range(cat.shape[1] // EDGE):
        block = jnp.maximum(blocks[t], 0)
        half = (block >> 1) & 1
        at = block >> 2
        near = (block & 1) == me
        for q in range(n_repl):
            a = own[half * n_repl + q, at]
            b = far[half * n_repl + q, at]
            picked[q * part : (q + 1) * part, t * EDGE : (t + 1) * EDGE] = jnp.where(near, a, b)
    total = dot(picked[...], cat[...], NT)
    terms = keep[...] + came[...]
    for r in range(n_repl):
        send[r, 0:EDGE] = total
        send[r, EDGE:] = terms


def layer_kernel(repl, parts, got, up, inv, features, bias_two, send, base, packed, pad):
    chunk = GRADS // send.shape[0]
    n_repl = got.shape[0]
    both = parts[0]
    for r in range(1, n_repl):
        both = both + parts[r]
    mean = (both[0:EDGE] * inv[0:1]).astype(BF)
    feat = features[...]
    last = lax.broadcasted_iota(jnp.int32, (WIDE, EDGE), 0) == CLASSES
    unit = jnp.where(last, 1.0, 0.0).astype(BF)
    none = jnp.zeros((64, EDGE), BF)

    def before(r):
        bias = dot(got[r, 128:176], unit, TN)[0:64]
        return (dot(got[r, 0:64], feat) + dot(got[r, 64:128], mean)) + bias

    projected = jnp.zeros((WIDE, EDGE), F32)
    skipped = jnp.zeros((WIDE, EDGE), F32)
    for r in range(n_repl):
        pre = before(r)
        hidden = (pre * jax.nn.sigmoid(pre)).astype(BF)
        projected = projected + dot(got[r, 128:176], jnp.concatenate([hidden, none], axis=0))
        skipped = skipped + dot(got[r, 128:176], jnp.concatenate([none, hidden], axis=0))
    projected = projected.astype(BF)
    pad[...] = jnp.zeros_like(pad)
    pad[0:1, 0:CLASSES] = bias_two[...].astype(F32)
    base[...] = skipped + dot(pad[...].astype(BF), jnp.ones((8, EDGE), BF), TN)[0:WIDE]

    pulled = both[EDGE:].astype(BF)
    upstream = up[...]
    mine = repl[0]
    pre = before(mine)
    sigmoid = jax.nn.sigmoid(pre)
    hidden = (pre * sigmoid).astype(BF)
    second = got[mine, 128:176]
    hidden_grad = dot(second, upstream, TN)[64:128] + dot(second, pulled, TN)[0:64]
    pre_grad = (hidden_grad * sigmoid * (1.0 + pre * (1.0 - sigmoid))).astype(BF)
    packed[0:64] = dot(pre_grad, feat, NT)
    packed[64:128] = dot(pre_grad, mean, NT)
    ones = jnp.ones((8, EDGE), BF)
    twice = jnp.concatenate([hidden, hidden], axis=0)
    left = lax.broadcasted_iota(jnp.int32, (WIDE, EDGE), 1) < 64
    grads_two = jnp.where(left, dot(pulled, twice, NT), dot(upstream, twice, NT))
    bias_one = dot(ones, jnp.concatenate([pre_grad, none], axis=0), NT)[0:1]
    packed[128:176] = jnp.where(last, bias_one, grads_two)
    packed[176:184] = dot(ones, jnp.concatenate([upstream, jnp.zeros((EDGE - WIDE, EDGE), BF)], axis=0), NT)
    packed[184:GRADS] = jnp.zeros((GRADS - 184, EDGE), F32)
    for j in range(send.shape[0]):
        send[j, 0:WIDE] = projected
        send[j, WIDE:] = halves(packed[j * chunk : (j + 1) * chunk])


def relay_kernel(got, send):
    sheet = got.shape[0]
    chunk = GRADS // sheet
    total = got[0, WIDE:].astype(F32)
    for j in range(1, sheet):
        total = total + got[j, WIDE:].astype(F32)
    both = halves(total[0:chunk] + total[chunk:])
    for d in range(send.shape[0]):
        for j in range(sheet):
            send[d, j * WIDE : (j + 1) * WIDE] = got[j, 0:WIDE]
        send[d, sheet * WIDE :] = both


def gather_two_kernel(blocks, core, own, far, cat, send, grads, picked):
    me = core[0]
    sheet, chunk = grads.shape[0], grads.shape[1]
    for t in range(cat.shape[1] // EDGE):
        block = jnp.maximum(blocks[t], 0)
        place = block >> 1
        line = place // sheet
        rows = pl.ds(pl.multiple_of((place - line * sheet) * WIDE, 16), WIDE)
        near = (block & 1) == me
        a = own[line, rows]
        b = far[line, rows]
        picked[:, t * EDGE : (t + 1) * EDGE] = jnp.where(near, a, b)
    send[...] = dot(picked[...], cat[...], NT)
    sums = []
    for ref in (own, far):
        both = jnp.zeros((2 * chunk, EDGE), F32)
        for i in range(own.shape[0]):
            both = both + ref[i, sheet * WIDE :].astype(F32)
        sums.append(both[0:chunk] + both[chunk:])
    whole = sums[0] + sums[1]
    for j in range(sheet):
        grads[j] = whole


def scores_kernel(repl, own, first, second, third, base, inv, scores, parts):
    n_repl = parts.shape[0]
    for k, ref in enumerate((own, first, second, third)[:n_repl]):
        at = repl[0] + k
        parts[jnp.where(at >= n_repl, at - n_repl, at)] = ref[...]
    total = parts[0]
    for r in range(1, n_repl):
        total = total + parts[r]
    scores[...] = (base[...] + total * inv[0:1])[0:CLASSES]


def unpack_kernel(grads, self_one, neighbor_one, bias_one, self_two, neighbor_two, bias_two):
    self_one[...] = grads[0:64]
    neighbor_one[...] = grads[64:128]
    neighbor_two[...] = grads[128 : 128 + CLASSES, 0:64]
    self_two[...] = grads[128 : 128 + CLASSES, 64:128]
    bias_one[...] = grads[175:176, 0:64]
    bias_two[...] = grads[176:177, 0:CLASSES]


def per_device(
    sizes,
    features,
    tile_blocks,
    tile_counts,
    train_mask,
    cotangent,
    self_one,
    neighbor_one,
    bias_one,
    self_two,
    neighbor_two,
    bias_two,
):
    n_repl = sizes["yl"]
    plane = sizes["x"] * sizes["z"]
    halves_n = sizes["yh"]
    column = halves_n * n_repl
    tiles = tile_counts.shape[0]
    sheet = sizes["z"] * halves_n
    chunk = GRADS // sheet
    core = lax.axis_index("core").astype(jnp.int32).reshape(1)
    repl = lax.axis_index("yl").astype(jnp.int32).reshape(1)
    side = lax.axis_index("yh").astype(jnp.int32).reshape(1)
    swap = [(0, 1), (1, 0)]

    part = features.shape[0] // n_repl
    quarter = lax.dynamic_slice_in_dim(features, repl[0] * part, part, 0)
    quarters = lax.all_to_all(
        jnp.broadcast_to(quarter[None], (plane, part, EDGE)), PLANE, 0, 0, tiled=True
    )
    order, quarters = lax.optimization_barrier((core, quarters))
    near = lax.all_gather(quarters.reshape(plane * part, EDGE), COLUMN, axis=0, tiled=True)

    send = call(
        prepare_kernel,
        jax.ShapeDtypeStruct((n_repl, 192, EDGE), BF),
        [SMEM] * 2 + [pl.BlockSpec(memory_space=pl.ANY)] * 6,
        [
            pltpu.VMEM((tiles, EDGE, EDGE), jnp.int32),
            pltpu.VMEM((64, EDGE), BF),
            pltpu.VMEM((64, EDGE), BF),
            pltpu.VMEM((CLASSES, 64), BF),
            pltpu.VMEM((CLASSES, 64), BF),
            pltpu.VMEM((1, 64), BF),
            pltpu.VMEM((WIDE, EDGE), F32),
            pltpu.SemaphoreType.DMA((8,)),
            pltpu.SemaphoreType.DMA((5,)),
        ],
        60,
    )(
        tile_blocks,
        order,
        tile_counts,
        self_one.T,
        neighbor_one.T,
        neighbor_two.T,
        self_two.T,
        bias_one[None, :],
    )
    got = lax.all_to_all(send, "yl", 0, 0, tiled=True)
    cat = call(lay_kernel, jax.ShapeDtypeStruct((EDGE, tiles * EDGE), BF), [SMEM, VMEM])(
        tile_blocks, tile_counts
    )

    cot = jnp.pad(cotangent, ((0, WIDE - CLASSES), (0, 0)))
    mine, other, up, inv = call(
        spread_kernel,
        (
            jax.ShapeDtypeStruct((plane * halves_n, WIDE, EDGE), F32),
            jax.ShapeDtypeStruct((plane * halves_n, WIDE, EDGE), BF),
            jax.ShapeDtypeStruct((WIDE, EDGE), BF),
            jax.ShapeDtypeStruct((8, EDGE), F32),
        ),
        [SMEM, SMEM] + [VMEM] * 4,
        [pltpu.VMEM((plane * halves_n, WIDE, EDGE), F32)],
    )(tile_blocks, core, cat, got, cot, train_mask[None, :])
    back = call(
        pair_sum_kernel,
        jax.ShapeDtypeStruct((plane * halves_n, WIDE, EDGE), BF),
        [VMEM] * 2,
    )(mine, lax.ppermute(other, "core", swap))
    back = lax.all_to_all(back.reshape(plane, halves_n * WIDE, EDGE), PLANE, 0, 0, tiled=True)
    near, back = lax.optimization_barrier((near, back))
    far = lax.ppermute(near, "core", swap)
    half = jax.ShapeDtypeStruct((WIDE, EDGE), F32)
    keep, give = call(plane_sum_kernel, (half, half), [SMEM, VMEM])(side, back)
    came = lax.ppermute(give, "yh", swap)

    shape = (column, plane, part, EDGE)
    parts = call(
        gather_one_kernel,
        jax.ShapeDtypeStruct((n_repl, EDGE + WIDE, EDGE), F32),
        [SMEM, SMEM] + [VMEM] * 5,
        [pltpu.VMEM((EDGE, tiles * EDGE), BF)],
    )(tile_blocks, core, near.reshape(shape), far.reshape(shape), cat, keep, came)
    parts = lax.all_to_all(parts, "yl", 0, 0, tiled=True)

    send, base = call(
        layer_kernel,
        (
            jax.ShapeDtypeStruct((sheet, WIDE + 2 * chunk, EDGE), BF),
            jax.ShapeDtypeStruct((WIDE, EDGE), F32),
        ),
        [SMEM] + [VMEM] * 6,
        [pltpu.VMEM((GRADS, EDGE), F32), pltpu.VMEM((8, EDGE), F32)],
    )(repl, parts, got, up, inv, features, bias_two[None, :])
    relay = lax.all_to_all(send, SHEET, 0, 0, tiled=True)
    relay = call(
        relay_kernel,
        jax.ShapeDtypeStruct((sizes["x"], sheet * WIDE + 2 * chunk, EDGE), BF),
        [VMEM],
    )(relay)
    near_two = lax.all_to_all(relay, "x", 0, 0, tiled=True)
    far_two = lax.ppermute(near_two, "core", swap)
    second, grads = call(
        gather_two_kernel,
        (
            jax.ShapeDtypeStruct((WIDE, EDGE), F32),
            jax.ShapeDtypeStruct((sheet, chunk, EDGE), F32),
        ),
        [SMEM] * 2 + [VMEM] * 3,
        [pltpu.VMEM((WIDE, tiles * EDGE), BF)],
    )(tile_blocks, core, near_two, far_two, cat)
    others = [
        lax.ppermute(second, "yl", [((i + k) % n_repl, i) for i in range(n_repl)])
        for k in range(1, n_repl)
    ]
    grads = lax.all_to_all(grads, SHEET, 0, 0, tiled=True).reshape(GRADS, EDGE)
    others = others + [second] * (3 - len(others))
    scores = call(
        scores_kernel,
        jax.ShapeDtypeStruct((CLASSES, EDGE), F32),
        [SMEM] + [VMEM] * 6,
        [pltpu.VMEM((n_repl, WIDE, EDGE), F32)],
    )(repl, second, *others, base, inv)
    one = jax.ShapeDtypeStruct((64, EDGE), F32)
    two = jax.ShapeDtypeStruct((CLASSES, 64), F32)
    self_one, neighbor_one, bias_one, self_two, neighbor_two, bias_two = call(
        unpack_kernel,
        (
            one,
            one,
            jax.ShapeDtypeStruct((1, 64), F32),
            two,
            two,
            jax.ShapeDtypeStruct((1, CLASSES), F32),
        ),
        [VMEM],
    )(grads)
    return (
        scores,
        self_one.T,
        neighbor_one.T,
        bias_one[0],
        self_two.T,
        neighbor_two.T,
        bias_two[0],
    )


def solution(mesh):
    sizes = {"x": 4, "z": 8, "yh": 2, "core": 2, "yl": 4}
    fine = Mesh(mesh.devices.reshape(tuple(sizes.values())), tuple(sizes))
    return sharded(fine, sizes)


def sharded(fine, sizes):
    both = ROWS + ("yl",)
    return jax.shard_map(
        functools.partial(per_device, sizes),
        mesh=fine,
        in_specs=(
            P(None, ROWS),
            P(both),
            P(both, None, None),
            P(ROWS),
            P(None, ROWS),
            P(None, "yl"),
            P(None, "yl"),
            P("yl"),
            P("yl", None),
            P("yl", None),
            P(),
        ),
        out_specs=(
            P(None, ROWS),
            P(None, "yl"),
            P(None, "yl"),
            P("yl"),
            P("yl", None),
            P("yl", None),
            P(),
        ),
        check_vma=False,
    )
```

time: 196 us -> 185 us (0.944)
  the two profiles are of different devices: /device:TPU:2 before, /device:TPU:48 now
where the time goes in v3:
time: 185 us; the launch traced here: 184 us
  blocking collectives  74.9 us (40%)
  starting transfers between devices  46.8 us (25%)
  waiting for transfers between devices  32.5 us (18%)
  between operations  14.2 us (8%)
  Pallas kernels  11.7 us (6%)
  local copies, waits for them, and re-layouts  3.93 us (2%)
    all_to_all x1, blocking collectives, per_device(): lax.all_to_all(back.reshape(plane, halves_n * WIDE, EDGE), PLANE, 0, 0, t...  26.8 us
    all_to_all x1, blocking collectives, per_device(): relay = lax.all_to_all(send, SHEET, 0, 0, tiled=True)  20.3 us
    all_to_all x1, blocking collectives, per_device(): near_two = lax.all_to_all(relay, 'x', 0, 0, tiled=True)  14.5 us
    all_to_all x1, blocking collectives, per_device(): parts = lax.all_to_all(parts, 'yl', 0, 0, tiled=True)  13.4 us
    all_to_all x1, starting transfers between devices, per_device(): lax.all_to_all(jnp.broadcast_to(quarter[None], (plane, part, EDGE)), PLAN...  13.2 us
    all_to_all x1, waiting for transfers between devices, per_device(): lax.all_to_all(jnp.broadcast_to(quarter[None], (plane, part, EDGE)), PLAN...  12.4 us
    ppermute x3, starting transfers between devices, per_device(): lax.ppermute(second, 'yl', [((i + k) % n_repl, i) for i in range(n_repl)])  10.1 us
    all_to_all x1, starting transfers between devices, per_device(): grads = lax.all_to_all(grads, SHEET, 0, 0, tiled=True).reshape(GRADS, EDGE)  9.37 us
  transfers between devices with their start and end apart: 11, of which 6 were waited for; matrix products, arithmetic and copies ran while one was open for 0% of the time, Pallas kernels for 3%

profile of v3, /device:TPU:48, one launch (start us, length us, event | category | flops | bytes accessed | tf_op | source)
XLA Modules:
  0.0 184.2 jit_solution(1262392769926113209)
XLA Ops:
  8.8 13.2 %all-to-all-start = ((bf16[32,32,128]{2,1,0:T(8,128)(2,1)}), bf16[32,32,128]{2,1,0:T(8,128)(2,1)S(1)}, u32[]{:S(2)}, u32[]{:S(2)}) async-start(bf16[32,32,128]{2,1,0:T(8,128)(2,1)} %broadcast_in_dim.15), calls=%async_computation | async-start | bytes 524288 | tf_op jit(solution)/shard_map/all_to_all | solution.py:282
  22.0 12.4 %all-to-all-done = bf16[32,32,128]{2,1,0:T(8,128)(2,1)S(1)} async-done(((bf16[32,32,128]{2,1,0:T(8,128)(2,1)}), bf16[32,32,128]{2,1,0:T(8,128)(2,1)S(1)}, u32[]{:S(2)}, u32[]{:S(2)}) %all-to-all-start) | async-done | bytes 262176 | tf_op jit(solution)/shard_map/all_to_all | solution.py:282
  35.2 3.2 %shard_map.163 = bf16[4,192,128]{2,1,0:T(8,128)(2,1)} custom-call(s32[32]{0:T(128)} %blocks.9, s32[1]{0:T(128)} %bitcast.1.order.core, s32[32,128,128]{2,1,0:T(8,128)} %counts.3, bf16[64,128]{1,0:T(8,128)(2,1)} %bitcast.27, bf16[64,128]{1,0:T(8,128)(2,1)} %bitcast.28, bf16[47,64]{1,0:T(8,128)(2,1)} %bitcast.29, bf16[47,64]{1,0:T(8,128)(2,1)} %bitcast.30, ...), custom_call_target="tpu_custom_call" | custom-call | tf_op jit(solution)/shard_map/pallas_call | solution.py:288
  38.4 5.5 %all-to-all-start.1 = ((bf16[4,192,128]{2,1,0:T(8,128)(2,1)}), bf16[4,192,128]{2,1,0:T(8,128)(2,1)S(1)}, u32[]{:S(2)}, u32[]{:S(2)}) async-start(bf16[4,192,128]{2,1,0:T(8,128)(2,1)} %shard_map.163), calls=%async_computation.1 | async-start | bytes 393216 | tf_op jit(solution)/shard_map/all_to_all | solution.py:314
  44.7 5.1 %all-to-all-done.1.got = bf16[4,192,128]{2,1,0:T(8,128)(2,1)S(1)} async-done(((bf16[4,192,128]{2,1,0:T(8,128)(2,1)}), bf16[4,192,128]{2,1,0:T(8,128)(2,1)S(1)}, u32[]{:S(2)}, u32[]{:S(2)}) %all-to-all-start.1) | async-done | bytes 196640 | tf_op jit(solution)/shard_map/all_to_all | solution.py:314
  51.1 1.9 %collective-permute-start = (bf16[64,48,128]{2,1,0:T(8,128)(2,1)S(1)}, bf16[64,48,128]{2,1,0:T(8,128)(2,1)S(1)}, u32[]{:S(2)}, u32[]{:S(2)}) collective-permute-start(bf16[64,48,128]{2,1,0:T(8,128)(2,1)S(1)} %get-tuple-element.30), channel_id=1, source_target_pairs={{0,4},{4,0},{1,5},{5,1},{2,6},{6,2},{3,7},{7,3},{8,12},{12,8},{9,1... | collective-permute-start | bytes 2359304 | tf_op jit(solution)/shard_map/ppermute | solution.py:335
  53.0 2.3 %collective-permute-done.other = bf16[64,48,128]{2,1,0:T(8,128)(2,1)S(1)} collective-permute-done((bf16[64,48,128]{2,1,0:T(8,128)(2,1)S(1)}, bf16[64,48,128]{2,1,0:T(8,128)(2,1)S(1)}, u32[]{:S(2)}, u32[]{:S(2)}) %collective-permute-start) | collective-permute-done | bytes 786464 | tf_op jit(solution)/shard_map/ppermute | solution.py:335
  55.4 26.8 %all_to_all.35.got = bf16[32,96,128]{2,1,0:T(8,128)(2,1)S(1)} all-to-all(bf16[32,96,128]{2,1,0:T(8,128)(2,1)S(1)} %bitcast.21), channel_id=1, replica_groups=mesh['x'=4,'z'=8,'yh'=2,'core'=2,'yl'=4] {'x','z'}, dimensions={0} | all-to-all | bytes 1572864 | tf_op jit(solution)/shard_map/all_to_all | solution.py:336
  82.1 1.9 %collective-permute-start.1 = (bf16[8192,128]{1,0:T(8,128)(2,1)}, bf16[8192,128]{1,0:T(8,128)(2,1)}, u32[]{:S(2)}, u32[]{:S(2)}) collective-permute-start(bf16[8192,128]{1,0:T(8,128)(2,1)} %all-gather.2.cloned.1.call-done), channel_id=1, source_target_pairs={{0,4},{4,0},{1,5},{5,1},{2,6},{6,2},{3,7},{7,3},{8,12},{12,8},{9,1... | collective-permute-start | bytes 6291464 | tf_op jit(solution)/shard_map/ppermute | solution.py:338
  84.2 2.9 %collective-permute-start.2 = (f32[48,128]{1,0:T(8,128)S(1)}, f32[48,128]{1,0:T(8,128)S(1)}, u32[]{:S(2)}, u32[]{:S(2)}) collective-permute-start(f32[48,128]{1,0:T(8,128)S(1)} %get-tuple-element.34), channel_id=1, source_target_pairs={{0,8},{8,0},{1,9},{9,1},{2,10},{10,2},{3,11},{11,3},{4,12},{12,4},... | collective-permute-start | bytes 73736 | tf_op jit(solution)/shard_map/ppermute | solution.py:341
  87.1 6.7 %collective-permute-done.2.came = f32[48,128]{1,0:T(8,128)S(1)} collective-permute-done((f32[48,128]{1,0:T(8,128)S(1)}, f32[48,128]{1,0:T(8,128)S(1)}, u32[]{:S(2)}, u32[]{:S(2)}) %collective-permute-start.2) | collective-permute-done | bytes 24608 | tf_op jit(solution)/shard_map/ppermute | solution.py:341
  93.8 1.6 copy-done.1
  95.4 2.2 %shard_map.167 = f32[4,176,128]{2,1,0:T(8,128)S(1)} custom-call(s32[32]{0:T(128)S(1)} %copy-done.3, s32[1]{0:T(128)} %bitcast.1.order.core, bf16[8,32,32,128]{3,2,1,0:T(8,128)(2,1)S(1)} %bitcast.22, bf16[8,32,32,128]{3,2,1,0:T(8,128)(2,1)} %bitcast.11.far, bf16[128,4096]{1,0:T(8,128)(2,1)S(1)} %shard_map.162.cat, f32[48,128]{1,0:T(8,128)S(1)} %get-tuple-element.33.keep, ...), custom_call_target="tpu_custom_call" | custom-call | tf_op jit(solution)/shard_map/pallas_call | solution.py:344
  97.6 13.4 %all_to_all.36.parts = f32[4,176,128]{2,1,0:T(8,128)S(1)} all-to-all(f32[4,176,128]{2,1,0:T(8,128)S(1)} %shard_map.167), channel_id=1, replica_groups=mesh['x'=4,'z'=8,'yh'=2,'core'=2,'yl'=4] {'yl'}, dimensions={0} | all-to-all | bytes 720896 | tf_op jit(solution)/shard_map/all_to_all | solution.py:350
  112.0 20.3 %all_to_all.37.got = bf16[16,80,128]{2,1,0:T(8,128)(2,1)S(1)} all-to-all(bf16[16,80,128]{2,1,0:T(8,128)(2,1)S(1)} %get-tuple-element.37), channel_id=1, replica_groups=mesh['x'=4,'z'=8,'yh'=2,'core'=2,'yl'=4] {'z','yh'}, dimensions={0} | all-to-all | bytes 655360 | tf_op jit(solution)/shard_map/all_to_all | solution.py:361
  132.4 14.5 %all_to_all.38.own = bf16[4,800,128]{2,1,0:T(8,128)(2,1)S(1)} all-to-all(bf16[4,800,128]{2,1,0:T(8,128)(2,1)S(1)} %shard_map.169), channel_id=1, replica_groups=mesh['x'=4,'z'=8,'yh'=2,'core'=2,'yl'=4] {'x'}, dimensions={0} | all-to-all | bytes 1638400 | tf_op jit(solution)/shard_map/all_to_all | solution.py:367
  146.9 1.9 %collective-permute-start.3 = (bf16[4,800,128]{2,1,0:T(8,128)(2,1)S(1)}, bf16[4,800,128]{2,1,0:T(8,128)(2,1)S(1)}, u32[]{:S(2)}, u32[]{:S(2)}) collective-permute-start(bf16[4,800,128]{2,1,0:T(8,128)(2,1)S(1)} %all_to_all.38.own), channel_id=1, source_target_pairs={{0,4},{4,0},{1,5},{5,1},{2,6},{6,2},{3,7},{7,3},{8,12},{12,8},{9,1... | collective-permute-start | bytes 2457608 | tf_op jit(solution)/shard_map/ppermute | solution.py:368
  148.8 2.3 %collective-permute-done.3.far = bf16[4,800,128]{2,1,0:T(8,128)(2,1)S(1)} collective-permute-done((bf16[4,800,128]{2,1,0:T(8,128)(2,1)S(1)}, bf16[4,800,128]{2,1,0:T(8,128)(2,1)S(1)}, u32[]{:S(2)}, u32[]{:S(2)}) %collective-permute-start.3) | collective-permute-done | bytes 819232 | tf_op jit(solution)/shard_map/ppermute | solution.py:368
  151.1 1.6 shard_map.170
  152.7 9.4 %all-to-all-start.6 = ((f32[16,16,128]{2,1,0:T(8,128)}), f32[16,16,128]{2,1,0:T(8,128)S(1)}, u32[]{:S(2)}, u32[]{:S(2)}) async-start(f32[16,16,128]{2,1,0:T(8,128)} %get-tuple-element.40), calls=%async_computation.6 | async-start | bytes 262144 | tf_op jit(solution)/shard_map/all_to_all | solution.py:382
  162.1 1.9 %collective-permute-start.4 = (f32[48,128]{1,0:T(8,128)S(1)}, f32[48,128]{1,0:T(8,128)S(1)}, u32[]{:S(2)}, u32[]{:S(2)}) collective-permute-start(f32[48,128]{1,0:T(8,128)S(1)} %get-tuple-element.38.own), channel_id=1, source_target_pairs={{1,0},{2,1},{3,2},{0,3},{5,4},{6,5},{7,6},{4,7},{9,8},{10,9},{11,1... | collective-permute-start | bytes 73736 | tf_op jit(solution)/shard_map/ppermute | solution.py:379
  164.0 6.2 %collective-permute-start.5 = (f32[48,128]{1,0:T(8,128)S(1)}, f32[48,128]{1,0:T(8,128)S(1)}, u32[]{:S(2)}, u32[]{:S(2)}) collective-permute-start(f32[48,128]{1,0:T(8,128)S(1)} %get-tuple-element.38.own), channel_id=1, source_target_pairs={{2,0},{3,1},{0,2},{1,3},{6,4},{7,5},{4,6},{5,7},{10,8},{11,9},{8,1... | collective-permute-start | bytes 73736 | tf_op jit(solution)/shard_map/ppermute | solution.py:379
  170.3 1.9 %collective-permute-start.6 = (f32[48,128]{1,0:T(8,128)S(1)}, f32[48,128]{1,0:T(8,128)S(1)}, u32[]{:S(2)}, u32[]{:S(2)}) collective-permute-start(f32[48,128]{1,0:T(8,128)S(1)} %get-tuple-element.38.own), channel_id=1, source_target_pairs={{3,0},{0,1},{1,2},{2,3},{7,4},{4,5},{5,6},{6,7},{11,8},{8,9},{9,10... | collective-permute-start | bytes 73736 | tf_op jit(solution)/shard_map/ppermute | solution.py:379
  172.2 3.8 %collective-permute-done.6.third = f32[48,128]{1,0:T(8,128)S(1)} collective-permute-done((f32[48,128]{1,0:T(8,128)S(1)}, f32[48,128]{1,0:T(8,128)S(1)}, u32[]{:S(2)}, u32[]{:S(2)}) %collective-permute-start.6) | collective-permute-done | bytes 24608 | tf_op jit(solution)/shard_map/ppermute | solution.py:379
  (33 shorter events, 7.2 us)
Async XLA Ops:
  7.2 36.7 %copy-start.3 = (s32[32]{0:T(128)S(1)}, s32[32]{0:T(128)}, u32[]{:S(2)}) copy-start(s32[32]{0:T(128)} %blocks.9) | copy-start | bytes 388
  7.2 36.7 %copy-start = (s32[32,128,128]{2,1,0:T(8,128)S(1)}, s32[32,128,128]{2,1,0:T(8,128)}, u32[]{:S(2)}) copy-start(s32[32,128,128]{2,1,0:T(8,128)} %counts.3) | copy-start | bytes 6291460
  8.8 25.6 %all-to-all-start = ((bf16[32,32,128]{2,1,0:T(8,128)(2,1)}), bf16[32,32,128]{2,1,0:T(8,128)(2,1)S(1)}, u32[]{:S(2)}, u32[]{:S(2)}) async-start(bf16[32,32,128]{2,1,0:T(8,128)(2,1)} %broadcast_in_dim.15), calls=%async_computation | async-start | bytes 524288 | tf_op jit(solution)/shard_map/all_to_all | solution.py:282
  22.0 60.2 %all-gather.2.cloned.1.call-start = ((), (), s32[]{:S(2)}) async-start(), calls=%async_computation.7 | async-start | bytes 2359296 | tf_op jit(solution)/shard_map/all_gather | solution.py:286
  34.4 0.7 copy-start.6
  38.3 6.3 %copy-start.7 = (bf16[47,128]{1,0:T(8,128)(2,1)S(1)}, bf16[47,128]{1,0:T(8,128)(2,1)}, u32[]{:S(2)}) copy-start(bf16[47,128]{1,0:T(8,128)(2,1)} %param.15) | copy-start | bytes 36100
  38.4 11.4 %copy-start.4 = (s32[128]{0:T(128)S(1)}, s32[128]{0:T(128)}, u32[]{:S(2)}) copy-start(s32[128]{0:T(128)} %param.14) | copy-start | bytes 1540
  38.4 11.4 %all-to-all-start.1 = ((bf16[4,192,128]{2,1,0:T(8,128)(2,1)}), bf16[4,192,128]{2,1,0:T(8,128)(2,1)S(1)}, u32[]{:S(2)}, u32[]{:S(2)}) async-start(bf16[4,192,128]{2,1,0:T(8,128)(2,1)} %shard_map.163), calls=%async_computation.1 | async-start | bytes 393216 | tf_op jit(solution)/shard_map/all_to_all | solution.py:314
  51.1 4.2 %collective-permute-start = (bf16[64,48,128]{2,1,0:T(8,128)(2,1)S(1)}, bf16[64,48,128]{2,1,0:T(8,128)(2,1)S(1)}, u32[]{:S(2)}, u32[]{:S(2)}) collective-permute-start(bf16[64,48,128]{2,1,0:T(8,128)(2,1)S(1)} %get-tuple-element.30), channel_id=1, source_target_pairs={{0,4},{4,0},{1,5},{5,1},{2,6},{6,2},{3,7},{7,3},{8,12},{12,8},{9,1... | collective-permute-start | bytes 2359304 | tf_op jit(solution)/shard_map/ppermute | solution.py:335
  82.1 11.7 %collective-permute-start.1 = (bf16[8192,128]{1,0:T(8,128)(2,1)}, bf16[8192,128]{1,0:T(8,128)(2,1)}, u32[]{:S(2)}, u32[]{:S(2)}) collective-permute-start(bf16[8192,128]{1,0:T(8,128)(2,1)} %all-gather.2.cloned.1.call-done), channel_id=1, source_target_pairs={{0,4},{4,0},{1,5},{5,1},{2,6},{6,2},{3,7},{7,3},{8,12},{12,8},{9,1... | collective-permute-start | bytes 6291464 | tf_op jit(solution)/shard_map/ppermute | solution.py:338
  84.2 9.6 %collective-permute-start.2 = (f32[48,128]{1,0:T(8,128)S(1)}, f32[48,128]{1,0:T(8,128)S(1)}, u32[]{:S(2)}, u32[]{:S(2)}) collective-permute-start(f32[48,128]{1,0:T(8,128)S(1)} %get-tuple-element.34), channel_id=1, source_target_pairs={{0,8},{8,0},{1,9},{9,1},{2,10},{10,2},{3,11},{11,3},{4,12},{12,4},... | collective-permute-start | bytes 73736 | tf_op jit(solution)/shard_map/ppermute | solution.py:341
  93.8 1.6 copy-start.1
  95.4 15.6 %copy-start.2 = (bf16[128,128]{1,0:T(8,128)(2,1)S(1)}, bf16[128,128]{1,0:T(8,128)(2,1)}, u32[]{:S(2)}) copy-start(bf16[128,128]{1,0:T(8,128)(2,1)} %features.1) | copy-start | bytes 98308
  95.4 15.6 %copy-start.5 = (bf16[47]{0:T(256)(128)(2,1)S(1)}, bf16[47]{0:T(256)(128)(2,1)}, u32[]{:S(2)}) copy-start(bf16[47]{0:T(256)(128)(2,1)} %param.21) | copy-start | bytes 286
  146.9 4.2 %collective-permute-start.3 = (bf16[4,800,128]{2,1,0:T(8,128)(2,1)S(1)}, bf16[4,800,128]{2,1,0:T(8,128)(2,1)S(1)}, u32[]{:S(2)}, u32[]{:S(2)}) collective-permute-start(bf16[4,800,128]{2,1,0:T(8,128)(2,1)S(1)} %all_to_all.38.own), channel_id=1, source_target_pairs={{0,4},{4,0},{1,5},{5,1},{2,6},{6,2},{3,7},{7,3},{8,12},{12,8},{9,1... | collective-permute-start | bytes 2457608 | tf_op jit(solution)/shard_map/ppermute | solution.py:368
  152.7 23.9 %all-to-all-start.6 = ((f32[16,16,128]{2,1,0:T(8,128)}), f32[16,16,128]{2,1,0:T(8,128)S(1)}, u32[]{:S(2)}, u32[]{:S(2)}) async-start(f32[16,16,128]{2,1,0:T(8,128)} %get-tuple-element.40), calls=%async_computation.6 | async-start | bytes 262144 | tf_op jit(solution)/shard_map/all_to_all | solution.py:382
  162.1 10.1 %collective-permute-start.4 = (f32[48,128]{1,0:T(8,128)S(1)}, f32[48,128]{1,0:T(8,128)S(1)}, u32[]{:S(2)}, u32[]{:S(2)}) collective-permute-start(f32[48,128]{1,0:T(8,128)S(1)} %get-tuple-element.38.own), channel_id=1, source_target_pairs={{1,0},{2,1},{3,2},{0,3},{5,4},{6,5},{7,6},{4,7},{9,8},{10,9},{11,1... | collective-permute-start | bytes 73736 | tf_op jit(solution)/shard_map/ppermute | solution.py:379
  164.0 8.2 %collective-permute-start.5 = (f32[48,128]{1,0:T(8,128)S(1)}, f32[48,128]{1,0:T(8,128)S(1)}, u32[]{:S(2)}, u32[]{:S(2)}) collective-permute-start(f32[48,128]{1,0:T(8,128)S(1)} %get-tuple-element.38.own), channel_id=1, source_target_pairs={{2,0},{3,1},{0,2},{1,3},{6,4},{7,5},{4,6},{5,7},{10,8},{11,9},{8,1... | collective-permute-start | bytes 73736 | tf_op jit(solution)/shard_map/ppermute | solution.py:379
  170.3 5.7 %collective-permute-start.6 = (f32[48,128]{1,0:T(8,128)S(1)}, f32[48,128]{1,0:T(8,128)S(1)}, u32[]{:S(2)}, u32[]{:S(2)}) collective-permute-start(f32[48,128]{1,0:T(8,128)S(1)} %get-tuple-element.38.own), channel_id=1, source_target_pairs={{3,0},{0,1},{1,2},{2,3},{7,4},{4,5},{5,6},{6,7},{11,8},{8,9},{9,10... | collective-permute-start | bytes 73736 | tf_op jit(solution)/shard_map/ppermute | solution.py:379
Sparse Core Ops, SparseCore 0:
  35.3 39.0 all-gather.1

commit v4 on v3

--- a/solution.py
+++ b/solution.py
@@ -43,13 +43,20 @@
     return jnp.concatenate([high, value - high], axis=0).astype(BF)
 
 
+def quarter_kernel(repl, features, send):
+    rows = send.shape[1]
+    part = features[pl.ds(pl.multiple_of(repl[0] * rows, 16), rows)]
+    for j in range(send.shape[0]):
+        send[j] = part
+
+
 def lay_kernel(blocks, counts, cat):
     for t in range(counts.shape[0]):
         tile = jnp.where(blocks[t] >= 0, counts[t], 0).astype(F32)
         cat[:, t * EDGE : (t + 1) * EDGE] = tile.astype(BF)
 
 
-def prepare_kernel(blocks, order, counts, one, two, three, four, five, send, *scratch):
+def prepare_kernel(blocks, counts, one, two, three, four, five, send, *scratch):
     held, self_one, neighbor_one, neighbor_two, self_two, bias, second, done, ready = scratch
     steps = done.shape[0]
     per = held.shape[0] // steps
@@ -123,9 +130,10 @@
     give[...] = jnp.where(first, total[WIDE:], total[0:WIDE])
 
 
-def gather_one_kernel(blocks, core, own, far, cat, keep, came, send, picked):
+def gather_one_kernel(blocks, core, own, far, cat, total, picked):
     me = core[0]
-    n_repl, part = send.shape[0], own.shape[2]
+    part = own.shape[2]
+    n_repl = EDGE // part
     for t in range(cat.shape[1] // EDGE):
         block = jnp.maximum(blocks[t], 0)
         half = (block >> 1) & 1
@@ -135,20 +143,24 @@
             a = own[half * n_repl + q, at]
             b = far[half * n_repl + q, at]
             picked[q * part : (q + 1) * part, t * EDGE : (t + 1) * EDGE] = jnp.where(near, a, b)
-    total = dot(picked[...], cat[...], NT)
-    terms = keep[...] + came[...]
-    for r in range(n_repl):
-        send[r, 0:EDGE] = total
-        send[r, EDGE:] = terms
+    total[...] = dot(picked[...], cat[...], NT)
+
+
+def mix_kernel(total, keep, came, send):
+    part = halves(total[...])
+    terms = (keep[...] + came[...]).astype(BF)
+    for r in range(send.shape[0]):
+        send[r, 0 : 2 * EDGE] = part
+        send[r, 2 * EDGE :] = terms
 
 
 def layer_kernel(repl, parts, got, up, inv, features, bias_two, send, base, packed, pad):
     chunk = GRADS // send.shape[0]
     n_repl = got.shape[0]
-    both = parts[0]
+    both = parts[0].astype(F32)
     for r in range(1, n_repl):
-        both = both + parts[r]
-    mean = (both[0:EDGE] * inv[0:1]).astype(BF)
+        both = both + parts[r].astype(F32)
+    mean = ((both[0:EDGE] + both[EDGE : 2 * EDGE]) * inv[0:1]).astype(BF)
     feat = features[...]
     last = lax.broadcasted_iota(jnp.int32, (WIDE, EDGE), 0) == CLASSES
     unit = jnp.where(last, 1.0, 0.0).astype(BF)
@@ -170,7 +182,7 @@
     pad[0:1, 0:CLASSES] = bias_two[...].astype(F32)
     base[...] = skipped + dot(pad[...].astype(BF), jnp.ones((8, EDGE), BF), TN)[0:WIDE]
 
-    pulled = both[EDGE:].astype(BF)
+    pulled = both[2 * EDGE :].astype(BF)
     upstream = up[...]
     mine = repl[0]
     pre = before(mine)
@@ -207,9 +219,8 @@
         send[d, sheet * WIDE :] = both
 
 
-def gather_two_kernel(blocks, core, own, far, cat, send, grads, picked):
+def gather_two_kernel(sheet, blocks, core, own, far, cat, send, picked):
     me = core[0]
-    sheet, chunk = grads.shape[0], grads.shape[1]
     for t in range(cat.shape[1] // EDGE):
         block = jnp.maximum(blocks[t], 0)
         place = block >> 1
@@ -220,15 +231,16 @@
         b = far[line, rows]
         picked[:, t * EDGE : (t + 1) * EDGE] = jnp.where(near, a, b)
     send[...] = dot(picked[...], cat[...], NT)
-    sums = []
-    for ref in (own, far):
-        both = jnp.zeros((2 * chunk, EDGE), F32)
-        for i in range(own.shape[0]):
-            both = both + ref[i, sheet * WIDE :].astype(F32)
-        sums.append(both[0:chunk] + both[chunk:])
-    whole = sums[0] + sums[1]
-    for j in range(sheet):
-        grads[j] = whole
+
+
+def chunk_sum_kernel(got, grads):
+    chunk = grads.shape[1]
+    both = got[0].astype(F32)
+    for i in range(1, got.shape[0]):
+        both = both + got[i].astype(F32)
+    total = both[0:chunk] + both[chunk:]
+    for j in range(grads.shape[0]):
+        grads[j] = total
 
 
 def scores_kernel(repl, own, first, second, third, base, inv, scores, parts):
@@ -242,7 +254,12 @@
     scores[...] = (base[...] + total * inv[0:1])[0:CLASSES]
 
 
-def unpack_kernel(grads, self_one, neighbor_one, bias_one, self_two, neighbor_two, bias_two):
+def unpack_kernel(
+    got, self_one, neighbor_one, bias_one, self_two, neighbor_two, bias_two, grads
+):
+    chunk = got.shape[1]
+    for j in range(got.shape[0] // 2):
+        grads[j * chunk : (j + 1) * chunk] = got[2 * j] + got[2 * j + 1]
     self_one[...] = grads[0:64]
     neighbor_one[...] = grads[64:128]
     neighbor_two[...] = grads[128 : 128 + CLASSES, 0:64]
@@ -278,17 +295,15 @@
     swap = [(0, 1), (1, 0)]
 
     part = features.shape[0] // n_repl
-    quarter = lax.dynamic_slice_in_dim(features, repl[0] * part, part, 0)
-    quarters = lax.all_to_all(
-        jnp.broadcast_to(quarter[None], (plane, part, EDGE)), PLANE, 0, 0, tiled=True
-    )
-    order, quarters = lax.optimization_barrier((core, quarters))
-    near = lax.all_gather(quarters.reshape(plane * part, EDGE), COLUMN, axis=0, tiled=True)
+    quarters = call(quarter_kernel, jax.ShapeDtypeStruct((plane, part, EDGE), BF), [SMEM, VMEM])(
+        repl, features
+    )
+    quarters = lax.all_to_all(quarters, PLANE, 0, 0, tiled=True)
 
     send = call(
         prepare_kernel,
         jax.ShapeDtypeStruct((n_repl, 192, EDGE), BF),
-        [SMEM] * 2 + [pl.BlockSpec(memory_space=pl.ANY)] * 6,
+        [SMEM] + [pl.BlockSpec(memory_space=pl.ANY)] * 6,
         [
             pltpu.VMEM((tiles, EDGE, EDGE), jnp.int32),
             pltpu.VMEM((64, EDGE), BF),
@@ -303,7 +318,6 @@
         60,
     )(
         tile_blocks,
-        order,
         tile_counts,
         self_one.T,
         neighbor_one.T,
@@ -311,6 +325,8 @@
         self_two.T,
         bias_one[None, :],
     )
+    quarters, send = lax.optimization_barrier((quarters, send))
+    near = lax.all_gather(quarters.reshape(plane * part, EDGE), COLUMN, axis=0, tiled=True)
     got = lax.all_to_all(send, "yl", 0, 0, tiled=True)
     cat = call(lay_kernel, jax.ShapeDtypeStruct((EDGE, tiles * EDGE), BF), [SMEM, VMEM])(
         tile_blocks, tile_counts
@@ -341,12 +357,15 @@
     came = lax.ppermute(give, "yh", swap)
 
     shape = (column, plane, part, EDGE)
+    total = call(
+        gather_one_kernel,
+        jax.ShapeDtypeStruct((EDGE, EDGE), F32),
+        [SMEM, SMEM] + [VMEM] * 3,
+        [pltpu.VMEM((EDGE, tiles * EDGE), BF)],
+    )(tile_blocks, core, near.reshape(shape), far.reshape(shape), cat)
     parts = call(
-        gather_one_kernel,
-        jax.ShapeDtypeStruct((n_repl, EDGE + WIDE, EDGE), F32),
-        [SMEM, SMEM] + [VMEM] * 5,
-        [pltpu.VMEM((EDGE, tiles * EDGE), BF)],
-    )(tile_blocks, core, near.reshape(shape), far.reshape(shape), cat, keep, came)
+        mix_kernel, jax.ShapeDtypeStruct((n_repl, 2 * EDGE + WIDE, EDGE), BF), [VMEM] * 3
+    )(total, keep, came)
     parts = lax.all_to_all(parts, "yl", 0, 0, tiled=True)
 
     send, base = call(
@@ -366,12 +385,13 @@
     )(relay)
     near_two = lax.all_to_all(relay, "x", 0, 0, tiled=True)
     far_two = lax.ppermute(near_two, "core", swap)
-    second, grads = call(
-        gather_two_kernel,
-        (
-            jax.ShapeDtypeStruct((WIDE, EDGE), F32),
-            jax.ShapeDtypeStruct((sheet, chunk, EDGE), F32),
-        ),
+    grads = call(
+        chunk_sum_kernel, jax.ShapeDtypeStruct((2 * sheet, chunk, EDGE), F32), [VMEM]
+    )(near_two[:, sheet * WIDE :])
+    grads = lax.all_to_all(grads, SHEET + ("core",), 0, 0, tiled=True)
+    second = call(
+        functools.partial(gather_two_kernel, sheet),
+        jax.ShapeDtypeStruct((WIDE, EDGE), F32),
         [SMEM] * 2 + [VMEM] * 3,
         [pltpu.VMEM((WIDE, tiles * EDGE), BF)],
     )(tile_blocks, core, near_two, far_two, cat)
@@ -379,7 +399,6 @@
         lax.ppermute(second, "yl", [((i + k) % n_repl, i) for i in range(n_repl)])
         for k in range(1, n_repl)
     ]
-    grads = lax.all_to_all(grads, SHEET, 0, 0, tiled=True).reshape(GRADS, EDGE)
     others = others + [second] * (3 - len(others))
     scores = call(
         scores_kernel,
@@ -400,6 +419,7 @@
             jax.ShapeDtypeStruct((1, CLASSES), F32),
         ),
         [VMEM],
+        [pltpu.VMEM((GRADS, EDGE), F32)],
     )(grads)
     return (
         scores,

time: 185 us -> 174 us (0.941)
  the two profiles are of different devices: /device:TPU:48 before, /device:TPU:17 now
where the time goes in v4:
time: 174 us; the launch traced here: 173 us
  blocking collectives  68.2 us (39%)
  starting transfers between devices  58.3 us (34%)
  waiting for transfers between devices  16.7 us (10%)
  between operations  14.3 us (8%)
  Pallas kernels  12.7 us (7%)
  local copies, waits for them, and re-layouts  3.23 us (2%)
    all_to_all x1, blocking collectives, per_device(): lax.all_to_all(back.reshape(plane, halves_n * WIDE, EDGE), PLANE, 0, 0, t...  22.8 us
    all_to_all x1, blocking collectives, per_device(): relay = lax.all_to_all(send, SHEET, 0, 0, tiled=True)  21.1 us
    all_to_all x1, starting transfers between devices, per_device(): quarters = lax.all_to_all(quarters, PLANE, 0, 0, tiled=True)  12.9 us
    all_to_all x1, blocking collectives, per_device(): parts = lax.all_to_all(parts, 'yl', 0, 0, tiled=True)  12.6 us
    all_to_all x1, blocking collectives, per_device(): near_two = lax.all_to_all(relay, 'x', 0, 0, tiled=True)  11.8 us
    ppermute x3, starting transfers between devices, per_device(): lax.ppermute(second, 'yl', [((i + k) % n_repl, i) for i in range(n_repl)])  9.43 us
    ppermute x1, starting transfers between devices, per_device(): lax.ppermute(other, 'core', swap)  7.06 us
    ppermute x1, starting transfers between devices, per_device(): far = lax.ppermute(near, 'core', swap)  6.59 us
  transfers between devices with their start and end apart: 11, of which 4 were waited for; matrix products, arithmetic and copies ran while one was open for 0% of the time, Pallas kernels for 6%

profile of v4, /device:TPU:17, one launch (start us, length us, event | category | flops | bytes accessed | tf_op | source)
XLA Modules:
  0.0 173.4 jit_solution(10164087232025037599)
XLA Ops:
  8.8 12.9 %all-to-all-start = ((bf16[32,32,128]{2,1,0:T(8,128)(2,1)}), bf16[32,32,128]{2,1,0:T(8,128)(2,1)S(1)}, u32[]{:S(2)}, u32[]{:S(2)}) async-start(bf16[32,32,128]{2,1,0:T(8,128)(2,1)} %shard_map.162), calls=%async_computation | async-start | bytes 524288 | tf_op jit(solution)/shard_map/all_to_all | solution.py:301
  21.8 3.2 %shard_map.163 = bf16[4,192,128]{2,1,0:T(8,128)(2,1)} custom-call(s32[32]{0:T(128)} %blocks.9, s32[32,128,128]{2,1,0:T(8,128)} %counts.3, bf16[64,128]{1,0:T(8,128)(2,1)} %bitcast.25, bf16[64,128]{1,0:T(8,128)(2,1)} %bitcast.26, bf16[47,64]{1,0:T(8,128)(2,1)} %bitcast.27, bf16[47,64]{1,0:T(8,128)(2,1)} %bitcast.28, bf16[1,64]{1,0:T(2,128)(2,1)} %bitcast.29), custom_call_target="tpu_custom_call" | custom-call | tf_op jit(solution)/shard_map/pallas_call | solution.py:303
  25.0 6.4 %all-to-all-done = bf16[32,32,128]{2,1,0:T(8,128)(2,1)S(1)} async-done(((bf16[32,32,128]{2,1,0:T(8,128)(2,1)}), bf16[32,32,128]{2,1,0:T(8,128)(2,1)S(1)}, u32[]{:S(2)}, u32[]{:S(2)}) %all-to-all-start) | async-done | bytes 262176 | tf_op jit(solution)/shard_map/all_to_all | solution.py:301
  32.1 4.7 %all-to-all-start.1 = ((bf16[4,192,128]{2,1,0:T(8,128)(2,1)}), bf16[4,192,128]{2,1,0:T(8,128)(2,1)S(1)}, u32[]{:S(2)}, u32[]{:S(2)}) async-start(bf16[4,192,128]{2,1,0:T(8,128)(2,1)} %shard_map.163), calls=%async_computation.1 | async-start | bytes 393216 | tf_op jit(solution)/shard_map/all_to_all | solution.py:330
  37.7 2.5 %all-to-all-done.1.got = bf16[4,192,128]{2,1,0:T(8,128)(2,1)S(1)} async-done(((bf16[4,192,128]{2,1,0:T(8,128)(2,1)}), bf16[4,192,128]{2,1,0:T(8,128)(2,1)S(1)}, u32[]{:S(2)}, u32[]{:S(2)}) %all-to-all-start.1) | async-done | bytes 196640 | tf_op jit(solution)/shard_map/all_to_all | solution.py:330
  40.2 1.2 shard_map.165
  41.5 7.1 %collective-permute-start = (bf16[64,48,128]{2,1,0:T(8,128)(2,1)S(1)}, bf16[64,48,128]{2,1,0:T(8,128)(2,1)S(1)}, u32[]{:S(2)}, u32[]{:S(2)}) collective-permute-start(bf16[64,48,128]{2,1,0:T(8,128)(2,1)S(1)} %get-tuple-element.28), channel_id=1, source_target_pairs={{0,4},{4,0},{1,5},{5,1},{2,6},{6,2},{3,7},{7,3},{8,12},{12,8},{9,1... | collective-permute-start | bytes 2359304 | tf_op jit(solution)/shard_map/ppermute | solution.py:351
  48.5 1.9 %collective-permute-done.other = bf16[64,48,128]{2,1,0:T(8,128)(2,1)S(1)} collective-permute-done((bf16[64,48,128]{2,1,0:T(8,128)(2,1)S(1)}, bf16[64,48,128]{2,1,0:T(8,128)(2,1)S(1)}, u32[]{:S(2)}, u32[]{:S(2)}) %collective-permute-start) | collective-permute-done | bytes 786464 | tf_op jit(solution)/shard_map/ppermute | solution.py:351
  50.6 22.8 %all_to_all.35.got = bf16[32,96,128]{2,1,0:T(8,128)(2,1)S(1)} all-to-all(bf16[32,96,128]{2,1,0:T(8,128)(2,1)S(1)} %bitcast.20), channel_id=1, replica_groups=mesh['x'=4,'z'=8,'yh'=2,'core'=2,'yl'=4] {'x','z'}, dimensions={0} | all-to-all | bytes 1572864 | tf_op jit(solution)/shard_map/all_to_all | solution.py:352
  73.3 6.6 %collective-permute-start.1 = (bf16[8192,128]{1,0:T(8,128)(2,1)}, bf16[8192,128]{1,0:T(8,128)(2,1)}, u32[]{:S(2)}, u32[]{:S(2)}) collective-permute-start(bf16[8192,128]{1,0:T(8,128)(2,1)} %all-gather.2.cloned.1.call-done), channel_id=1, source_target_pairs={{0,4},{4,0},{1,5},{5,1},{2,6},{6,2},{3,7},{7,3},{8,12},{12,8},{9,1... | collective-permute-start | bytes 6291464 | tf_op jit(solution)/shard_map/ppermute | solution.py:354
  80.1 5.9 %collective-permute-start.2 = (f32[48,128]{1,0:T(8,128)S(1)}, f32[48,128]{1,0:T(8,128)S(1)}, u32[]{:S(2)}, u32[]{:S(2)}) collective-permute-start(f32[48,128]{1,0:T(8,128)S(1)} %get-tuple-element.32), channel_id=1, source_target_pairs={{0,8},{8,0},{1,9},{9,1},{2,10},{10,2},{3,11},{11,3},{4,12},{12,4},... | collective-permute-start | bytes 73736 | tf_op jit(solution)/shard_map/ppermute | solution.py:357
  86.0 1.6 copy-done.1
  87.6 2.2 %shard_map.167.total = f32[128,128]{1,0:T(8,128)S(1)} custom-call(s32[32]{0:T(128)S(1)} %copy-done.4, s32[1]{0:T(128)} %bitcast.1.core, bf16[8,32,32,128]{3,2,1,0:T(8,128)(2,1)S(1)} %bitcast.21, bf16[8,32,32,128]{3,2,1,0:T(8,128)(2,1)} %bitcast.11.far, bf16[128,4096]{1,0:T(8,128)(2,1)S(1)} %shard_map.164.cat), custom_call_target="tpu_custom_call" | custom-call | tf_op jit(solution)/shard_map/pallas_call | solution.py:360
  89.8 12.6 %all_to_all.36.parts = bf16[4,304,128]{2,1,0:T(8,128)(2,1)S(1)} all-to-all(bf16[4,304,128]{2,1,0:T(8,128)(2,1)S(1)} %shard_map.169), channel_id=1, replica_groups=mesh['x'=4,'z'=8,'yh'=2,'core'=2,'yl'=4] {'yl'}, dimensions={0} | all-to-all | bytes 622592 | tf_op jit(solution)/shard_map/all_to_all | solution.py:369
  102.4 1.0 shard_map.170
  103.4 21.1 %all_to_all.37.got = bf16[16,80,128]{2,1,0:T(8,128)(2,1)S(1)} all-to-all(bf16[16,80,128]{2,1,0:T(8,128)(2,1)S(1)} %get-tuple-element.35), channel_id=1, replica_groups=mesh['x'=4,'z'=8,'yh'=2,'core'=2,'yl'=4] {'z','yh'}, dimensions={0} | all-to-all | bytes 655360 | tf_op jit(solution)/shard_map/all_to_all | solution.py:380
  124.7 11.8 %all_to_all.38.own = bf16[4,800,128]{2,1,0:T(8,128)(2,1)S(1)} all-to-all(bf16[4,800,128]{2,1,0:T(8,128)(2,1)S(1)} %shard_map.171), channel_id=1, replica_groups=mesh['x'=4,'z'=8,'yh'=2,'core'=2,'yl'=4] {'x'}, dimensions={0} | all-to-all | bytes 1638400 | tf_op jit(solution)/shard_map/all_to_all | solution.py:386
  136.4 6.1 %collective-permute-start.3 = (bf16[4,800,128]{2,1,0:T(8,128)(2,1)S(1)}, bf16[4,800,128]{2,1,0:T(8,128)(2,1)S(1)}, u32[]{:S(2)}, u32[]{:S(2)}) collective-permute-start(bf16[4,800,128]{2,1,0:T(8,128)(2,1)S(1)} %all_to_all.38.own), channel_id=1, source_target_pairs={{0,4},{4,0},{1,5},{5,1},{2,6},{6,2},{3,7},{7,3},{8,12},{12,8},{9,1... | collective-permute-start | bytes 2457608 | tf_op jit(solution)/shard_map/ppermute | solution.py:387
  143.3 5.6 %all-to-all-start.6 = ((f32[32,16,128]{2,1,0:T(8,128)}), f32[32,16,128]{2,1,0:T(8,128)S(1)}, u32[]{:S(2)}, u32[]{:S(2)}) async-start(f32[32,16,128]{2,1,0:T(8,128)} %shard_map.174), calls=%async_computation.6 | async-start | bytes 524288 | tf_op jit(solution)/shard_map/all_to_all | solution.py:391
  148.9 1.0 shard_map.172.own
  149.9 1.9 %collective-permute-start.4 = (f32[48,128]{1,0:T(8,128)S(1)}, f32[48,128]{1,0:T(8,128)S(1)}, u32[]{:S(2)}, u32[]{:S(2)}) collective-permute-start(f32[48,128]{1,0:T(8,128)S(1)} %shard_map.172.own), channel_id=1, source_target_pairs={{1,0},{2,1},{3,2},{0,3},{5,4},{6,5},{7,6},{4,7},{9,8},{10,9},{11,1... | collective-permute-start | bytes 73736 | tf_op jit(solution)/shard_map/ppermute | solution.py:399
  151.8 5.6 %collective-permute-start.5 = (f32[48,128]{1,0:T(8,128)S(1)}, f32[48,128]{1,0:T(8,128)S(1)}, u32[]{:S(2)}, u32[]{:S(2)}) collective-permute-start(f32[48,128]{1,0:T(8,128)S(1)} %shard_map.172.own), channel_id=1, source_target_pairs={{2,0},{3,1},{0,2},{1,3},{6,4},{7,5},{4,6},{5,7},{10,8},{11,9},{8,1... | collective-permute-start | bytes 73736 | tf_op jit(solution)/shard_map/ppermute | solution.py:399
  157.4 1.9 %collective-permute-start.6 = (f32[48,128]{1,0:T(8,128)S(1)}, f32[48,128]{1,0:T(8,128)S(1)}, u32[]{:S(2)}, u32[]{:S(2)}) collective-permute-start(f32[48,128]{1,0:T(8,128)S(1)} %shard_map.172.own), channel_id=1, source_target_pairs={{3,0},{0,1},{1,2},{2,3},{7,4},{4,5},{5,6},{6,7},{11,8},{8,9},{9,10... | collective-permute-start | bytes 73736 | tf_op jit(solution)/shard_map/ppermute | solution.py:399
  159.4 5.8 %all-to-all-done.6.got = f32[32,16,128]{2,1,0:T(8,128)S(1)} async-done(((f32[32,16,128]{2,1,0:T(8,128)}), f32[32,16,128]{2,1,0:T(8,128)S(1)}, u32[]{:S(2)}, u32[]{:S(2)}) %all-to-all-start.6) | async-done | bytes 262176 | tf_op jit(solution)/shard_map/all_to_all | solution.py:391
  (37 shorter events, 5.8 us)
Async XLA Ops:
  7.2 29.6 %copy-start = (s32[32,128,128]{2,1,0:T(8,128)S(1)}, s32[32,128,128]{2,1,0:T(8,128)}, u32[]{:S(2)}) copy-start(s32[32,128,128]{2,1,0:T(8,128)} %counts.3) | copy-start | bytes 6291460
  7.2 0.9 copy-start.2
  8.1 28.7 %copy-start.4 = (s32[32]{0:T(128)S(1)}, s32[32]{0:T(128)}, u32[]{:S(2)}) copy-start(s32[32]{0:T(128)} %blocks.9) | copy-start | bytes 388
  8.8 22.6 %all-to-all-start = ((bf16[32,32,128]{2,1,0:T(8,128)(2,1)}), bf16[32,32,128]{2,1,0:T(8,128)(2,1)S(1)}, u32[]{:S(2)}, u32[]{:S(2)}) async-start(bf16[32,32,128]{2,1,0:T(8,128)(2,1)} %shard_map.162), calls=%async_computation | async-start | bytes 524288 | tf_op jit(solution)/shard_map/all_to_all | solution.py:301
  21.7 51.6 %all-gather.2.cloned.1.call-start = ((), (), s32[]{:S(2)}) async-start(), calls=%async_computation.7 | async-start | bytes 2359296 | tf_op jit(solution)/shard_map/all_gather | solution.py:329
  25.0 12.7 %copy-start.8 = (bf16[47,128]{1,0:T(8,128)(2,1)S(1)}, bf16[47,128]{1,0:T(8,128)(2,1)}, u32[]{:S(2)}) copy-start(bf16[47,128]{1,0:T(8,128)(2,1)} %param.15) | copy-start | bytes 36100
  25.0 15.2 %copy-start.5 = (s32[128]{0:T(128)S(1)}, s32[128]{0:T(128)}, u32[]{:S(2)}) copy-start(s32[128]{0:T(128)} %param.14) | copy-start | bytes 1540
  31.4 0.7 copy-start.7
  32.1 8.1 %all-to-all-start.1 = ((bf16[4,192,128]{2,1,0:T(8,128)(2,1)}), bf16[4,192,128]{2,1,0:T(8,128)(2,1)S(1)}, u32[]{:S(2)}, u32[]{:S(2)}) async-start(bf16[4,192,128]{2,1,0:T(8,128)(2,1)} %shard_map.163), calls=%async_computation.1 | async-start | bytes 393216 | tf_op jit(solution)/shard_map/all_to_all | solution.py:330
  41.5 9.0 %collective-permute-start = (bf16[64,48,128]{2,1,0:T(8,128)(2,1)S(1)}, bf16[64,48,128]{2,1,0:T(8,128)(2,1)S(1)}, u32[]{:S(2)}, u32[]{:S(2)}) collective-permute-start(bf16[64,48,128]{2,1,0:T(8,128)(2,1)S(1)} %get-tuple-element.28), channel_id=1, source_target_pairs={{0,4},{4,0},{1,5},{5,1},{2,6},{6,2},{3,7},{7,3},{8,12},{12,8},{9,1... | collective-permute-start | bytes 2359304 | tf_op jit(solution)/shard_map/ppermute | solution.py:351
  73.3 12.7 %collective-permute-start.1 = (bf16[8192,128]{1,0:T(8,128)(2,1)}, bf16[8192,128]{1,0:T(8,128)(2,1)}, u32[]{:S(2)}, u32[]{:S(2)}) collective-permute-start(bf16[8192,128]{1,0:T(8,128)(2,1)} %all-gather.2.cloned.1.call-done), channel_id=1, source_target_pairs={{0,4},{4,0},{1,5},{5,1},{2,6},{6,2},{3,7},{7,3},{8,12},{12,8},{9,1... | collective-permute-start | bytes 6291464 | tf_op jit(solution)/shard_map/ppermute | solution.py:354
  80.1 9.7 %collective-permute-start.2 = (f32[48,128]{1,0:T(8,128)S(1)}, f32[48,128]{1,0:T(8,128)S(1)}, u32[]{:S(2)}, u32[]{:S(2)}) collective-permute-start(f32[48,128]{1,0:T(8,128)S(1)} %get-tuple-element.32), channel_id=1, source_target_pairs={{0,8},{8,0},{1,9},{9,1},{2,10},{10,2},{3,11},{11,3},{4,12},{12,4},... | collective-permute-start | bytes 73736 | tf_op jit(solution)/shard_map/ppermute | solution.py:357
  86.0 1.6 copy-start.1
  87.6 14.8 %copy-start.3 = (bf16[128,128]{1,0:T(8,128)(2,1)S(1)}, bf16[128,128]{1,0:T(8,128)(2,1)}, u32[]{:S(2)}) copy-start(bf16[128,128]{1,0:T(8,128)(2,1)} %features.3) | copy-start | bytes 98308
  87.6 14.8 %copy-start.6 = (bf16[47]{0:T(256)(128)(2,1)S(1)}, bf16[47]{0:T(256)(128)(2,1)}, u32[]{:S(2)}) copy-start(bf16[47]{0:T(256)(128)(2,1)} %param.21) | copy-start | bytes 286
  136.4 12.4 %collective-permute-start.3 = (bf16[4,800,128]{2,1,0:T(8,128)(2,1)S(1)}, bf16[4,800,128]{2,1,0:T(8,128)(2,1)S(1)}, u32[]{:S(2)}, u32[]{:S(2)}) collective-permute-start(bf16[4,800,128]{2,1,0:T(8,128)(2,1)S(1)} %all_to_all.38.own), channel_id=1, source_target_pairs={{0,4},{4,0},{1,5},{5,1},{2,6},{6,2},{3,7},{7,3},{8,12},{12,8},{9,1... | collective-permute-start | bytes 2457608 | tf_op jit(solution)/shard_map/ppermute | solution.py:387
  143.3 21.9 %all-to-all-start.6 = ((f32[32,16,128]{2,1,0:T(8,128)}), f32[32,16,128]{2,1,0:T(8,128)S(1)}, u32[]{:S(2)}, u32[]{:S(2)}) async-start(f32[32,16,128]{2,1,0:T(8,128)} %shard_map.174), calls=%async_computation.6 | async-start | bytes 524288 | tf_op jit(solution)/shard_map/all_to_all | solution.py:391
  149.9 16.0 %collective-permute-start.4 = (f32[48,128]{1,0:T(8,128)S(1)}, f32[48,128]{1,0:T(8,128)S(1)}, u32[]{:S(2)}, u32[]{:S(2)}) collective-permute-start(f32[48,128]{1,0:T(8,128)S(1)} %shard_map.172.own), channel_id=1, source_target_pairs={{1,0},{2,1},{3,2},{0,3},{5,4},{6,5},{7,6},{4,7},{9,8},{10,9},{11,1... | collective-permute-start | bytes 73736 | tf_op jit(solution)/shard_map/ppermute | solution.py:399
  151.8 14.0 %collective-permute-start.5 = (f32[48,128]{1,0:T(8,128)S(1)}, f32[48,128]{1,0:T(8,128)S(1)}, u32[]{:S(2)}, u32[]{:S(2)}) collective-permute-start(f32[48,128]{1,0:T(8,128)S(1)} %shard_map.172.own), channel_id=1, source_target_pairs={{2,0},{3,1},{0,2},{1,3},{6,4},{7,5},{4,6},{5,7},{10,8},{11,9},{8,1... | collective-permute-start | bytes 73736 | tf_op jit(solution)/shard_map/ppermute | solution.py:399
  157.4 8.5 %collective-permute-start.6 = (f32[48,128]{1,0:T(8,128)S(1)}, f32[48,128]{1,0:T(8,128)S(1)}, u32[]{:S(2)}, u32[]{:S(2)}) collective-permute-start(f32[48,128]{1,0:T(8,128)S(1)} %shard_map.172.own), channel_id=1, source_target_pairs={{3,0},{0,1},{1,2},{2,3},{7,4},{4,5},{5,6},{6,7},{11,8},{8,9},{9,10... | collective-permute-start | bytes 73736 | tf_op jit(solution)/shard_map/ppermute | solution.py:399
Sparse Core Ops, SparseCore 0:
  32.3 38.2 all-gather.1

commit v5 on v4

--- a/solution.py
+++ b/solution.py
@@ -147,11 +147,11 @@
 
 
 def mix_kernel(total, keep, came, send):
-    part = halves(total[...])
+    part = total[...].astype(BF)
     terms = (keep[...] + came[...]).astype(BF)
     for r in range(send.shape[0]):
-        send[r, 0 : 2 * EDGE] = part
-        send[r, 2 * EDGE :] = terms
+        send[r, 0:EDGE] = part
+        send[r, EDGE:] = terms
 
 
 def layer_kernel(repl, parts, got, up, inv, features, bias_two, send, base, packed, pad):
@@ -160,7 +160,7 @@
     both = parts[0].astype(F32)
     for r in range(1, n_repl):
         both = both + parts[r].astype(F32)
-    mean = ((both[0:EDGE] + both[EDGE : 2 * EDGE]) * inv[0:1]).astype(BF)
+    mean = (both[0:EDGE] * inv[0:1]).astype(BF)
     feat = features[...]
     last = lax.broadcasted_iota(jnp.int32, (WIDE, EDGE), 0) == CLASSES
     unit = jnp.where(last, 1.0, 0.0).astype(BF)
@@ -182,7 +182,7 @@
     pad[0:1, 0:CLASSES] = bias_two[...].astype(F32)
     base[...] = skipped + dot(pad[...].astype(BF), jnp.ones((8, EDGE), BF), TN)[0:WIDE]
 
-    pulled = both[2 * EDGE :].astype(BF)
+    pulled = both[EDGE:].astype(BF)
     upstream = up[...]
     mine = repl[0]
     pre = before(mine)
@@ -350,11 +350,11 @@
         [VMEM] * 2,
     )(mine, lax.ppermute(other, "core", swap))
     back = lax.all_to_all(back.reshape(plane, halves_n * WIDE, EDGE), PLANE, 0, 0, tiled=True)
-    near, back = lax.optimization_barrier((near, back))
-    far = lax.ppermute(near, "core", swap)
     half = jax.ShapeDtypeStruct((WIDE, EDGE), F32)
     keep, give = call(plane_sum_kernel, (half, half), [SMEM, VMEM])(side, back)
+    near, give = lax.optimization_barrier((near, give))
     came = lax.ppermute(give, "yh", swap)
+    far = lax.ppermute(near, "core", swap)
 
     shape = (column, plane, part, EDGE)
     total = call(
@@ -364,7 +364,7 @@
         [pltpu.VMEM((EDGE, tiles * EDGE), BF)],
     )(tile_blocks, core, near.reshape(shape), far.reshape(shape), cat)
     parts = call(
-        mix_kernel, jax.ShapeDtypeStruct((n_repl, 2 * EDGE + WIDE, EDGE), BF), [VMEM] * 3
+        mix_kernel, jax.ShapeDtypeStruct((n_repl, EDGE + WIDE, EDGE), BF), [VMEM] * 3
     )(total, keep, came)
     parts = lax.all_to_all(parts, "yl", 0, 0, tiled=True)
 

time: 174 us -> 172 us (0.989)
  the two profiles are of different devices: /device:TPU:17 before, /device:TPU:16 now
where the time goes in v5:
time: 172 us; the launch traced here: 171 us
  starting transfers between devices  51.1 us (30%)
  blocking collectives  46 us (27%)
  waiting for transfers between devices  44 us (26%)
  between operations  14.3 us (8%)
  Pallas kernels  12.5 us (7%)
  local copies, waits for them, and re-layouts  3.22 us (2%)
    all_to_all x1, blocking collectives, per_device(): relay = lax.all_to_all(send, SHEET, 0, 0, tiled=True)  23.4 us
    all_to_all x1, waiting for transfers between devices, per_device(): lax.all_to_all(back.reshape(plane, halves_n * WIDE, EDGE), PLANE, 0, 0, t...  22.9 us
    all_to_all x1, starting transfers between devices, per_device(): quarters = lax.all_to_all(quarters, PLANE, 0, 0, tiled=True)  13.2 us
    all_to_all x1, blocking collectives, per_device(): near_two = lax.all_to_all(relay, 'x', 0, 0, tiled=True)  12.6 us
    ppermute x3, starting transfers between devices, per_device(): lax.ppermute(second, 'yl', [((i + k) % n_repl, i) for i in range(n_repl)])  10.3 us
    all_to_all x1, blocking collectives, per_device(): parts = lax.all_to_all(parts, 'yl', 0, 0, tiled=True)  9.91 us
    all_to_all x1, waiting for transfers between devices, per_device(): quarters = lax.all_to_all(quarters, PLANE, 0, 0, tiled=True)  9.2 us
    ppermute x1, starting transfers between devices, per_device(): came = lax.ppermute(give, 'yh', swap)  6.2 us
  transfers between devices with their start and end apart: 12, of which 6 were waited for; matrix products, arithmetic and copies ran while one was open for 0% of the time, Pallas kernels for 6%

profile of v5, /device:TPU:16, one launch (start us, length us, event | category | flops | bytes accessed | tf_op | source)
XLA Modules:
  0.0 171.1 jit_solution(1746717669340223634)
XLA Ops:
  8.8 13.2 %all-to-all-start = ((bf16[32,32,128]{2,1,0:T(8,128)(2,1)}), bf16[32,32,128]{2,1,0:T(8,128)(2,1)S(1)}, u32[]{:S(2)}, u32[]{:S(2)}) async-start(bf16[32,32,128]{2,1,0:T(8,128)(2,1)} %shard_map.162), calls=%async_computation | async-start | bytes 524288 | tf_op jit(solution)/shard_map/all_to_all | solution.py:301
  22.1 3.2 %shard_map.163 = bf16[4,192,128]{2,1,0:T(8,128)(2,1)} custom-call(s32[32]{0:T(128)} %blocks.9, s32[32,128,128]{2,1,0:T(8,128)} %counts.3, bf16[64,128]{1,0:T(8,128)(2,1)} %bitcast.25, bf16[64,128]{1,0:T(8,128)(2,1)} %bitcast.26, bf16[47,64]{1,0:T(8,128)(2,1)} %bitcast.27, bf16[47,64]{1,0:T(8,128)(2,1)} %bitcast.28, bf16[1,64]{1,0:T(2,128)(2,1)} %bitcast.29), custom_call_target="tpu_custom_call" | custom-call | tf_op jit(solution)/shard_map/pallas_call | solution.py:303
  25.3 9.2 %all-to-all-done = bf16[32,32,128]{2,1,0:T(8,128)(2,1)S(1)} async-done(((bf16[32,32,128]{2,1,0:T(8,128)(2,1)}), bf16[32,32,128]{2,1,0:T(8,128)(2,1)S(1)}, u32[]{:S(2)}, u32[]{:S(2)}) %all-to-all-start) | async-done | bytes 262176 | tf_op jit(solution)/shard_map/all_to_all | solution.py:301
  35.2 5.2 %all-to-all-start.1 = ((bf16[4,192,128]{2,1,0:T(8,128)(2,1)}), bf16[4,192,128]{2,1,0:T(8,128)(2,1)S(1)}, u32[]{:S(2)}, u32[]{:S(2)}) async-start(bf16[4,192,128]{2,1,0:T(8,128)(2,1)} %shard_map.163), calls=%async_computation.1 | async-start | bytes 393216 | tf_op jit(solution)/shard_map/all_to_all | solution.py:330
  41.3 3.4 %all-to-all-done.1.got = bf16[4,192,128]{2,1,0:T(8,128)(2,1)S(1)} async-done(((bf16[4,192,128]{2,1,0:T(8,128)(2,1)}), bf16[4,192,128]{2,1,0:T(8,128)(2,1)S(1)}, u32[]{:S(2)}, u32[]{:S(2)}) %all-to-all-start.1) | async-done | bytes 196640 | tf_op jit(solution)/shard_map/all_to_all | solution.py:330
  44.7 1.2 shard_map.165
  45.9 1.9 %collective-permute-start = (bf16[64,48,128]{2,1,0:T(8,128)(2,1)S(1)}, bf16[64,48,128]{2,1,0:T(8,128)(2,1)S(1)}, u32[]{:S(2)}, u32[]{:S(2)}) collective-permute-start(bf16[64,48,128]{2,1,0:T(8,128)(2,1)S(1)} %get-tuple-element.28), channel_id=1, source_target_pairs={{0,4},{4,0},{1,5},{5,1},{2,6},{6,2},{3,7},{7,3},{8,12},{12,8},{9,1... | collective-permute-start | bytes 2359304 | tf_op jit(solution)/shard_map/ppermute | solution.py:351
  47.8 2.3 %collective-permute-done.other = bf16[64,48,128]{2,1,0:T(8,128)(2,1)S(1)} collective-permute-done((bf16[64,48,128]{2,1,0:T(8,128)(2,1)S(1)}, bf16[64,48,128]{2,1,0:T(8,128)(2,1)S(1)}, u32[]{:S(2)}, u32[]{:S(2)}) %collective-permute-start) | collective-permute-done | bytes 786464 | tf_op jit(solution)/shard_map/ppermute | solution.py:351
  50.1 1.1 shard_map.166
  51.2 4.4 %all-to-all-start.2 = ((bf16[32,96,128]{2,1,0:T(8,128)(2,1)}), bf16[32,96,128]{2,1,0:T(8,128)(2,1)S(1)}, u32[]{:S(2)}, u32[]{:S(2)}) async-start(bf16[32,96,128]{2,1,0:T(8,128)(2,1)} %bitcast.10), calls=%async_computation.2 | async-start | bytes 1572864 | tf_op jit(solution)/shard_map/all_to_all | solution.py:352
  55.6 22.9 %all-to-all-done.2.got = bf16[32,96,128]{2,1,0:T(8,128)(2,1)S(1)} async-done(((bf16[32,96,128]{2,1,0:T(8,128)(2,1)}), bf16[32,96,128]{2,1,0:T(8,128)(2,1)S(1)}, u32[]{:S(2)}, u32[]{:S(2)}) %all-to-all-start.2) | async-done | bytes 786464 | tf_op jit(solution)/shard_map/all_to_all | solution.py:352
  78.6 1.9 %collective-permute-start.1 = (bf16[8192,128]{1,0:T(8,128)(2,1)}, bf16[8192,128]{1,0:T(8,128)(2,1)S(1)}, u32[]{:S(2)}, u32[]{:S(2)}) collective-permute-start(bf16[8192,128]{1,0:T(8,128)(2,1)} %all-gather.2.cloned.1.call-done), channel_id=1, source_target_pairs={{0,4},{4,0},{1,5},{5,1},{2,6},{6,2},{3,7},{7,3},{8,12},{12,8},{9,1... | collective-permute-start | bytes 6291464 | tf_op jit(solution)/shard_map/ppermute | solution.py:357
  80.6 6.2 %collective-permute-start.2 = (f32[48,128]{1,0:T(8,128)S(1)}, f32[48,128]{1,0:T(8,128)S(1)}, u32[]{:S(2)}, u32[]{:S(2)}) collective-permute-start(f32[48,128]{1,0:T(8,128)S(1)} %get-tuple-element.32), channel_id=1, source_target_pairs={{0,8},{8,0},{1,9},{9,1},{2,10},{10,2},{3,11},{11,3},{4,12},{12,4},... | collective-permute-start | bytes 73736 | tf_op jit(solution)/shard_map/ppermute | solution.py:356
  86.8 1.6 copy-done.1
  88.4 1.1 shard_map.168.total
  90.2 9.9 %all_to_all.35.parts = bf16[4,176,128]{2,1,0:T(8,128)(2,1)S(1)} all-to-all(bf16[4,176,128]{2,1,0:T(8,128)(2,1)S(1)} %shard_map.169), channel_id=1, replica_groups=mesh['x'=4,'z'=8,'yh'=2,'core'=2,'yl'=4] {'yl'}, dimensions={0} | all-to-all | bytes 360448 | tf_op jit(solution)/shard_map/all_to_all | solution.py:369
  101.1 23.4 %all_to_all.36.got = bf16[16,80,128]{2,1,0:T(8,128)(2,1)S(1)} all-to-all(bf16[16,80,128]{2,1,0:T(8,128)(2,1)S(1)} %get-tuple-element.35), channel_id=1, replica_groups=mesh['x'=4,'z'=8,'yh'=2,'core'=2,'yl'=4] {'z','yh'}, dimensions={0} | all-to-all | bytes 655360 | tf_op jit(solution)/shard_map/all_to_all | solution.py:380
  124.7 12.6 %all_to_all.37.own = bf16[4,800,128]{2,1,0:T(8,128)(2,1)S(1)} all-to-all(bf16[4,800,128]{2,1,0:T(8,128)(2,1)S(1)} %shard_map.171), channel_id=1, replica_groups=mesh['x'=4,'z'=8,'yh'=2,'core'=2,'yl'=4] {'x'}, dimensions={0} | all-to-all | bytes 1638400 | tf_op jit(solution)/shard_map/all_to_all | solution.py:386
  137.3 1.9 %collective-permute-start.3 = (bf16[4,800,128]{2,1,0:T(8,128)(2,1)S(1)}, bf16[4,800,128]{2,1,0:T(8,128)(2,1)S(1)}, u32[]{:S(2)}, u32[]{:S(2)}) collective-permute-start(bf16[4,800,128]{2,1,0:T(8,128)(2,1)S(1)} %all_to_all.37.own), channel_id=1, source_target_pairs={{0,4},{4,0},{1,5},{5,1},{2,6},{6,2},{3,7},{7,3},{8,12},{12,8},{9,1... | collective-permute-start | bytes 2457608 | tf_op jit(solution)/shard_map/ppermute | solution.py:387
  140.0 6.0 %all-to-all-start.6 = ((f32[32,16,128]{2,1,0:T(8,128)}), f32[32,16,128]{2,1,0:T(8,128)S(1)}, u32[]{:S(2)}, u32[]{:S(2)}) async-start(f32[32,16,128]{2,1,0:T(8,128)} %shard_map.174), calls=%async_computation.6 | async-start | bytes 524288 | tf_op jit(solution)/shard_map/all_to_all | solution.py:391
  147.1 1.9 %collective-permute-start.4 = (f32[48,128]{1,0:T(8,128)S(1)}, f32[48,128]{1,0:T(8,128)S(1)}, u32[]{:S(2)}, u32[]{:S(2)}) collective-permute-start(f32[48,128]{1,0:T(8,128)S(1)} %shard_map.172.own), channel_id=1, source_target_pairs={{1,0},{2,1},{3,2},{0,3},{5,4},{6,5},{7,6},{4,7},{9,8},{10,9},{11,1... | collective-permute-start | bytes 73736 | tf_op jit(solution)/shard_map/ppermute | solution.py:399
  149.0 6.5 %collective-permute-start.5 = (f32[48,128]{1,0:T(8,128)S(1)}, f32[48,128]{1,0:T(8,128)S(1)}, u32[]{:S(2)}, u32[]{:S(2)}) collective-permute-start(f32[48,128]{1,0:T(8,128)S(1)} %shard_map.172.own), channel_id=1, source_target_pairs={{2,0},{3,1},{0,2},{1,3},{6,4},{7,5},{4,6},{5,7},{10,8},{11,9},{8,1... | collective-permute-start | bytes 73736 | tf_op jit(solution)/shard_map/ppermute | solution.py:399
  155.5 1.9 %collective-permute-start.6 = (f32[48,128]{1,0:T(8,128)S(1)}, f32[48,128]{1,0:T(8,128)S(1)}, u32[]{:S(2)}, u32[]{:S(2)}) collective-permute-start(f32[48,128]{1,0:T(8,128)S(1)} %shard_map.172.own), channel_id=1, source_target_pairs={{3,0},{0,1},{1,2},{2,3},{7,4},{4,5},{5,6},{6,7},{11,8},{8,9},{9,10... | collective-permute-start | bytes 73736 | tf_op jit(solution)/shard_map/ppermute | solution.py:399
  157.4 5.5 %all-to-all-done.6.got = f32[32,16,128]{2,1,0:T(8,128)S(1)} async-done(((f32[32,16,128]{2,1,0:T(8,128)}), f32[32,16,128]{2,1,0:T(8,128)S(1)}, u32[]{:S(2)}, u32[]{:S(2)}) %all-to-all-start.6) | async-done | bytes 262176 | tf_op jit(solution)/shard_map/all_to_all | solution.py:391
  (38 shorter events, 8.4 us)
Async XLA Ops:
  7.2 33.2 %copy-start = (s32[32,128,128]{2,1,0:T(8,128)S(1)}, s32[32,128,128]{2,1,0:T(8,128)}, u32[]{:S(2)}) copy-start(s32[32,128,128]{2,1,0:T(8,128)} %counts.3) | copy-start | bytes 6291460
  7.2 0.9 copy-start.2
  8.1 32.3 %copy-start.4 = (s32[32]{0:T(128)S(1)}, s32[32]{0:T(128)}, u32[]{:S(2)}) copy-start(s32[32]{0:T(128)} %blocks.9) | copy-start | bytes 388
  8.8 25.6 %all-to-all-start = ((bf16[32,32,128]{2,1,0:T(8,128)(2,1)}), bf16[32,32,128]{2,1,0:T(8,128)(2,1)S(1)}, u32[]{:S(2)}, u32[]{:S(2)}) async-start(bf16[32,32,128]{2,1,0:T(8,128)(2,1)} %shard_map.162), calls=%async_computation | async-start | bytes 524288 | tf_op jit(solution)/shard_map/all_to_all | solution.py:301
  22.0 56.6 %all-gather.2.cloned.1.call-start = ((), (), s32[]{:S(2)}) async-start(), calls=%async_computation.7 | async-start | bytes 2359296 | tf_op jit(solution)/shard_map/all_gather | solution.py:329
  25.2 16.0 %copy-start.8 = (bf16[47,128]{1,0:T(8,128)(2,1)S(1)}, bf16[47,128]{1,0:T(8,128)(2,1)}, u32[]{:S(2)}) copy-start(bf16[47,128]{1,0:T(8,128)(2,1)} %param.15) | copy-start | bytes 36100
  25.2 19.4 %copy-start.5 = (s32[128]{0:T(128)S(1)}, s32[128]{0:T(128)}, u32[]{:S(2)}) copy-start(s32[128]{0:T(128)} %param.14) | copy-start | bytes 1540
  34.5 0.7 copy-start.7
  35.2 9.5 %all-to-all-start.1 = ((bf16[4,192,128]{2,1,0:T(8,128)(2,1)}), bf16[4,192,128]{2,1,0:T(8,128)(2,1)S(1)}, u32[]{:S(2)}, u32[]{:S(2)}) async-start(bf16[4,192,128]{2,1,0:T(8,128)(2,1)} %shard_map.163), calls=%async_computation.1 | async-start | bytes 393216 | tf_op jit(solution)/shard_map/all_to_all | solution.py:330
  45.9 4.2 %collective-permute-start = (bf16[64,48,128]{2,1,0:T(8,128)(2,1)S(1)}, bf16[64,48,128]{2,1,0:T(8,128)(2,1)S(1)}, u32[]{:S(2)}, u32[]{:S(2)}) collective-permute-start(bf16[64,48,128]{2,1,0:T(8,128)(2,1)S(1)} %get-tuple-element.28), channel_id=1, source_target_pairs={{0,4},{4,0},{1,5},{5,1},{2,6},{6,2},{3,7},{7,3},{8,12},{12,8},{9,1... | collective-permute-start | bytes 2359304 | tf_op jit(solution)/shard_map/ppermute | solution.py:351
  51.2 27.3 %all-to-all-start.2 = ((bf16[32,96,128]{2,1,0:T(8,128)(2,1)}), bf16[32,96,128]{2,1,0:T(8,128)(2,1)S(1)}, u32[]{:S(2)}, u32[]{:S(2)}) async-start(bf16[32,96,128]{2,1,0:T(8,128)(2,1)} %bitcast.10), calls=%async_computation.2 | async-start | bytes 1572864 | tf_op jit(solution)/shard_map/all_to_all | solution.py:352
  78.6 8.1 %collective-permute-start.1 = (bf16[8192,128]{1,0:T(8,128)(2,1)}, bf16[8192,128]{1,0:T(8,128)(2,1)S(1)}, u32[]{:S(2)}, u32[]{:S(2)}) collective-permute-start(bf16[8192,128]{1,0:T(8,128)(2,1)} %all-gather.2.cloned.1.call-done), channel_id=1, source_target_pairs={{0,4},{4,0},{1,5},{5,1},{2,6},{6,2},{3,7},{7,3},{8,12},{12,8},{9,1... | collective-permute-start | bytes 6291464 | tf_op jit(solution)/shard_map/ppermute | solution.py:357
  80.6 9.6 %collective-permute-start.2 = (f32[48,128]{1,0:T(8,128)S(1)}, f32[48,128]{1,0:T(8,128)S(1)}, u32[]{:S(2)}, u32[]{:S(2)}) collective-permute-start(f32[48,128]{1,0:T(8,128)S(1)} %get-tuple-element.32), channel_id=1, source_target_pairs={{0,8},{8,0},{1,9},{9,1},{2,10},{10,2},{3,11},{11,3},{4,12},{12,4},... | collective-permute-start | bytes 73736 | tf_op jit(solution)/shard_map/ppermute | solution.py:356
  86.8 1.6 copy-start.1
  88.4 11.7 %copy-start.3 = (bf16[128,128]{1,0:T(8,128)(2,1)S(1)}, bf16[128,128]{1,0:T(8,128)(2,1)}, u32[]{:S(2)}) copy-start(bf16[128,128]{1,0:T(8,128)(2,1)} %features.3) | copy-start | bytes 98308
  88.4 11.7 %copy-start.6 = (bf16[47]{0:T(256)(128)(2,1)S(1)}, bf16[47]{0:T(256)(128)(2,1)}, u32[]{:S(2)}) copy-start(bf16[47]{0:T(256)(128)(2,1)} %param.21) | copy-start | bytes 286
  137.3 8.7 %collective-permute-start.3 = (bf16[4,800,128]{2,1,0:T(8,128)(2,1)S(1)}, bf16[4,800,128]{2,1,0:T(8,128)(2,1)S(1)}, u32[]{:S(2)}, u32[]{:S(2)}) collective-permute-start(bf16[4,800,128]{2,1,0:T(8,128)(2,1)S(1)} %all_to_all.37.own), channel_id=1, source_target_pairs={{0,4},{4,0},{1,5},{5,1},{2,6},{6,2},{3,7},{7,3},{8,12},{12,8},{9,1... | collective-permute-start | bytes 2457608 | tf_op jit(solution)/shard_map/ppermute | solution.py:387
  140.0 22.9 %all-to-all-start.6 = ((f32[32,16,128]{2,1,0:T(8,128)}), f32[32,16,128]{2,1,0:T(8,128)S(1)}, u32[]{:S(2)}, u32[]{:S(2)}) async-start(f32[32,16,128]{2,1,0:T(8,128)} %shard_map.174), calls=%async_computation.6 | async-start | bytes 524288 | tf_op jit(solution)/shard_map/all_to_all | solution.py:391
  147.1 16.5 %collective-permute-start.4 = (f32[48,128]{1,0:T(8,128)S(1)}, f32[48,128]{1,0:T(8,128)S(1)}, u32[]{:S(2)}, u32[]{:S(2)}) collective-permute-start(f32[48,128]{1,0:T(8,128)S(1)} %shard_map.172.own), channel_id=1, source_target_pairs={{1,0},{2,1},{3,2},{0,3},{5,4},{6,5},{7,6},{4,7},{9,8},{10,9},{11,1... | collective-permute-start | bytes 73736 | tf_op jit(solution)/shard_map/ppermute | solution.py:399
  149.0 14.6 %collective-permute-start.5 = (f32[48,128]{1,0:T(8,128)S(1)}, f32[48,128]{1,0:T(8,128)S(1)}, u32[]{:S(2)}, u32[]{:S(2)}) collective-permute-start(f32[48,128]{1,0:T(8,128)S(1)} %shard_map.172.own), channel_id=1, source_target_pairs={{2,0},{3,1},{0,2},{1,3},{6,4},{7,5},{4,6},{5,7},{10,8},{11,9},{8,1... | collective-permute-start | bytes 73736 | tf_op jit(solution)/shard_map/ppermute | solution.py:399
  155.5 8.1 %collective-permute-start.6 = (f32[48,128]{1,0:T(8,128)S(1)}, f32[48,128]{1,0:T(8,128)S(1)}, u32[]{:S(2)}, u32[]{:S(2)}) collective-permute-start(f32[48,128]{1,0:T(8,128)S(1)} %shard_map.172.own), channel_id=1, source_target_pairs={{3,0},{0,1},{1,2},{2,3},{7,4},{4,5},{5,6},{6,7},{11,8},{8,9},{9,10... | collective-permute-start | bytes 73736 | tf_op jit(solution)/shard_map/ppermute | solution.py:399
Sparse Core Ops, SparseCore 0:
  35.3 38.3 all-gather.1

commit v6 on v4

--- a/solution.py
+++ b/solution.py
@@ -350,11 +350,11 @@
         [VMEM] * 2,
     )(mine, lax.ppermute(other, "core", swap))
     back = lax.all_to_all(back.reshape(plane, halves_n * WIDE, EDGE), PLANE, 0, 0, tiled=True)
-    near, back = lax.optimization_barrier((near, back))
-    far = lax.ppermute(near, "core", swap)
     half = jax.ShapeDtypeStruct((WIDE, EDGE), F32)
     keep, give = call(plane_sum_kernel, (half, half), [SMEM, VMEM])(side, back)
+    near, give = lax.optimization_barrier((near, give))
     came = lax.ppermute(give, "yh", swap)
+    far = lax.ppermute(near, "core", swap)
 
     shape = (column, plane, part, EDGE)
     total = call(

time: 174 us -> 174 us (level)
  the two profiles are of different devices: /device:TPU:17 before, /device:TPU:48 now
where the time goes in v6:
time: 174 us; the launch traced here: 173 us
  starting transfers between devices  52.5 us (30%)
  blocking collectives  46.4 us (27%)
  waiting for transfers between devices  44.2 us (25%)
  between operations  14.3 us (8%)
  Pallas kernels  12.5 us (7%)
  local copies, waits for them, and re-layouts  3.23 us (2%)
    all_to_all x1, waiting for transfers between devices, per_device(): lax.all_to_all(back.reshape(plane, halves_n * WIDE, EDGE), PLANE, 0, 0, t...  22.9 us
    all_to_all x1, blocking collectives, per_device(): relay = lax.all_to_all(send, SHEET, 0, 0, tiled=True)  21 us
    all_to_all x1, starting transfers between devices, per_device(): quarters = lax.all_to_all(quarters, PLANE, 0, 0, tiled=True)  13.2 us
    all_to_all x1, blocking collectives, per_device(): near_two = lax.all_to_all(relay, 'x', 0, 0, tiled=True)  12.8 us
    all_to_all x1, blocking collectives, per_device(): parts = lax.all_to_all(parts, 'yl', 0, 0, tiled=True)  12.5 us
    all_to_all x1, starting transfers between devices, per_device(): grads = lax.all_to_all(grads, SHEET + ('core',), 0, 0, tiled=True)  10.3 us
    ppermute x3, starting transfers between devices, per_device(): lax.ppermute(second, 'yl', [((i + k) % n_repl, i) for i in range(n_repl)])  9.8 us
    all_to_all x1, waiting for transfers between devices, per_device(): quarters = lax.all_to_all(quarters, PLANE, 0, 0, tiled=True)  9.2 us
  transfers between devices with their start and end apart: 12, of which 8 were waited for; matrix products, arithmetic and copies ran while one was open for 0% of the time, Pallas kernels for 6%

profile of v6, /device:TPU:48, one launch (start us, length us, event | category | flops | bytes accessed | tf_op | source)
XLA Modules:
  0.0 173.1 jit_solution(7773032798744651248)
XLA Ops:
  8.8 13.2 %all-to-all-start = ((bf16[32,32,128]{2,1,0:T(8,128)(2,1)}), bf16[32,32,128]{2,1,0:T(8,128)(2,1)S(1)}, u32[]{:S(2)}, u32[]{:S(2)}) async-start(bf16[32,32,128]{2,1,0:T(8,128)(2,1)} %shard_map.162), calls=%async_computation | async-start | bytes 524288 | tf_op jit(solution)/shard_map/all_to_all | solution.py:301
  22.1 3.2 %shard_map.163 = bf16[4,192,128]{2,1,0:T(8,128)(2,1)} custom-call(s32[32]{0:T(128)} %blocks.9, s32[32,128,128]{2,1,0:T(8,128)} %counts.3, bf16[64,128]{1,0:T(8,128)(2,1)} %bitcast.25, bf16[64,128]{1,0:T(8,128)(2,1)} %bitcast.26, bf16[47,64]{1,0:T(8,128)(2,1)} %bitcast.27, bf16[47,64]{1,0:T(8,128)(2,1)} %bitcast.28, bf16[1,64]{1,0:T(2,128)(2,1)} %bitcast.29), custom_call_target="tpu_custom_call" | custom-call | tf_op jit(solution)/shard_map/pallas_call | solution.py:303
  25.3 9.2 %all-to-all-done = bf16[32,32,128]{2,1,0:T(8,128)(2,1)S(1)} async-done(((bf16[32,32,128]{2,1,0:T(8,128)(2,1)}), bf16[32,32,128]{2,1,0:T(8,128)(2,1)S(1)}, u32[]{:S(2)}, u32[]{:S(2)}) %all-to-all-start) | async-done | bytes 262176 | tf_op jit(solution)/shard_map/all_to_all | solution.py:301
  35.2 5.5 %all-to-all-start.1 = ((bf16[4,192,128]{2,1,0:T(8,128)(2,1)}), bf16[4,192,128]{2,1,0:T(8,128)(2,1)S(1)}, u32[]{:S(2)}, u32[]{:S(2)}) async-start(bf16[4,192,128]{2,1,0:T(8,128)(2,1)} %shard_map.163), calls=%async_computation.1 | async-start | bytes 393216 | tf_op jit(solution)/shard_map/all_to_all | solution.py:330
  41.5 3.4 %all-to-all-done.1.got = bf16[4,192,128]{2,1,0:T(8,128)(2,1)S(1)} async-done(((bf16[4,192,128]{2,1,0:T(8,128)(2,1)}), bf16[4,192,128]{2,1,0:T(8,128)(2,1)S(1)}, u32[]{:S(2)}, u32[]{:S(2)}) %all-to-all-start.1) | async-done | bytes 196640 | tf_op jit(solution)/shard_map/all_to_all | solution.py:330
  44.9 1.2 shard_map.165
  46.2 1.9 %collective-permute-start = (bf16[64,48,128]{2,1,0:T(8,128)(2,1)S(1)}, bf16[64,48,128]{2,1,0:T(8,128)(2,1)S(1)}, u32[]{:S(2)}, u32[]{:S(2)}) collective-permute-start(bf16[64,48,128]{2,1,0:T(8,128)(2,1)S(1)} %get-tuple-element.28), channel_id=1, source_target_pairs={{0,4},{4,0},{1,5},{5,1},{2,6},{6,2},{3,7},{7,3},{8,12},{12,8},{9,1... | collective-permute-start | bytes 2359304 | tf_op jit(solution)/shard_map/ppermute | solution.py:351
  48.1 2.3 %collective-permute-done.other = bf16[64,48,128]{2,1,0:T(8,128)(2,1)S(1)} collective-permute-done((bf16[64,48,128]{2,1,0:T(8,128)(2,1)S(1)}, bf16[64,48,128]{2,1,0:T(8,128)(2,1)S(1)}, u32[]{:S(2)}, u32[]{:S(2)}) %collective-permute-start) | collective-permute-done | bytes 786464 | tf_op jit(solution)/shard_map/ppermute | solution.py:351
  51.5 4.4 %all-to-all-start.2 = ((bf16[32,96,128]{2,1,0:T(8,128)(2,1)}), bf16[32,96,128]{2,1,0:T(8,128)(2,1)S(1)}, u32[]{:S(2)}, u32[]{:S(2)}) async-start(bf16[32,96,128]{2,1,0:T(8,128)(2,1)} %bitcast.10), calls=%async_computation.2 | async-start | bytes 1572864 | tf_op jit(solution)/shard_map/all_to_all | solution.py:352
  55.9 22.9 %all-to-all-done.2.got = bf16[32,96,128]{2,1,0:T(8,128)(2,1)S(1)} async-done(((bf16[32,96,128]{2,1,0:T(8,128)(2,1)}), bf16[32,96,128]{2,1,0:T(8,128)(2,1)S(1)}, u32[]{:S(2)}, u32[]{:S(2)}) %all-to-all-start.2) | async-done | bytes 786464 | tf_op jit(solution)/shard_map/all_to_all | solution.py:352
  78.9 1.9 %collective-permute-start.1 = (bf16[8192,128]{1,0:T(8,128)(2,1)}, bf16[8192,128]{1,0:T(8,128)(2,1)S(1)}, u32[]{:S(2)}, u32[]{:S(2)}) collective-permute-start(bf16[8192,128]{1,0:T(8,128)(2,1)} %all-gather.2.cloned.1.call-done), channel_id=1, source_target_pairs={{0,4},{4,0},{1,5},{5,1},{2,6},{6,2},{3,7},{7,3},{8,12},{12,8},{9,1... | collective-permute-start | bytes 6291464 | tf_op jit(solution)/shard_map/ppermute | solution.py:357
  80.8 3.5 %collective-permute-start.2 = (f32[48,128]{1,0:T(8,128)S(1)}, f32[48,128]{1,0:T(8,128)S(1)}, u32[]{:S(2)}, u32[]{:S(2)}) collective-permute-start(f32[48,128]{1,0:T(8,128)S(1)} %get-tuple-element.32), channel_id=1, source_target_pairs={{0,8},{8,0},{1,9},{9,1},{2,10},{10,2},{3,11},{11,3},{4,12},{12,4},... | collective-permute-start | bytes 73736 | tf_op jit(solution)/shard_map/ppermute | solution.py:356
  85.2 1.6 copy-done.1
  87.9 2.6 %collective-permute-done.2.came = f32[48,128]{1,0:T(8,128)S(1)} collective-permute-done((f32[48,128]{1,0:T(8,128)S(1)}, f32[48,128]{1,0:T(8,128)S(1)}, u32[]{:S(2)}, u32[]{:S(2)}) %collective-permute-start.2) | collective-permute-done | bytes 24608 | tf_op jit(solution)/shard_map/ppermute | solution.py:356
  90.5 12.5 %all_to_all.35.parts = bf16[4,304,128]{2,1,0:T(8,128)(2,1)S(1)} all-to-all(bf16[4,304,128]{2,1,0:T(8,128)(2,1)S(1)} %shard_map.169), channel_id=1, replica_groups=mesh['x'=4,'z'=8,'yh'=2,'core'=2,'yl'=4] {'yl'}, dimensions={0} | all-to-all | bytes 622592 | tf_op jit(solution)/shard_map/all_to_all | solution.py:369
  104.0 21.0 %all_to_all.36.got = bf16[16,80,128]{2,1,0:T(8,128)(2,1)S(1)} all-to-all(bf16[16,80,128]{2,1,0:T(8,128)(2,1)S(1)} %get-tuple-element.35), channel_id=1, replica_groups=mesh['x'=4,'z'=8,'yh'=2,'core'=2,'yl'=4] {'z','yh'}, dimensions={0} | all-to-all | bytes 655360 | tf_op jit(solution)/shard_map/all_to_all | solution.py:380
  125.2 12.8 %all_to_all.37.own = bf16[4,800,128]{2,1,0:T(8,128)(2,1)S(1)} all-to-all(bf16[4,800,128]{2,1,0:T(8,128)(2,1)S(1)} %shard_map.171), channel_id=1, replica_groups=mesh['x'=4,'z'=8,'yh'=2,'core'=2,'yl'=4] {'x'}, dimensions={0} | all-to-all | bytes 1638400 | tf_op jit(solution)/shard_map/all_to_all | solution.py:386
  138.0 1.9 %collective-permute-start.3 = (bf16[4,800,128]{2,1,0:T(8,128)(2,1)S(1)}, bf16[4,800,128]{2,1,0:T(8,128)(2,1)S(1)}, u32[]{:S(2)}, u32[]{:S(2)}) collective-permute-start(bf16[4,800,128]{2,1,0:T(8,128)(2,1)S(1)} %all_to_all.37.own), channel_id=1, source_target_pairs={{0,4},{4,0},{1,5},{5,1},{2,6},{6,2},{3,7},{7,3},{8,12},{12,8},{9,1... | collective-permute-start | bytes 2457608 | tf_op jit(solution)/shard_map/ppermute | solution.py:387
  140.6 10.3 %all-to-all-start.6 = ((f32[32,16,128]{2,1,0:T(8,128)}), f32[32,16,128]{2,1,0:T(8,128)S(1)}, u32[]{:S(2)}, u32[]{:S(2)}) async-start(f32[32,16,128]{2,1,0:T(8,128)} %shard_map.174), calls=%async_computation.6 | async-start | bytes 524288 | tf_op jit(solution)/shard_map/all_to_all | solution.py:391
  152.0 1.9 %collective-permute-start.4 = (f32[48,128]{1,0:T(8,128)S(1)}, f32[48,128]{1,0:T(8,128)S(1)}, u32[]{:S(2)}, u32[]{:S(2)}) collective-permute-start(f32[48,128]{1,0:T(8,128)S(1)} %shard_map.172.own), channel_id=1, source_target_pairs={{1,0},{2,1},{3,2},{0,3},{5,4},{6,5},{7,6},{4,7},{9,8},{10,9},{11,1... | collective-permute-start | bytes 73736 | tf_op jit(solution)/shard_map/ppermute | solution.py:399
  154.0 6.0 %collective-permute-start.5 = (f32[48,128]{1,0:T(8,128)S(1)}, f32[48,128]{1,0:T(8,128)S(1)}, u32[]{:S(2)}, u32[]{:S(2)}) collective-permute-start(f32[48,128]{1,0:T(8,128)S(1)} %shard_map.172.own), channel_id=1, source_target_pairs={{2,0},{3,1},{0,2},{1,3},{6,4},{7,5},{4,6},{5,7},{10,8},{11,9},{8,1... | collective-permute-start | bytes 73736 | tf_op jit(solution)/shard_map/ppermute | solution.py:399
  159.9 1.9 %collective-permute-start.6 = (f32[48,128]{1,0:T(8,128)S(1)}, f32[48,128]{1,0:T(8,128)S(1)}, u32[]{:S(2)}, u32[]{:S(2)}) collective-permute-start(f32[48,128]{1,0:T(8,128)S(1)} %shard_map.172.own), channel_id=1, source_target_pairs={{3,0},{0,1},{1,2},{2,3},{7,4},{4,5},{5,6},{6,7},{11,8},{8,9},{9,10... | collective-permute-start | bytes 73736 | tf_op jit(solution)/shard_map/ppermute | solution.py:399
  161.8 1.1 all-to-all-done.6.got
  163.7 2.0 %collective-permute-done.6.third = f32[48,128]{1,0:T(8,128)S(1)} collective-permute-done((f32[48,128]{1,0:T(8,128)S(1)}, f32[48,128]{1,0:T(8,128)S(1)}, u32[]{:S(2)}, u32[]{:S(2)}) %collective-permute-start.6) | collective-permute-done | bytes 24608 | tf_op jit(solution)/shard_map/ppermute | solution.py:399
  (38 shorter events, 10.6 us)
Async XLA Ops:
  7.2 33.5 %copy-start = (s32[32,128,128]{2,1,0:T(8,128)S(1)}, s32[32,128,128]{2,1,0:T(8,128)}, u32[]{:S(2)}) copy-start(s32[32,128,128]{2,1,0:T(8,128)} %counts.3) | copy-start | bytes 6291460
  7.2 0.9 copy-start.2
  8.1 32.6 %copy-start.4 = (s32[32]{0:T(128)S(1)}, s32[32]{0:T(128)}, u32[]{:S(2)}) copy-start(s32[32]{0:T(128)} %blocks.9) | copy-start | bytes 388
  8.8 25.6 %all-to-all-start = ((bf16[32,32,128]{2,1,0:T(8,128)(2,1)}), bf16[32,32,128]{2,1,0:T(8,128)(2,1)S(1)}, u32[]{:S(2)}, u32[]{:S(2)}) async-start(bf16[32,32,128]{2,1,0:T(8,128)(2,1)} %shard_map.162), calls=%async_computation | async-start | bytes 524288 | tf_op jit(solution)/shard_map/all_to_all | solution.py:301
  22.0 56.9 %all-gather.2.cloned.1.call-start = ((), (), s32[]{:S(2)}) async-start(), calls=%async_computation.7 | async-start | bytes 2359296 | tf_op jit(solution)/shard_map/all_gather | solution.py:329
  25.2 16.3 %copy-start.8 = (bf16[47,128]{1,0:T(8,128)(2,1)S(1)}, bf16[47,128]{1,0:T(8,128)(2,1)}, u32[]{:S(2)}) copy-start(bf16[47,128]{1,0:T(8,128)(2,1)} %param.15) | copy-start | bytes 36100
  25.2 19.7 %copy-start.5 = (s32[128]{0:T(128)S(1)}, s32[128]{0:T(128)}, u32[]{:S(2)}) copy-start(s32[128]{0:T(128)} %param.14) | copy-start | bytes 1540
  34.5 0.7 copy-start.7
  35.2 9.7 %all-to-all-start.1 = ((bf16[4,192,128]{2,1,0:T(8,128)(2,1)}), bf16[4,192,128]{2,1,0:T(8,128)(2,1)S(1)}, u32[]{:S(2)}, u32[]{:S(2)}) async-start(bf16[4,192,128]{2,1,0:T(8,128)(2,1)} %shard_map.163), calls=%async_computation.1 | async-start | bytes 393216 | tf_op jit(solution)/shard_map/all_to_all | solution.py:330
  46.2 4.2 %collective-permute-start = (bf16[64,48,128]{2,1,0:T(8,128)(2,1)S(1)}, bf16[64,48,128]{2,1,0:T(8,128)(2,1)S(1)}, u32[]{:S(2)}, u32[]{:S(2)}) collective-permute-start(bf16[64,48,128]{2,1,0:T(8,128)(2,1)S(1)} %get-tuple-element.28), channel_id=1, source_target_pairs={{0,4},{4,0},{1,5},{5,1},{2,6},{6,2},{3,7},{7,3},{8,12},{12,8},{9,1... | collective-permute-start | bytes 2359304 | tf_op jit(solution)/shard_map/ppermute | solution.py:351
  51.5 27.3 %all-to-all-start.2 = ((bf16[32,96,128]{2,1,0:T(8,128)(2,1)}), bf16[32,96,128]{2,1,0:T(8,128)(2,1)S(1)}, u32[]{:S(2)}, u32[]{:S(2)}) async-start(bf16[32,96,128]{2,1,0:T(8,128)(2,1)} %bitcast.10), calls=%async_computation.2 | async-start | bytes 1572864 | tf_op jit(solution)/shard_map/all_to_all | solution.py:352
  78.9 6.3 %collective-permute-start.1 = (bf16[8192,128]{1,0:T(8,128)(2,1)}, bf16[8192,128]{1,0:T(8,128)(2,1)S(1)}, u32[]{:S(2)}, u32[]{:S(2)}) collective-permute-start(bf16[8192,128]{1,0:T(8,128)(2,1)} %all-gather.2.cloned.1.call-done), channel_id=1, source_target_pairs={{0,4},{4,0},{1,5},{5,1},{2,6},{6,2},{3,7},{7,3},{8,12},{12,8},{9,1... | collective-permute-start | bytes 6291464 | tf_op jit(solution)/shard_map/ppermute | solution.py:357
  80.8 9.6 %collective-permute-start.2 = (f32[48,128]{1,0:T(8,128)S(1)}, f32[48,128]{1,0:T(8,128)S(1)}, u32[]{:S(2)}, u32[]{:S(2)}) collective-permute-start(f32[48,128]{1,0:T(8,128)S(1)} %get-tuple-element.32), channel_id=1, source_target_pairs={{0,8},{8,0},{1,9},{9,1},{2,10},{10,2},{3,11},{11,3},{4,12},{12,4},... | collective-permute-start | bytes 73736 | tf_op jit(solution)/shard_map/ppermute | solution.py:356
  85.2 1.6 copy-start.1
  86.7 16.3 %copy-start.3 = (bf16[128,128]{1,0:T(8,128)(2,1)S(1)}, bf16[128,128]{1,0:T(8,128)(2,1)}, u32[]{:S(2)}) copy-start(bf16[128,128]{1,0:T(8,128)(2,1)} %features.3) | copy-start | bytes 98308
  86.7 16.3 %copy-start.6 = (bf16[47]{0:T(256)(128)(2,1)S(1)}, bf16[47]{0:T(256)(128)(2,1)}, u32[]{:S(2)}) copy-start(bf16[47]{0:T(256)(128)(2,1)} %param.21) | copy-start | bytes 286
  138.0 13.0 %collective-permute-start.3 = (bf16[4,800,128]{2,1,0:T(8,128)(2,1)S(1)}, bf16[4,800,128]{2,1,0:T(8,128)(2,1)S(1)}, u32[]{:S(2)}, u32[]{:S(2)}) collective-permute-start(bf16[4,800,128]{2,1,0:T(8,128)(2,1)S(1)} %all_to_all.37.own), channel_id=1, source_target_pairs={{0,4},{4,0},{1,5},{5,1},{2,6},{6,2},{3,7},{7,3},{8,12},{12,8},{9,1... | collective-permute-start | bytes 2457608 | tf_op jit(solution)/shard_map/ppermute | solution.py:387
  140.6 22.3 %all-to-all-start.6 = ((f32[32,16,128]{2,1,0:T(8,128)}), f32[32,16,128]{2,1,0:T(8,128)S(1)}, u32[]{:S(2)}, u32[]{:S(2)}) async-start(f32[32,16,128]{2,1,0:T(8,128)} %shard_map.174), calls=%async_computation.6 | async-start | bytes 524288 | tf_op jit(solution)/shard_map/all_to_all | solution.py:391
  152.0 11.6 %collective-permute-start.4 = (f32[48,128]{1,0:T(8,128)S(1)}, f32[48,128]{1,0:T(8,128)S(1)}, u32[]{:S(2)}, u32[]{:S(2)}) collective-permute-start(f32[48,128]{1,0:T(8,128)S(1)} %shard_map.172.own), channel_id=1, source_target_pairs={{1,0},{2,1},{3,2},{0,3},{5,4},{6,5},{7,6},{4,7},{9,8},{10,9},{11,1... | collective-permute-start | bytes 73736 | tf_op jit(solution)/shard_map/ppermute | solution.py:399
  154.0 9.7 %collective-permute-start.5 = (f32[48,128]{1,0:T(8,128)S(1)}, f32[48,128]{1,0:T(8,128)S(1)}, u32[]{:S(2)}, u32[]{:S(2)}) collective-permute-start(f32[48,128]{1,0:T(8,128)S(1)} %shard_map.172.own), channel_id=1, source_target_pairs={{2,0},{3,1},{0,2},{1,3},{6,4},{7,5},{4,6},{5,7},{10,8},{11,9},{8,1... | collective-permute-start | bytes 73736 | tf_op jit(solution)/shard_map/ppermute | solution.py:399
  159.9 5.7 %collective-permute-start.6 = (f32[48,128]{1,0:T(8,128)S(1)}, f32[48,128]{1,0:T(8,128)S(1)}, u32[]{:S(2)}, u32[]{:S(2)}) collective-permute-start(f32[48,128]{1,0:T(8,128)S(1)} %shard_map.172.own), channel_id=1, source_target_pairs={{3,0},{0,1},{1,2},{2,3},{7,4},{4,5},{5,6},{6,7},{11,8},{8,9},{9,10... | collective-permute-start | bytes 73736 | tf_op jit(solution)/shard_map/ppermute | solution.py:399
Sparse Core Ops, SparseCore 0:
  35.3 37.2 all-gather.1

commit v7 on v6

--- a/solution.py
+++ b/solution.py
@@ -352,9 +352,9 @@
     back = lax.all_to_all(back.reshape(plane, halves_n * WIDE, EDGE), PLANE, 0, 0, tiled=True)
     half = jax.ShapeDtypeStruct((WIDE, EDGE), F32)
     keep, give = call(plane_sum_kernel, (half, half), [SMEM, VMEM])(side, back)
-    near, give = lax.optimization_barrier((near, give))
+    late, give = lax.optimization_barrier((near, give))
     came = lax.ppermute(give, "yh", swap)
-    far = lax.ppermute(near, "core", swap)
+    far = lax.ppermute(late, "core", swap)
 
     shape = (column, plane, part, EDGE)
     total = call(

time: 174 us -> 174 us (level)
  no operation moved by 1% of the time
where the time goes in v7:
time: 174 us; the launch traced here: 173 us
  starting transfers between devices  52.5 us (30%)
  blocking collectives  46.3 us (27%)
  waiting for transfers between devices  44.2 us (25%)
  between operations  14.3 us (8%)
  Pallas kernels  12.5 us (7%)
  local copies, waits for them, and re-layouts  3.23 us (2%)
    all_to_all x1, waiting for transfers between devices, per_device(): lax.all_to_all(back.reshape(plane, halves_n * WIDE, EDGE), PLANE, 0, 0, t...  22.9 us
    all_to_all x1, blocking collectives, per_device(): relay = lax.all_to_all(send, SHEET, 0, 0, tiled=True)  21.1 us
    all_to_all x1, starting transfers between devices, per_device(): quarters = lax.all_to_all(quarters, PLANE, 0, 0, tiled=True)  13.2 us
    all_to_all x1, blocking collectives, per_device(): near_two = lax.all_to_all(relay, 'x', 0, 0, tiled=True)  12.7 us
    all_to_all x1, blocking collectives, per_device(): parts = lax.all_to_all(parts, 'yl', 0, 0, tiled=True)  12.5 us
    all_to_all x1, starting transfers between devices, per_device(): grads = lax.all_to_all(grads, SHEET + ('core',), 0, 0, tiled=True)  10.3 us
    ppermute x3, starting transfers between devices, per_device(): lax.ppermute(second, 'yl', [((i + k) % n_repl, i) for i in range(n_repl)])  9.82 us
    all_to_all x1, waiting for transfers between devices, per_device(): quarters = lax.all_to_all(quarters, PLANE, 0, 0, tiled=True)  9.2 us
  transfers between devices with their start and end apart: 12, of which 8 were waited for; matrix products, arithmetic and copies ran while one was open for 0% of the time, Pallas kernels for 6%

profile of v7, /device:TPU:48, one launch (start us, length us, event | category | flops | bytes accessed | tf_op | source)
XLA Modules:
  0.0 173.1 jit_solution(7773032798744651248)
XLA Ops:
  8.8 13.2 %all-to-all-start = ((bf16[32,32,128]{2,1,0:T(8,128)(2,1)}), bf16[32,32,128]{2,1,0:T(8,128)(2,1)S(1)}, u32[]{:S(2)}, u32[]{:S(2)}) async-start(bf16[32,32,128]{2,1,0:T(8,128)(2,1)} %shard_map.162), calls=%async_computation | async-start | bytes 524288 | tf_op jit(solution)/shard_map/all_to_all | solution.py:301
  22.1 3.2 %shard_map.163 = bf16[4,192,128]{2,1,0:T(8,128)(2,1)} custom-call(s32[32]{0:T(128)} %blocks.9, s32[32,128,128]{2,1,0:T(8,128)} %counts.3, bf16[64,128]{1,0:T(8,128)(2,1)} %bitcast.25, bf16[64,128]{1,0:T(8,128)(2,1)} %bitcast.26, bf16[47,64]{1,0:T(8,128)(2,1)} %bitcast.27, bf16[47,64]{1,0:T(8,128)(2,1)} %bitcast.28, bf16[1,64]{1,0:T(2,128)(2,1)} %bitcast.29), custom_call_target="tpu_custom_call" | custom-call | tf_op jit(solution)/shard_map/pallas_call | solution.py:303
  25.3 9.2 %all-to-all-done = bf16[32,32,128]{2,1,0:T(8,128)(2,1)S(1)} async-done(((bf16[32,32,128]{2,1,0:T(8,128)(2,1)}), bf16[32,32,128]{2,1,0:T(8,128)(2,1)S(1)}, u32[]{:S(2)}, u32[]{:S(2)}) %all-to-all-start) | async-done | bytes 262176 | tf_op jit(solution)/shard_map/all_to_all | solution.py:301
  35.2 5.5 %all-to-all-start.1 = ((bf16[4,192,128]{2,1,0:T(8,128)(2,1)}), bf16[4,192,128]{2,1,0:T(8,128)(2,1)S(1)}, u32[]{:S(2)}, u32[]{:S(2)}) async-start(bf16[4,192,128]{2,1,0:T(8,128)(2,1)} %shard_map.163), calls=%async_computation.1 | async-start | bytes 393216 | tf_op jit(solution)/shard_map/all_to_all | solution.py:330
  41.5 3.4 %all-to-all-done.1.got = bf16[4,192,128]{2,1,0:T(8,128)(2,1)S(1)} async-done(((bf16[4,192,128]{2,1,0:T(8,128)(2,1)}), bf16[4,192,128]{2,1,0:T(8,128)(2,1)S(1)}, u32[]{:S(2)}, u32[]{:S(2)}) %all-to-all-start.1) | async-done | bytes 196640 | tf_op jit(solution)/shard_map/all_to_all | solution.py:330
  44.9 1.2 shard_map.165
  46.2 1.9 %collective-permute-start = (bf16[64,48,128]{2,1,0:T(8,128)(2,1)S(1)}, bf16[64,48,128]{2,1,0:T(8,128)(2,1)S(1)}, u32[]{:S(2)}, u32[]{:S(2)}) collective-permute-start(bf16[64,48,128]{2,1,0:T(8,128)(2,1)S(1)} %get-tuple-element.28), channel_id=1, source_target_pairs={{0,4},{4,0},{1,5},{5,1},{2,6},{6,2},{3,7},{7,3},{8,12},{12,8},{9,1... | collective-permute-start | bytes 2359304 | tf_op jit(solution)/shard_map/ppermute | solution.py:351
  48.1 2.3 %collective-permute-done.other = bf16[64,48,128]{2,1,0:T(8,128)(2,1)S(1)} collective-permute-done((bf16[64,48,128]{2,1,0:T(8,128)(2,1)S(1)}, bf16[64,48,128]{2,1,0:T(8,128)(2,1)S(1)}, u32[]{:S(2)}, u32[]{:S(2)}) %collective-permute-start) | collective-permute-done | bytes 786464 | tf_op jit(solution)/shard_map/ppermute | solution.py:351
  51.5 4.4 %all-to-all-start.2 = ((bf16[32,96,128]{2,1,0:T(8,128)(2,1)}), bf16[32,96,128]{2,1,0:T(8,128)(2,1)S(1)}, u32[]{:S(2)}, u32[]{:S(2)}) async-start(bf16[32,96,128]{2,1,0:T(8,128)(2,1)} %bitcast.11), calls=%async_computation.2 | async-start | bytes 1572864 | tf_op jit(solution)/shard_map/all_to_all | solution.py:352
  55.9 22.9 %all-to-all-done.2.got = bf16[32,96,128]{2,1,0:T(8,128)(2,1)S(1)} async-done(((bf16[32,96,128]{2,1,0:T(8,128)(2,1)}), bf16[32,96,128]{2,1,0:T(8,128)(2,1)S(1)}, u32[]{:S(2)}, u32[]{:S(2)}) %all-to-all-start.2) | async-done | bytes 786464 | tf_op jit(solution)/shard_map/all_to_all | solution.py:352
  78.9 1.9 %collective-permute-start.1 = (bf16[8192,128]{1,0:T(8,128)(2,1)}, bf16[8192,128]{1,0:T(8,128)(2,1)S(1)}, u32[]{:S(2)}, u32[]{:S(2)}) collective-permute-start(bf16[8192,128]{1,0:T(8,128)(2,1)} %all-gather.2.cloned.1.call-done), channel_id=1, source_target_pairs={{0,4},{4,0},{1,5},{5,1},{2,6},{6,2},{3,7},{7,3},{8,12},{12,8},{9,1... | collective-permute-start | bytes 6291464 | tf_op jit(solution)/shard_map/ppermute | solution.py:357
  80.8 3.6 %collective-permute-start.2 = (f32[48,128]{1,0:T(8,128)S(1)}, f32[48,128]{1,0:T(8,128)S(1)}, u32[]{:S(2)}, u32[]{:S(2)}) collective-permute-start(f32[48,128]{1,0:T(8,128)S(1)} %get-tuple-element.32), channel_id=1, source_target_pairs={{0,8},{8,0},{1,9},{9,1},{2,10},{10,2},{3,11},{11,3},{4,12},{12,4},... | collective-permute-start | bytes 73736 | tf_op jit(solution)/shard_map/ppermute | solution.py:356
  85.2 1.6 copy-done.1
  87.8 2.6 %collective-permute-done.2.came = f32[48,128]{1,0:T(8,128)S(1)} collective-permute-done((f32[48,128]{1,0:T(8,128)S(1)}, f32[48,128]{1,0:T(8,128)S(1)}, u32[]{:S(2)}, u32[]{:S(2)}) %collective-permute-start.2) | collective-permute-done | bytes 24608 | tf_op jit(solution)/shard_map/ppermute | solution.py:356
  90.5 12.5 %all_to_all.35.parts = bf16[4,304,128]{2,1,0:T(8,128)(2,1)S(1)} all-to-all(bf16[4,304,128]{2,1,0:T(8,128)(2,1)S(1)} %shard_map.169), channel_id=1, replica_groups=mesh['x'=4,'z'=8,'yh'=2,'core'=2,'yl'=4] {'yl'}, dimensions={0} | all-to-all | bytes 622592 | tf_op jit(solution)/shard_map/all_to_all | solution.py:369
  104.0 21.1 %all_to_all.36.got = bf16[16,80,128]{2,1,0:T(8,128)(2,1)S(1)} all-to-all(bf16[16,80,128]{2,1,0:T(8,128)(2,1)S(1)} %get-tuple-element.35), channel_id=1, replica_groups=mesh['x'=4,'z'=8,'yh'=2,'core'=2,'yl'=4] {'z','yh'}, dimensions={0} | all-to-all | bytes 655360 | tf_op jit(solution)/shard_map/all_to_all | solution.py:380
  125.2 12.7 %all_to_all.37.own = bf16[4,800,128]{2,1,0:T(8,128)(2,1)S(1)} all-to-all(bf16[4,800,128]{2,1,0:T(8,128)(2,1)S(1)} %shard_map.171), channel_id=1, replica_groups=mesh['x'=4,'z'=8,'yh'=2,'core'=2,'yl'=4] {'x'}, dimensions={0} | all-to-all | bytes 1638400 | tf_op jit(solution)/shard_map/all_to_all | solution.py:386
  138.0 1.9 %collective-permute-start.3 = (bf16[4,800,128]{2,1,0:T(8,128)(2,1)S(1)}, bf16[4,800,128]{2,1,0:T(8,128)(2,1)S(1)}, u32[]{:S(2)}, u32[]{:S(2)}) collective-permute-start(bf16[4,800,128]{2,1,0:T(8,128)(2,1)S(1)} %all_to_all.37.own), channel_id=1, source_target_pairs={{0,4},{4,0},{1,5},{5,1},{2,6},{6,2},{3,7},{7,3},{8,12},{12,8},{9,1... | collective-permute-start | bytes 2457608 | tf_op jit(solution)/shard_map/ppermute | solution.py:387
  140.6 10.3 %all-to-all-start.6 = ((f32[32,16,128]{2,1,0:T(8,128)}), f32[32,16,128]{2,1,0:T(8,128)S(1)}, u32[]{:S(2)}, u32[]{:S(2)}) async-start(f32[32,16,128]{2,1,0:T(8,128)} %shard_map.174), calls=%async_computation.6 | async-start | bytes 524288 | tf_op jit(solution)/shard_map/all_to_all | solution.py:391
  152.0 1.9 %collective-permute-start.4 = (f32[48,128]{1,0:T(8,128)S(1)}, f32[48,128]{1,0:T(8,128)S(1)}, u32[]{:S(2)}, u32[]{:S(2)}) collective-permute-start(f32[48,128]{1,0:T(8,128)S(1)} %shard_map.172.own), channel_id=1, source_target_pairs={{1,0},{2,1},{3,2},{0,3},{5,4},{6,5},{7,6},{4,7},{9,8},{10,9},{11,1... | collective-permute-start | bytes 73736 | tf_op jit(solution)/shard_map/ppermute | solution.py:399
  153.9 6.0 %collective-permute-start.5 = (f32[48,128]{1,0:T(8,128)S(1)}, f32[48,128]{1,0:T(8,128)S(1)}, u32[]{:S(2)}, u32[]{:S(2)}) collective-permute-start(f32[48,128]{1,0:T(8,128)S(1)} %shard_map.172.own), channel_id=1, source_target_pairs={{2,0},{3,1},{0,2},{1,3},{6,4},{7,5},{4,6},{5,7},{10,8},{11,9},{8,1... | collective-permute-start | bytes 73736 | tf_op jit(solution)/shard_map/ppermute | solution.py:399
  159.9 1.9 %collective-permute-start.6 = (f32[48,128]{1,0:T(8,128)S(1)}, f32[48,128]{1,0:T(8,128)S(1)}, u32[]{:S(2)}, u32[]{:S(2)}) collective-permute-start(f32[48,128]{1,0:T(8,128)S(1)} %shard_map.172.own), channel_id=1, source_target_pairs={{3,0},{0,1},{1,2},{2,3},{7,4},{4,5},{5,6},{6,7},{11,8},{8,9},{9,10... | collective-permute-start | bytes 73736 | tf_op jit(solution)/shard_map/ppermute | solution.py:399
  161.8 1.1 all-to-all-done.6.got
  163.6 2.0 %collective-permute-done.6.third = f32[48,128]{1,0:T(8,128)S(1)} collective-permute-done((f32[48,128]{1,0:T(8,128)S(1)}, f32[48,128]{1,0:T(8,128)S(1)}, u32[]{:S(2)}, u32[]{:S(2)}) %collective-permute-start.6) | collective-permute-done | bytes 24608 | tf_op jit(solution)/shard_map/ppermute | solution.py:399
  (38 shorter events, 10.6 us)
Async XLA Ops:
  7.2 33.5 %copy-start = (s32[32,128,128]{2,1,0:T(8,128)S(1)}, s32[32,128,128]{2,1,0:T(8,128)}, u32[]{:S(2)}) copy-start(s32[32,128,128]{2,1,0:T(8,128)} %counts.3) | copy-start | bytes 6291460
  7.2 0.9 copy-start.2
  8.1 32.6 %copy-start.4 = (s32[32]{0:T(128)S(1)}, s32[32]{0:T(128)}, u32[]{:S(2)}) copy-start(s32[32]{0:T(128)} %blocks.9) | copy-start | bytes 388
  8.8 25.6 %all-to-all-start = ((bf16[32,32,128]{2,1,0:T(8,128)(2,1)}), bf16[32,32,128]{2,1,0:T(8,128)(2,1)S(1)}, u32[]{:S(2)}, u32[]{:S(2)}) async-start(bf16[32,32,128]{2,1,0:T(8,128)(2,1)} %shard_map.162), calls=%async_computation | async-start | bytes 524288 | tf_op jit(solution)/shard_map/all_to_all | solution.py:301
  22.0 56.9 %all-gather.2.cloned.1.call-start = ((), (), s32[]{:S(2)}) async-start(), calls=%async_computation.7 | async-start | bytes 2359296 | tf_op jit(solution)/shard_map/all_gather | solution.py:329
  25.2 16.3 %copy-start.8 = (bf16[47,128]{1,0:T(8,128)(2,1)S(1)}, bf16[47,128]{1,0:T(8,128)(2,1)}, u32[]{:S(2)}) copy-start(bf16[47,128]{1,0:T(8,128)(2,1)} %param.15) | copy-start | bytes 36100
  25.2 19.7 %copy-start.5 = (s32[128]{0:T(128)S(1)}, s32[128]{0:T(128)}, u32[]{:S(2)}) copy-start(s32[128]{0:T(128)} %param.14) | copy-start | bytes 1540
  34.5 0.7 copy-start.7
  35.2 9.7 %all-to-all-start.1 = ((bf16[4,192,128]{2,1,0:T(8,128)(2,1)}), bf16[4,192,128]{2,1,0:T(8,128)(2,1)S(1)}, u32[]{:S(2)}, u32[]{:S(2)}) async-start(bf16[4,192,128]{2,1,0:T(8,128)(2,1)} %shard_map.163), calls=%async_computation.1 | async-start | bytes 393216 | tf_op jit(solution)/shard_map/all_to_all | solution.py:330
  46.2 4.2 %collective-permute-start = (bf16[64,48,128]{2,1,0:T(8,128)(2,1)S(1)}, bf16[64,48,128]{2,1,0:T(8,128)(2,1)S(1)}, u32[]{:S(2)}, u32[]{:S(2)}) collective-permute-start(bf16[64,48,128]{2,1,0:T(8,128)(2,1)S(1)} %get-tuple-element.28), channel_id=1, source_target_pairs={{0,4},{4,0},{1,5},{5,1},{2,6},{6,2},{3,7},{7,3},{8,12},{12,8},{9,1... | collective-permute-start | bytes 2359304 | tf_op jit(solution)/shard_map/ppermute | solution.py:351
  51.5 27.3 %all-to-all-start.2 = ((bf16[32,96,128]{2,1,0:T(8,128)(2,1)}), bf16[32,96,128]{2,1,0:T(8,128)(2,1)S(1)}, u32[]{:S(2)}, u32[]{:S(2)}) async-start(bf16[32,96,128]{2,1,0:T(8,128)(2,1)} %bitcast.11), calls=%async_computation.2 | async-start | bytes 1572864 | tf_op jit(solution)/shard_map/all_to_all | solution.py:352
  78.9 6.3 %collective-permute-start.1 = (bf16[8192,128]{1,0:T(8,128)(2,1)}, bf16[8192,128]{1,0:T(8,128)(2,1)S(1)}, u32[]{:S(2)}, u32[]{:S(2)}) collective-permute-start(bf16[8192,128]{1,0:T(8,128)(2,1)} %all-gather.2.cloned.1.call-done), channel_id=1, source_target_pairs={{0,4},{4,0},{1,5},{5,1},{2,6},{6,2},{3,7},{7,3},{8,12},{12,8},{9,1... | collective-permute-start | bytes 6291464 | tf_op jit(solution)/shard_map/ppermute | solution.py:357
  80.8 9.6 %collective-permute-start.2 = (f32[48,128]{1,0:T(8,128)S(1)}, f32[48,128]{1,0:T(8,128)S(1)}, u32[]{:S(2)}, u32[]{:S(2)}) collective-permute-start(f32[48,128]{1,0:T(8,128)S(1)} %get-tuple-element.32), channel_id=1, source_target_pairs={{0,8},{8,0},{1,9},{9,1},{2,10},{10,2},{3,11},{11,3},{4,12},{12,4},... | collective-permute-start | bytes 73736 | tf_op jit(solution)/shard_map/ppermute | solution.py:356
  85.2 1.6 copy-start.1
  86.7 16.3 %copy-start.3 = (bf16[128,128]{1,0:T(8,128)(2,1)S(1)}, bf16[128,128]{1,0:T(8,128)(2,1)}, u32[]{:S(2)}) copy-start(bf16[128,128]{1,0:T(8,128)(2,1)} %features.3) | copy-start | bytes 98308
  86.7 16.3 %copy-start.6 = (bf16[47]{0:T(256)(128)(2,1)S(1)}, bf16[47]{0:T(256)(128)(2,1)}, u32[]{:S(2)}) copy-start(bf16[47]{0:T(256)(128)(2,1)} %param.21) | copy-start | bytes 286
  138.0 13.0 %collective-permute-start.3 = (bf16[4,800,128]{2,1,0:T(8,128)(2,1)S(1)}, bf16[4,800,128]{2,1,0:T(8,128)(2,1)S(1)}, u32[]{:S(2)}, u32[]{:S(2)}) collective-permute-start(bf16[4,800,128]{2,1,0:T(8,128)(2,1)S(1)} %all_to_all.37.own), channel_id=1, source_target_pairs={{0,4},{4,0},{1,5},{5,1},{2,6},{6,2},{3,7},{7,3},{8,12},{12,8},{9,1... | collective-permute-start | bytes 2457608 | tf_op jit(solution)/shard_map/ppermute | solution.py:387
  140.6 22.3 %all-to-all-start.6 = ((f32[32,16,128]{2,1,0:T(8,128)}), f32[32,16,128]{2,1,0:T(8,128)S(1)}, u32[]{:S(2)}, u32[]{:S(2)}) async-start(f32[32,16,128]{2,1,0:T(8,128)} %shard_map.174), calls=%async_computation.6 | async-start | bytes 524288 | tf_op jit(solution)/shard_map/all_to_all | solution.py:391
  152.0 11.6 %collective-permute-start.4 = (f32[48,128]{1,0:T(8,128)S(1)}, f32[48,128]{1,0:T(8,128)S(1)}, u32[]{:S(2)}, u32[]{:S(2)}) collective-permute-start(f32[48,128]{1,0:T(8,128)S(1)} %shard_map.172.own), channel_id=1, source_target_pairs={{1,0},{2,1},{3,2},{0,3},{5,4},{6,5},{7,6},{4,7},{9,8},{10,9},{11,1... | collective-permute-start | bytes 73736 | tf_op jit(solution)/shard_map/ppermute | solution.py:399
  153.9 9.7 %collective-permute-start.5 = (f32[48,128]{1,0:T(8,128)S(1)}, f32[48,128]{1,0:T(8,128)S(1)}, u32[]{:S(2)}, u32[]{:S(2)}) collective-permute-start(f32[48,128]{1,0:T(8,128)S(1)} %shard_map.172.own), channel_id=1, source_target_pairs={{2,0},{3,1},{0,2},{1,3},{6,4},{7,5},{4,6},{5,7},{10,8},{11,9},{8,1... | collective-permute-start | bytes 73736 | tf_op jit(solution)/shard_map/ppermute | solution.py:399
  159.9 5.7 %collective-permute-start.6 = (f32[48,128]{1,0:T(8,128)S(1)}, f32[48,128]{1,0:T(8,128)S(1)}, u32[]{:S(2)}, u32[]{:S(2)}) collective-permute-start(f32[48,128]{1,0:T(8,128)S(1)} %shard_map.172.own), channel_id=1, source_target_pairs={{3,0},{0,1},{1,2},{2,3},{7,4},{4,5},{5,6},{6,7},{11,8},{8,9},{9,10... | collective-permute-start | bytes 73736 | tf_op jit(solution)/shard_map/ppermute | solution.py:399
Sparse Core Ops, SparseCore 0:
  35.3 37.2 all-gather.1
